TPU v7x, 128 devices: a whole 4x4x4 slice. The times are simulated.
128 devices in a mesh: grp: 4 (over x_lo, core), blk: 32 (over z, x_hi, y).
Axes of the slice: x: 4 (x_hi: 2, x_lo: 2; x = x_hi * 2 + x_lo), y: 4, z: 4, core: 2. Of those that a mesh axis runs over, the one named last changes fastest.
Arguments:
- incident: float32 [768, 480], P(('grp', 'blk')), may hold values from -24 to 24
- sphere_site: int32 [768], replicated, may hold values from 0 to 767, each once
- jitter: float32 [3, 768], replicated, may hold values from -0.4 to 0.4
- rotation_table: bfloat16 [480, 480], replicated, may hold values from -0.25 to 0.25
- axial_tables: bfloat16 [2, 480, 480], replicated, may hold values from -0.25 to 0.25
- tmatrix: float32 [2, 240], replicated, may hold values from -0.3 to 0.3
- radius_factor: float32 [768], P(('grp', 'blk')), may hold values from 0.29 to 3.3
- probe_field: bfloat16 [32768, 480], P(('grp', 'blk')), may hold values from -0.25 to 0.25
- probe_group: int32 [32768], P(('grp', 'blk')), may hold values from 0 to 3
Outputs:
- solution: float32 [768, 480], P(('grp', 'blk'))
- sensitivity: float32 [768, 480], P(('grp', 'blk'))
- arnoldi: float32 [4], replicated
Inputs may be any that keep to these rules, and one draw needn't show every extreme that they name: sphere_site is a permutation of the sites 0 to 767.
All inputs are finite; a program needn't handle non-finite values.
Results may differ from a plain program's by a relative error of at most 0.011.
Values sent between devices are 32-bit elements; how exact they have to be, the bound alone decides.
No kernel may reach another device: no remote copies, remote signals or barrier semaphores. Data moves between devices by JAX's collectives and lax.ppermute only.
A program may use at most 128 MiB of HBM per device.

v0:
```python
import jax
import jax.numpy as jnp
import numpy as np
from jax import lax
from jax.sharding import PartitionSpec as P

ORDER = 10


WAVENUMBER = 1.3
LATTICE_STEP = 2.5


def order_table(degree_max):
    entries = np.arange(degree_max * (degree_max + 2))
    degree = np.floor(np.sqrt(entries + 1.0) + 1e-09)
    orders = entries + 1 - degree * degree - degree
    return np.concatenate([orders, orders]).astype(np.float32)


def positions(sphere_site, jitter):
    lattice_xyz = jnp.stack([sphere_site % 8, sphere_site // 8 % 8, sphere_site // 64]).astype(
        jnp.float32
    )
    return lattice_xyz * LATTICE_STEP + jitter


def geometry(out_places, out_ids, src_places, src_ids, flip, orders):
    factor = -1.0 if flip else 1.0
    offset = (out_places[:, :, None] - src_places[:, None, :]) * factor
    self_pair = out_ids[:, None] == src_ids[None, :]
    dist_sq = jnp.sum(offset * offset, axis=0)
    distance = jnp.sqrt(jnp.where(self_pair, 1.0, dist_sq))
    azimuth = jnp.arctan2(offset[1], offset[0])
    phase_arg = WAVENUMBER * distance
    radial_cos = jnp.where(self_pair, 0.0, jnp.cos(phase_arg) / phase_arg)
    radial_sin = jnp.where(self_pair, 0.0, jnp.sin(phase_arg) / phase_arg)
    phase = azimuth[:, :, None] * orders
    return (jnp.cos(phase), jnp.sin(phase), radial_cos, radial_sin)


def translate(source, pair_geometry, rotation_table, axial_pair):
    cos_rot, sin_rot, radial_cos, radial_sin = pair_geometry
    out_count, src_count, half_width = cos_rot.shape
    full_width = 2 * half_width
    source_real = source[None, :, :half_width]
    source_imag = source[None, :, half_width:]
    rotated = jnp.concatenate(
        [
            cos_rot * source_real - sin_rot * source_imag,
            sin_rot * source_real + cos_rot * source_imag,
        ],
        axis=2,
    ).astype(jnp.bfloat16)
    flattened = rotated.reshape(out_count * src_count, full_width)
    turned = jnp.dot(flattened, rotation_table, preferred_element_type=jnp.float32).astype(
        jnp.bfloat16
    )
    axial_out = jnp.dot(turned, axial_pair, preferred_element_type=jnp.float32)
    shifted = (
        radial_cos.reshape(-1, 1) * axial_out[:, :full_width]
        + radial_sin.reshape(-1, 1) * axial_out[:, full_width:]
    ).astype(jnp.bfloat16)
    returned = lax.dot_general(
        shifted, rotation_table, (((1,), (1,)), ((), ())), preferred_element_type=jnp.float32
    ).reshape(out_count, src_count, full_width)
    back_real = returned[:, :, :half_width]
    back_imag = returned[:, :, half_width:]
    return jnp.concatenate(
        [
            jnp.sum(cos_rot * back_real + sin_rot * back_imag, axis=1),
            jnp.sum(cos_rot * back_imag - sin_rot * back_real, axis=1),
        ],
        axis=1,
    )


def scatter_apply(field, tmatrix, radius):
    half_width = tmatrix.shape[1]
    real_part, imag_part = (tmatrix[0], tmatrix[1])
    field_real, field_imag = (field[:, :half_width], field[:, half_width:])
    return (
        jnp.concatenate(
            [
                real_part * field_real - imag_part * field_imag,
                imag_part * field_real + real_part * field_imag,
            ],
            axis=1,
        )
        * radius[:, None]
    )


def scatter_adjoint(field, tmatrix, radius):
    half_width = tmatrix.shape[1]
    real_part, imag_part = (tmatrix[0], tmatrix[1])
    field_real, field_imag = (field[:, :half_width], field[:, half_width:])
    return (
        jnp.concatenate(
            [
                real_part * field_real + imag_part * field_imag,
                real_part * field_imag - imag_part * field_real,
            ],
            axis=1,
        )
        * radius[:, None]
    )


def on_device(
    incident,
    sphere_site,
    jitter,
    rotation_table,
    axial_tables,
    tmatrix,
    radius_factor,
    probe_field,
    probe_group,
):
    local_rows = incident.shape[0]
    groups = lax.axis_size("grp")
    blocks = lax.axis_size("blk")
    sphere_count = local_rows * groups * blocks
    per_group = sphere_count // groups
    group_index = lax.axis_index("grp")
    block_index = lax.axis_index("blk")
    orders = jnp.asarray(order_table(ORDER))
    places = positions(sphere_site, jitter)
    everyone = jnp.arange(sphere_count, dtype=jnp.int32)
    own_ids = (
        group_index * per_group + block_index * local_rows + jnp.arange(local_rows, dtype=jnp.int32)
    )
    forward_pair = jnp.concatenate([axial_tables[0], axial_tables[1]], axis=1)
    adjoint_pair = jnp.concatenate([axial_tables[0].T, axial_tables[1].T], axis=1)

    def pair_terms(out_ids, src_ids, flip):
        return geometry(places[:, out_ids], out_ids, places[:, src_ids], src_ids, flip, orders)

    def forward(vector):
        gathered = lax.all_gather(vector, ("grp", "blk"), axis=0, tiled=True)
        field = translate(
            gathered, pair_terms(own_ids, everyone, False), rotation_table, forward_pair
        )
        return vector - scatter_apply(field, tmatrix, radius_factor)

    initial_norm = jnp.sqrt(lax.psum(jnp.sum(incident * incident), ("grp", "blk")))
    basis_first = incident / initial_norm
    image_first = forward(basis_first)
    diag_first = lax.psum(jnp.sum(basis_first * image_first), ("grp", "blk"))
    ortho_first = image_first - diag_first * basis_first
    below_sq = lax.psum(jnp.sum(ortho_first * ortho_first), ("grp", "blk"))
    below_first = jnp.sqrt(below_sq)
    gram_first = diag_first * diag_first + below_sq
    basis_second = ortho_first / below_first
    image_second = forward(basis_second)
    upper_second, diag_second = lax.psum(
        (jnp.sum(basis_first * image_second), jnp.sum(basis_second * image_second)), ("grp", "blk")
    )
    ortho_second = image_second - upper_second * basis_first - diag_second * basis_second
    rest_second = lax.psum(jnp.sum(ortho_second * ortho_second), ("grp", "blk"))
    gram_second = upper_second * upper_second + diag_second * diag_second + rest_second
    gram_cross = diag_first * upper_second + below_first * diag_second
    determinant = gram_first * gram_second - gram_cross * gram_cross
    coeff_first = (
        initial_norm * (diag_first * gram_second - upper_second * gram_cross) / determinant
    )
    coeff_second = (
        initial_norm * (gram_first * upper_second - gram_cross * diag_first) / determinant
    )
    solution = coeff_first * basis_first + coeff_second * basis_second
    arnoldi = jnp.stack([diag_first, below_first, diag_second, rest_second]).astype(jnp.float32)
    group_ids_all = jnp.arange(groups, dtype=jnp.int32)
    own_total = jnp.sum(solution, axis=0)
    table = jnp.where((group_ids_all == group_index)[:, None], own_total[None, :], 0.0)
    totals = lax.psum(table, ("grp", "blk"))
    totals_low = (totals / jnp.sqrt(jnp.float32(per_group))).astype(jnp.bfloat16)
    probe_values = lax.dot_general(
        probe_field, totals_low, (((1,), (1,)), ((), ())), preferred_element_type=jnp.float32
    )
    selector = (probe_group[:, None] == group_ids_all[None, :]).astype(jnp.float32)
    weighted = (selector * probe_values).astype(jnp.bfloat16)
    probe_count = probe_field.shape[0] * groups * blocks
    partial_value = lax.dot_general(
        weighted, probe_field, (((0,), (0,)), ((), ())), preferred_element_type=jnp.float32
    ) * (probe_field.shape[1] * groups / probe_count)
    every_grad = lax.psum(partial_value, ("grp", "blk"))
    own_grad = lax.dynamic_index_in_dim(every_grad, group_index, 0, keepdims=False)
    source = jnp.broadcast_to(own_grad[None, :], solution.shape)
    weighted_source = scatter_adjoint(source, tmatrix, radius_factor)
    gathered = lax.all_gather(weighted_source, ("grp", "blk"), axis=0, tiled=True)
    field = translate(gathered, pair_terms(own_ids, everyone, True), rotation_table, adjoint_pair)
    sensitivity = source - field
    return (solution, sensitivity, arnoldi)


def solution(mesh):
    return jax.shard_map(
        on_device,
        mesh=mesh,
        in_specs=(
            P(("grp", "blk"), None),
            P(),
            P(),
            P(),
            P(),
            P(),
            P(("grp", "blk")),
            P(("grp", "blk"), None),
            P(("grp", "blk")),
        ),
        out_specs=(P(("grp", "blk"), None), P(("grp", "blk"), None), P()),
        check_vma=False,
    )
```

profile of v0, /device:TPU:1, one launch (start us, length us, event | category | flops | bytes accessed | tf_op | source)
XLA Modules:
  0.0 1574.7 jit_solution(65660273384556811)
XLA Ops:
  8.6 68.7 %psum.56 = f32[]{:T(128)} all-reduce(f32[]{:T(128)} %multiply_reduce_fusion.7), channel_id=1, replica_groups=mesh['grp'=4,'blk'=32] {'grp','blk'}, use_global_device_ids=true, to_apply=%region_1.2 | all-reduce | flops 1 | bytes 8 | tf_op jit(solution)/shard_map/psum | solution.py:147
  85.4 2.4 slice_bitcast_fusion.2
  87.8 289.6 %all-gather.7.cloned.1.call-done = f32[128,6,480]{2,1,0:T(8,128)} async-done(((f32[1,6,480]{2,1,0:T(8,128)}), f32[128,6,480]{2,1,0:T(8,128)}) %all-gather.7.cloned.1.call-update) | async-done | bytes 1474576 | tf_op jit(solution)/shard_map/all_gather | solution.py:141
  379.3 21.4 %fusion.31 = (bf16[4608,240]{1,0:T(8,128)(2,1)S(1)}, bf16[4608,240]{1,0:T(8,128)(2,1)}) fusion(f32[768,240]{1,0:T(8,128)S(1)} %get-tuple-element.28, f32[768,240]{1,0:T(8,128)S(1)} %get-tuple-element.27, f32[240]{0:T(256)S(1)} %copy-done.4, f32[4608]{0:T(1024)} %atan2.31), kind=kLoop, calls=%fused_computation.62 | loop fusion | flops 9953280 | bytes 5917632 | tf_op jit(solution)/shard_map/convert.4
  400.7 12.6 fusion.64
  413.3 7.7 fusion.51
  421.0 21.0 %fusion.23 = (f32[6,240]{1,0:T(8,128)S(1)}, f32[6,240]{1,0:T(8,128)S(1)}) fusion(f32[6,768,480]{2,1,0:T(8,128)S(1)} %bitcast.107, f32[240]{0:T(256)S(1)} %copy-done.4, f32[6,768]{1,0:T(8,128)S(1)} %fusion.119), kind=kLoop, calls=%fused_computation.54 | loop fusion | flops 9950400 | bytes 8878272 | tf_op jit(solution)/shard_map/reduce_sum | solution.py:71
  442.7 65.8 %psum.57 = f32[]{:T(128)} all-reduce(f32[]{:T(128)} %multiply_reduce_fusion.6), channel_id=1, replica_groups=mesh['grp'=4,'blk'=32] {'grp','blk'}, use_global_device_ids=true, to_apply=%region_6.7 | all-reduce | flops 1 | bytes 8 | tf_op jit(solution)/shard_map/psum | solution.py:150
  509.8 62.9 %psum.58 = f32[]{:T(128)} all-reduce(f32[]{:T(128)} %multiply_reduce_fusion.5), channel_id=1, replica_groups=mesh['grp'=4,'blk'=32] {'grp','blk'}, use_global_device_ids=true, to_apply=%region_8.9 | all-reduce | flops 1 | bytes 8 | tf_op jit(solution)/shard_map/psum | solution.py:152
  577.2 296.0 %all-gather.9.cloned.1.call-done = f32[128,6,480]{2,1,0:T(8,128)} async-done(((f32[1,6,480]{2,1,0:T(8,128)}), f32[128,6,480]{2,1,0:T(8,128)}) %all-gather.9.cloned.1.call-update) | async-done | bytes 1474576 | tf_op jit(solution)/shard_map/all_gather | solution.py:141
  875.2 21.4 %fusion.35 = (bf16[4608,240]{1,0:T(8,128)(2,1)S(1)}, bf16[4608,240]{1,0:T(8,128)(2,1)}) fusion(f32[768,240]{1,0:T(8,128)S(1)} %get-tuple-element.26, f32[768,240]{1,0:T(8,128)S(1)} %get-tuple-element.25, f32[240]{0:T(256)S(1)} %copy-done.4, f32[4608]{0:T(1024)} %atan2.31), kind=kLoop, calls=%fused_computation.66 | loop fusion | flops 9953280 | bytes 5917632 | tf_op jit(solution)/shard_map/convert.2
  896.6 12.6 fusion.67
  909.2 7.7 fusion.53
  916.9 21.0 %fusion.27 = (f32[6,240]{1,0:T(8,128)S(1)}, f32[6,240]{1,0:T(8,128)S(1)}) fusion(f32[6,768,480]{2,1,0:T(8,128)S(1)} %bitcast.106, f32[240]{0:T(256)S(1)} %copy-done.4, f32[6,768]{1,0:T(8,128)S(1)} %fusion.119), kind=kLoop, calls=%fused_computation.58 | loop fusion | flops 9950400 | bytes 8878272 | tf_op jit(solution)/shard_map/reduce_sum | solution.py:71
  938.6 65.9 %all-reduce = (f32[]{:T(128)}, f32[]{:T(128)}) all-reduce(f32[]{:T(128)} %get-tuple-element.10, f32[]{:T(128)} %get-tuple-element.9), channel_id=1, replica_groups=mesh['grp'=4,'blk'=32] {'grp','blk'}, use_global_device_ids=true, to_apply=%region_12.13 | all-reduce | flops 2 | bytes 16 | tf_op jit(solution)/shard_map/psum | solution.py:157
  1012.6 63.0 %psum.61 = f32[]{:T(128)} all-reduce(f32[]{:T(128)} %multiply_reduce_fusion.2), channel_id=1, replica_groups=mesh['grp'=4,'blk'=32] {'grp','blk'}, use_global_device_ids=true, to_apply=%region_16.17 | all-reduce | flops 1 | bytes 8 | tf_op jit(solution)/shard_map/psum | solution.py:161
  1077.6 63.8 %psum.62 = f32[4,480]{1,0:T(4,128)S(1)} all-reduce(f32[4,480]{1,0:T(4,128)S(1)} %broadcast_select_fusion), channel_id=1, replica_groups=mesh['grp'=4,'blk'=32] {'grp','blk'}, use_global_device_ids=true, to_apply=%region_18.19 | all-reduce | flops 1920 | bytes 15360 | tf_op jit(solution)/shard_map/psum | solution.py:176
  1141.7 62.7 %psum.63 = f32[4,480]{1,0:T(4,128)S(1)} all-reduce(f32[4,480]{1,0:T(4,128)S(1)} %convolution_multiply_fusion), channel_id=1, replica_groups=mesh['grp'=4,'blk'=32] {'grp','blk'}, use_global_device_ids=true, to_apply=%region_19.20 | all-reduce | flops 1920 | bytes 15360 | tf_op jit(solution)/shard_map/psum | solution.py:187
  1205.3 2.4 pad_maximum_fusion.4
  1207.7 296.3 %all-gather.11.cloned.1.call-done = f32[128,6,480]{2,1,0:T(8,128)} async-done(((f32[1,6,480]{2,1,0:T(8,128)}), f32[128,6,480]{2,1,0:T(8,128)}) %all-gather.11.cloned.1.call-update) | async-done | bytes 1474576 | tf_op jit(solution)/shard_map/all_gather | solution.py:191
  1505.9 20.5 %fusion.39 = (bf16[4608,240]{1,0:T(8,128)(2,1)S(1)}, bf16[4608,240]{1,0:T(8,128)(2,1)}) fusion(f32[768,240]{1,0:T(8,128)S(1)} %get-tuple-element.24, f32[768,240]{1,0:T(8,128)S(1)} %get-tuple-element.23, f32[4608]{0:T(1024)S(1)} %atan2.34, f32[240]{0:T(256)S(1)} %copy-done.4), kind=kLoop, calls=%fused_computation.70 | loop fusion | flops 9953280 | bytes 5917632 | tf_op jit(solution)/shard_map/convert
  1526.4 12.4 fusion.71
  1538.8 7.7 fusion.55
  1546.5 21.0 %fusion.19 = (f32[6,240]{1,0:T(8,128)S(1)}, f32[6,240]{1,0:T(8,128)S(1)}) fusion(f32[6,768,480]{2,1,0:T(8,128)S(1)} %bitcast.105, f32[6,768]{1,0:T(8,128)S(1)} %fusion.118, f32[240]{0:T(256)S(1)} %copy-done.4), kind=kLoop, calls=%fused_computation.50 | loop fusion | flops 9950400 | bytes 8878272 | tf_op jit(solution)/shard_map/reduce_sum | solution.py:71
  (75 shorter events, 23.6 us)
Async XLA Ops:
  7.2 393.5 %copy-start = (bf16[480,480]{1,0:T(8,128)(2,1)S(1)}, bf16[480,480]{1,0:T(8,128)(2,1)}, u32[]{:S(2)}) copy-start(bf16[480,480]{1,0:T(8,128)(2,1)} %param.13) | copy-start | bytes 1382404
  7.2 370.2 %all-gather.7.cloned.1.call-start = ((), (), s32[]{:S(2)}) async-start(), calls=%async_computation | async-start | bytes 2113536 | tf_op jit(solution)/shard_map/all_gather | solution.py:141
  79.3 794.0 %all-gather.9.cloned.1.call-start = ((), (), s32[]{:S(2)}) async-start(), calls=%async_computation.1 | async-start | bytes 2113536 | tf_op jit(solution)/shard_map/all_gather | solution.py:141
  85.4 293.9 %copy-start.4 = (f32[240]{0:T(256)S(1)}, f32[240]{0:T(256)}, u32[]{:S(2)}) copy-start(f32[240]{0:T(256)} %constant.85.clone) | copy-start | bytes 2884
  421.0 21.0 %copy-start.1 = (f32[6,480]{1,0:T(8,128)S(1)}, f32[6,480]{1,0:T(8,128)}, u32[]{:S(2)}) copy-start(f32[6,480]{1,0:T(8,128)} %param.10) | copy-start | bytes 34564
  421.0 21.0 %copy-start.5 = (f32[6]{0:T(128)S(1)}, f32[6]{0:T(128)}, u32[]{:S(2)}) copy-start(f32[6]{0:T(128)} %param.16) | copy-start | bytes 76
  574.7 929.3 %all-gather.11.cloned.1.call-start = ((), (), s32[]{:S(2)}) async-start(), calls=%async_computation.2 | async-start | bytes 2113536 | tf_op jit(solution)/shard_map/all_gather | solution.py:191
  916.8 21.1 %copy-start.3 = (f32[6,480]{1,0:T(8,128)S(1)}, f32[6,480]{1,0:T(8,128)}, u32[]{:S(2)}) copy-start(f32[6,480]{1,0:T(8,128)} %broadcast_divide_fusion) | copy-start | bytes 34564
  916.9 160.7 %copy-start.7 = (pred[4]{0:T(512)(128)(4,1)S(1)}, pred[4]{0:T(512)(128)(4,1)}, u32[]{:S(2)}) copy-start(pred[4]{0:T(512)(128)(4,1)} %iota_compare_fusion.3) | copy-start | bytes 16
  916.9 224.5 %copy-start.2 = (bf16[256,480]{0,1:T(8,128)(2,1)S(1)}, bf16[256,480]{0,1:T(8,128)(2,1)}, u32[]{:S(2)}) copy-start(bf16[256,480]{0,1:T(8,128)(2,1)} %param.17) | copy-start | bytes 737284
  916.9 224.5 %copy-start.6 = (s32[256]{0:T(256)S(1)}, s32[256]{0:T(256)}, u32[]{:S(2)}) copy-start(s32[256]{0:T(256)} %param.18) | copy-start | bytes 3076
Sparse Core Ops, SparseCore 0:
  79.5 297.8 all-gather.6
  574.8 298.4 all-gather.8
  1205.3 298.6 all-gather.10
where the time goes:
time: 1580 us; the launch traced here: 1570 us
  waiting for transfers between devices  882 us (56%)
  blocking collectives  453 us (29%)
  other arithmetic  142 us (9%)
  matrix products  60.9 us (4%)
  between operations  25 us (2%)
    all_gather x2, waiting for transfers between devices, forward(): gathered = lax.all_gather(vector, ('grp', 'blk'), axis=0, tiled=True)  586 us
    all_gather x1, waiting for transfers between devices, on_device(): lax.all_gather(weighted_source, ('grp', 'blk'), axis=0, tiled=True)  296 us
    psum x1, blocking collectives, on_device(): lax.psum(jnp.sum(incident * incident), ('grp', 'blk'))  68.7 us
    psum x1, blocking collectives, on_device(): lax.psum((jnp.sum(basis_first * image_second), jnp.sum(basis_second * ima...  65.9 us
    psum x1, blocking collectives, on_device(): diag_first = lax.psum(jnp.sum(basis_first * image_first), ('grp', 'blk'))  65.8 us
    psum x1, blocking collectives, on_device(): totals = lax.psum(table, ('grp', 'blk'))  63.8 us
    another operation x3, other arithmetic  63.2 us
    reduce_sum x3, other arithmetic, translate(): jnp.sum(cos_rot * back_real + sin_rot * back_imag, axis=1)  63 us
  transfers between devices with their start and end apart: 3, of which 3 were waited for; matrix products, arithmetic and copies ran while one was open for 1% of the time, Pallas kernels for 0%

commit v1 on v0

v1 whole, which is shorter than its diff:
```python
import jax
import jax.numpy as jnp
import numpy as np
from jax import lax
from jax.experimental import pallas as pl
from jax.experimental.pallas import tpu as pltpu
from jax.sharding import Mesh
from jax.sharding import PartitionSpec as P

ORDER = 10
WAVENUMBER = 1.3
LATTICE_STEP = 2.5

SPHERES = 768
COEFF = 480
HALF = 240
GROUPS = 4
PER_GROUP = SPHERES // GROUPS
PROBES = 32768
OWN = 6
PROBES_OWN = 256
LANES = 128
WIDE = 256
FULL = 2 * WIDE
ROWS = 8
BLOCK = 2 * ROWS
BLOCKS = 4 * ORDER + 1
TOP = 2 * ORDER
CHUNK = OWN * FULL // LANES
FAR = 64
SCALE = 2.0**-14
PAD = HALF
BF = jnp.bfloat16
F32 = jnp.float32

FAR_AXES = ("xl", "z", "xh", "y")
ALL_AXES = ("xl", "co", "z", "xh", "y")


def order_table(degree_max):
    entries = np.arange(degree_max * (degree_max + 2))
    degree = np.floor(np.sqrt(entries + 1.0) + 1e-09)
    orders = entries + 1 - degree * degree - degree
    return np.concatenate([orders, orders]).astype(np.int32)


_ORDERS = order_table(ORDER)
_SORTED = np.lexsort((_ORDERS, np.abs(_ORDERS)))
_SOURCE = np.full((1, FULL), -1, np.int32)
_SOURCE[0, :HALF] = _SORTED
_SOURCE[0, WIDE : WIDE + HALF] = _SORTED + HALF
_LANE_ORDER = np.full((1, WIDE), 99, np.int32)
_LANE_ORDER[0, :HALF] = _ORDERS[_SORTED]
_SIGN = np.zeros((1, WIDE), np.float32)
_SIGN[0, :HALF] = np.sign(_ORDERS[_SORTED])


def classes_of(half):
    part = _LANE_ORDER[0, half * LANES : (half + 1) * LANES]
    return [int(m) for m in np.unique(part[part < 99])]


CLASSES = (classes_of(0), classes_of(1))


def dot(a, b):
    return jnp.dot(a, b, preferred_element_type=F32)


def dot_t(a, b):
    return lax.dot_general(a, b, (((1,), (1,)), ((), ())), preferred_element_type=F32)


def split(x):
    high = x.astype(BF)
    return high, (x - high.astype(F32)).astype(BF)


def exact_dot(x, onehot):
    high = x.astype(BF)
    rest = x - high.astype(F32)
    mid = rest.astype(BF)
    low = (rest - mid.astype(F32)).astype(BF)
    return dot(high, onehot) + dot(mid, onehot) + dot(low, onehot)


def onehot_in(source):
    rows = lax.broadcasted_iota(jnp.int32, (COEFF, FULL), 0)
    return jnp.where(rows == source, 1.0, 0.0).astype(BF)


def onehot_out(source_column):
    lanes = lax.broadcasted_iota(jnp.int32, (FULL, COEFF), 1)
    return jnp.where(lanes == source_column, 1.0, 0.0).astype(BF)


def own_group():
    return lax.axis_index("xl") * 2 + lax.axis_index("co")


def send_body(incident, source, radius, chunk, rows_out, radius_out, lines):
    value = jnp.concatenate([incident[...], jnp.zeros((ROWS - OWN, COEFF), F32)], axis=0) * SCALE
    rows = exact_dot(value, onehot_in(source[...]))
    rows_out[...] = rows
    lane = lax.broadcasted_iota(jnp.int32, (ROWS, FULL), 1)
    line = lax.broadcasted_iota(jnp.int32, (ROWS, LANES), 0)
    column = jnp.zeros((ROWS, LANES), F32)
    for r in range(OWN):
        column = jnp.where(line == r, radius[r], column)
    radius_out[...] = column
    marked = jnp.where(lane == PAD + own_group(), jnp.concatenate([column] * 4, axis=1), rows)
    write_chunks(marked, chunk, lines)


def write_chunks(rows, chunk, lines):
    for part in range(4):
        lines[pl.ds(part, ROWS, stride=4), :] = rows[:, part * LANES : (part + 1) * LANES]
    once = lines[:CHUNK, :]
    for far in range(FAR):
        chunk[far] = once


def prepare_body(
    site, jitter, rotation, axial, probes, tmat, source, source_column,
    pairs, tables, tables_t, probes_out, tmat_out,
):
    own = (
        (lax.axis_index("co") * 2 + lax.axis_index("xl")) * PER_GROUP
        + ((lax.axis_index("z") * 2 + lax.axis_index("xh")) * 4 + lax.axis_index("y")) * OWN
    )
    sites = site[...]
    place_x = (sites & 7).astype(F32) * LATTICE_STEP + jitter[0:1, :]
    place_y = ((sites >> 3) & 7).astype(F32) * LATTICE_STEP + jitter[1:2, :]
    place_z = (sites >> 6).astype(F32) * LATTICE_STEP + jitter[2:3, :]
    lane = lax.broadcasted_iota(jnp.int32, (ROWS, SPHERES), 1)
    line = lax.broadcasted_iota(jnp.int32, (ROWS, SPHERES), 0)
    same = lane == line + own

    def offset(place):
        here = jnp.sum(jnp.where(same, place, 0.0), axis=1, keepdims=True)
        return here - place

    dx, dy, dz = offset(place_x), offset(place_y), offset(place_z)
    distance = jnp.sqrt(jnp.where(same, 1.0, dx * dx + dy * dy + dz * dz))
    phase = WAVENUMBER * distance
    none = same | (line >= OWN)
    radial_cos = jnp.where(none, 0.0, jnp.cos(phase) / phase)
    radial_sin = jnp.where(none, 0.0, jnp.sin(phase) / phase)
    larger = jnp.maximum(jnp.abs(dx), jnp.abs(dy))
    apart = larger > 0.0
    inverse = 1.0 / jnp.where(apart, larger, 1.0)
    ax, ay = dx * inverse, dy * inverse
    length = jnp.sqrt(jnp.where(apart, ax * ax + ay * ay, 1.0))
    cos_one = jnp.where(apart, ax / length, 1.0)
    sin_one = jnp.where(apart, ay / length, 0.0)

    def put(block, factor):
        value = jnp.concatenate([radial_cos * factor, radial_sin * factor], axis=0)
        pairs[block * BLOCK : (block + 1) * BLOCK, :] = value.astype(BF)

    pairs[0:BLOCK, :] = jnp.concatenate([radial_cos, radial_sin], axis=0).astype(BF)
    cos_k, sin_k = cos_one, sin_one
    for k in range(1, TOP + 1):
        put(k, cos_k)
        put(TOP + k, sin_k)
        if k < TOP:
            cos_k, sin_k = (
                cos_k * cos_one - sin_k * sin_one,
                sin_k * cos_one + cos_k * sin_one,
            )

    inwards = onehot_in(source[...])
    outwards = onehot_out(source_column[...])
    turned = dot(outwards, rotation[...]).astype(BF)
    for radial in range(2):
        mixed_high, mixed_low = split(0.5 * dot(turned, axial[radial]))
        tables[radial] = (dot_t(mixed_high, turned) + dot_t(mixed_low, turned)).astype(BF)
        tables_t[radial] = (dot_t(turned, mixed_high) + dot_t(turned, mixed_low)).astype(BF)
    probes_out[...] = dot(probes[...], inwards).astype(BF)
    tmat_rows = jnp.concatenate([tmat[...], jnp.zeros((ROWS - 2, HALF), F32)], axis=0)
    tmat_out[...] = exact_dot(tmat_rows, inwards[:HALF, :WIDE])


def load_rows(gathered, rows):
    for part in range(4):
        lines = gathered[pl.ds(part, SPHERES, stride=4), :]
        rows[:, part * LANES : (part + 1) * LANES] = lines.astype(BF)


def group_sums(gathered):
    groups = []
    for place in (0, 2, 1, 3):
        parts = []
        for part in range(4):
            lines = gathered[pl.ds(place * PER_GROUP * 4 + part, PER_GROUP, stride=4), :]
            parts.append(jnp.sum(lines, axis=0, keepdims=True))
        groups.append(jnp.concatenate(parts, axis=1))
    return jnp.concatenate(groups, axis=0)


def mix(sums, shifted, tables, lane_order, sign):
    for k in range(1, TOP + 1):
        at_cos, at_sin = pl.ds(k * BLOCK, BLOCK), pl.ds((TOP + k) * BLOCK, BLOCK)
        cos_re, cos_im = sums[at_cos, :WIDE], sums[at_cos, WIDE:]
        sin_re, sin_im = sums[at_sin, :WIDE], sums[at_sin, WIDE:]
        sums[at_cos, :WIDE] = cos_re - sin_im
        sums[at_cos, WIDE:] = cos_im + sin_re
        sums[at_sin, :WIDE] = cos_re + sin_im
        sums[at_sin, WIDE:] = cos_im - sin_re

    def block_of(k):
        return (k if k >= 0 else TOP - k) * BLOCK

    for half in range(2):
        orders = jnp.broadcast_to(lane_order[:, half * LANES : (half + 1) * LANES], (BLOCK, LANES))
        masks = [orders == m for m in CLASSES[half]]

        def pick(out_order, start):
            columns = slice(start + half * LANES, start + (half + 1) * LANES)
            value = None
            for m, mask in zip(CLASSES[half], masks):
                row = block_of(m - out_order)
                here = sums[row : row + BLOCK, columns]
                value = here if value is None else jnp.where(mask, here, value)
            return value

        for out_order in range(ORDER + 1):
            minus_re, minus_im = pick(out_order, 0), pick(out_order, WIDE)
            if out_order:
                plus_re, plus_im = pick(-out_order, 0), pick(-out_order, WIDE)
            else:
                plus_re, plus_im = minus_re, minus_im
            cos_part = (minus_re + plus_re, minus_im + plus_im)
            sin_part = (plus_im - minus_im, minus_re - plus_re)
            for which, start in ((0, 0), (1, WIDE)):
                columns = slice(start + half * LANES, start + (half + 1) * LANES)
                for radial in range(2):
                    lines = slice(radial * ROWS, (radial + 1) * ROWS)
                    value = jnp.concatenate([cos_part[which][lines], sin_part[which][lines]], axis=0)
                    shifted[radial, out_order * BLOCK : (out_order + 1) * BLOCK, columns] = value.astype(BF)

    back = dot(shifted[0], tables[0]) + dot(shifted[1], tables[1])
    parts_re, parts_im = [], []
    for half in range(2):
        columns = slice(half * LANES, (half + 1) * LANES)
        orders = jnp.abs(jnp.broadcast_to(lane_order[:, columns], (ROWS, LANES)))
        signs = sign[:, columns]
        field_re = field_im = None
        for m in sorted({abs(c) for c in CLASSES[half]}):
            cos_lines = slice(m * BLOCK, m * BLOCK + ROWS)
            sin_lines = slice(m * BLOCK + ROWS, (m + 1) * BLOCK)
            real, imag = columns, slice(WIDE + half * LANES, WIDE + (half + 1) * LANES)
            value_re = back[cos_lines, real] + signs * back[sin_lines, imag]
            value_im = back[cos_lines, imag] - signs * back[sin_lines, real]
            field_re = value_re if field_re is None else jnp.where(orders == m, value_re, field_re)
            field_im = value_im if field_im is None else jnp.where(orders == m, value_im, field_im)
        parts_re.append(field_re)
        parts_im.append(field_im)
    return jnp.concatenate(parts_re + parts_im, axis=1)


def scatter(field, tmat, radius):
    real, imag = tmat[0:1, :], tmat[1:2, :]
    field_re, field_im = field[:, :WIDE], field[:, WIDE:]
    wide = jnp.concatenate([radius, radius], axis=1)
    return jnp.concatenate(
        [
            wide * (imag * field_im - real * field_re),
            -wide * (imag * field_re + real * field_im),
        ],
        axis=1,
    )


def first_body(
    gathered, pairs, tables, tmat, radius, lane_order, sign,
    chunk, rows_out, weights_out, totals_out, rows, sums, shifted, lines,
):
    load_rows(gathered, rows)
    totals_out[...] = group_sums(gathered)
    sums[...] = dot(pairs[...], rows[...])
    for block in range(BLOCKS):
        k = block if block <= TOP else block - TOP
        at = pl.ds(block * BLOCK, BLOCK)
        value = sums[at, LANES:WIDE]
        weights_out[at, :] = (value if k % 2 == 0 else -value).astype(BF)
    field = mix(sums, shifted, tables, lane_order, sign)
    image = scatter(field, tmat, radius[...])
    rows_out[...] = image
    write_chunks(image, chunk, lines)


def gradient_body(gathered, totals_first, probes, probe_group, keep, send):
    totals = jnp.concatenate([totals_first[...], group_sums(gathered)], axis=0)
    lane = lax.broadcasted_iota(jnp.int32, (2 * GROUPS, FULL), 1)
    totals = jnp.where((lane & (WIDE - 1)) < HALF, totals, 0.0)
    total_high, total_low = split(totals)
    values = dot_t(total_high, probes[...]) + dot_t(total_low, probes[...])
    line = lax.broadcasted_iota(jnp.int32, (2 * GROUPS, PROBES_OWN), 0)
    values = jnp.where((line & (GROUPS - 1)) == probe_group[...], values, 0.0)
    value_high, value_low = split(values)
    gradient = dot(value_high, probes[...]) + dot(value_low, probes[...])
    core = lax.axis_index("co")
    first, second = gradient[:GROUPS], gradient[GROUPS:]
    keep[...] = jnp.where(core == 0, first, second)
    send[...] = jnp.where(core == 0, second, first)


def second_body(
    gathered, pairs, tables, tmat, radius, lane_order, sign, base, image,
    scalars, rows, sums, shifted,
):
    load_rows(gathered, rows)
    sums[...] = dot(pairs[...], rows[...])
    field = mix(sums, shifted, tables, lane_order, sign)
    last = scatter(field, tmat, radius[...])
    zero, one = base[...], image[...]
    line = lax.broadcasted_iota(jnp.int32, (GROUPS, FULL), 0)
    lane = lax.broadcasted_iota(jnp.int32, (GROUPS, FULL), 1)
    out = jnp.zeros((GROUPS, FULL), F32)
    pairs_of = ((zero, zero), (zero, one), (one, one), (zero, last), (one, last), (last, last))
    for index, (a, b) in enumerate(pairs_of):
        out = jnp.where((line == 0) & (lane == PAD + index), jnp.sum(a * b), out)
    scalars[...] = out


def finish_body(
    parts, weights, tables_t, tmat, lane_order, sign, source_column, incident, image,
    solution_out, sensitivity_out, arnoldi_out, places, sums, shifted,
):
    first = jnp.sum(parts[0], axis=0)
    second = jnp.sum(parts[1], axis=0)
    scal = (first + second)[0:1, :]
    g00, s01, s11, s02, s12, s22 = [scal[:, PAD + i : PAD + i + 1] for i in range(6)]
    g01, g11, g02, g12, g22 = s01 / g00, s11 / g00, s02 / g00, s12 / g00, s22 / g00
    diag_first = 1.0 + g01
    below_sq = g11 - g01 * g01
    below_first = jnp.sqrt(below_sq)
    upper_second = (g02 - g01 * g01) / below_first
    shift_second = (g12 - g01 * g11 - g01 * g02 + g01 * g01 * g01) / below_sq
    diag_second = 1.0 + shift_second
    norm_sq = (g22 - 2.0 * g01 * g12 + g01 * g01 * g11) / below_sq
    rest_second = norm_sq - upper_second * upper_second - shift_second * shift_second
    gram_first = diag_first * diag_first + below_sq
    gram_cross = diag_first * upper_second + below_first * diag_second
    gram_second = upper_second * upper_second + diag_second * diag_second + rest_second
    determinant = gram_first * gram_second - gram_cross * gram_cross
    step_first = (diag_first * gram_second - upper_second * gram_cross) / determinant
    step_second = (gram_first * upper_second - gram_cross * diag_first) / determinant
    for_image = step_second / below_first
    for_base = step_first - for_image * g01
    arnoldi_out[0] = diag_first[0, 0]
    arnoldi_out[1] = below_first[0, 0]
    arnoldi_out[2] = diag_second[0, 0]
    arnoldi_out[3] = rest_second[0, 0]

    factor = COEFF * GROUPS / PROBES / SCALE / float(np.sqrt(np.float32(PER_GROUP)))
    gradient = (for_base * first + for_image * second) * factor
    real, imag = tmat[0:1, :], tmat[1:2, :]
    grad_re, grad_im = gradient[:, :WIDE], gradient[:, WIDE:]
    places[...] = jnp.zeros((LANES, FULL), F32)
    at = pl.ds(PAD - LANES, GROUPS)
    places[at, :WIDE] = real * grad_re + imag * grad_im
    places[at, WIDE:] = real * grad_im - imag * grad_re
    sums[...] = dot(weights[...], places[...].astype(BF))
    field = mix(sums, shifted, tables_t, lane_order, sign)
    group = own_group()
    own = jnp.zeros((1, FULL), F32)
    for g in range(GROUPS):
        own = jnp.where(group == g, gradient[g : g + 1, :], own)
    lane = lax.broadcasted_iota(jnp.int32, (1, FULL), 1)
    own = jnp.where((lane & (WIDE - 1)) < HALF, own, 0.0)
    both = jnp.concatenate([image[...], own - field], axis=0)
    result = exact_dot(both, onehot_out(source_column[...]))
    image_rows = result[:OWN]
    solution_out[...] = for_base * incident[...] + (for_image / SCALE) * image_rows
    sensitivity_out[...] = result[ROWS : ROWS + OWN]


def call(body, outs, scratch=(), operands=(), smem=(), smem_outs=(), cost=None):
    vmem = pl.BlockSpec(memory_space=pltpu.VMEM)
    scalar = pl.BlockSpec(memory_space=pltpu.SMEM)
    return pl.pallas_call(
        body,
        out_shape=[jax.ShapeDtypeStruct(shape, kind) for shape, kind in outs],
        in_specs=[scalar if i in smem else vmem for i in range(len(operands))],
        out_specs=[scalar if i in smem_outs else vmem for i in range(len(outs))],
        scratch_shapes=list(scratch),
        compiler_params=pltpu.CompilerParams(vmem_limit_bytes=40 * 1024 * 1024),
        cost_estimate=cost,
    )(*operands)


def exchange(chunk):
    far = lax.all_to_all(chunk, FAR_AXES, 0, 0)
    return lax.all_gather(far, "co").reshape(2 * FAR * CHUNK, LANES)


def on_device(
    incident,
    sphere_site,
    jitter,
    rotation_table,
    axial_tables,
    tmatrix,
    radius_factor,
    probe_field,
    probe_group,
):
    source = jnp.asarray(_SOURCE)
    source_column = jnp.asarray(_SOURCE.reshape(FULL, 1))
    lane_order = jnp.asarray(_LANE_ORDER)
    sign = jnp.asarray(_SIGN)

    chunk, base, radius = call(
        send_body,
        [((FAR, CHUNK, LANES), F32), ((ROWS, FULL), F32), ((ROWS, LANES), F32)],
        [pltpu.VMEM((4 * ROWS, LANES), F32)],
        (incident, source, radius_factor),
        smem=(2,),
    )
    gathered_base = exchange(chunk)

    def by_core(array):
        lead = array.shape[:-1]
        return jnp.swapaxes(array.reshape(lead + (2, 2, PER_GROUP)), -3, -2).reshape(lead + (SPHERES,))

    pairs, tables, tables_t, probes, tmat = call(
        prepare_body,
        [
            ((BLOCKS * BLOCK, SPHERES), BF),
            ((2, FULL, FULL), BF),
            ((2, FULL, FULL), BF),
            ((PROBES_OWN, FULL), BF),
            ((ROWS, WIDE), F32),
        ],
        operands=(
            by_core(sphere_site[None, :]),
            by_core(jitter),
            rotation_table,
            axial_tables,
            probe_field,
            tmatrix,
            source,
            source_column,
        ),
        cost=pl.CostEstimate(flops=6_000_000_000, bytes_accessed=8_000_000, transcendentals=20_000),
    )

    row_scratch = pltpu.VMEM((SPHERES, FULL), BF)
    sum_scratch = pltpu.VMEM((BLOCKS * BLOCK, FULL), F32)
    shift_scratch = pltpu.VMEM((2, (ORDER + 1) * BLOCK, FULL), BF)
    line_scratch = pltpu.VMEM((4 * ROWS, LANES), F32)

    chunk, image, weights, totals_first = call(
        first_body,
        [
            ((FAR, CHUNK, LANES), F32),
            ((ROWS, FULL), F32),
            ((BLOCKS * BLOCK, LANES), BF),
            ((GROUPS, FULL), F32),
        ],
        [row_scratch, sum_scratch, shift_scratch, line_scratch],
        (gathered_base, pairs, tables, tmat, radius, lane_order, sign),
    )
    gathered_image = exchange(chunk)

    keep, send = call(
        gradient_body,
        [((GROUPS, FULL), F32), ((GROUPS, FULL), F32)],
        operands=(gathered_image, totals_first, probes, probe_group.reshape(1, PROBES_OWN)),
    )
    received = lax.ppermute(send, "co", [(0, 1), (1, 0)])
    (scalars,) = call(
        second_body,
        [((GROUPS, FULL), F32)],
        [row_scratch, sum_scratch, shift_scratch],
        (gathered_image, pairs, tables, tmat, radius, lane_order, sign, base, image),
        cost=pl.CostEstimate(flops=1_000_000_000, bytes_accessed=8_000_000, transcendentals=0),
    )
    lane = jnp.arange(FULL, dtype=jnp.int32)
    share = jnp.where((lane & (WIDE - 1)) < HALF, keep + received, scalars)
    spread = jnp.broadcast_to(share[None], (FAR, GROUPS, FULL))
    parts = lax.all_gather(lax.all_to_all(spread, FAR_AXES, 0, 0), "co")
    solution_rows, sensitivity_rows, arnoldi = call(
        finish_body,
        [((OWN, COEFF), F32), ((OWN, COEFF), F32), ((4,), F32)],
        [pltpu.VMEM((LANES, FULL), F32), sum_scratch, shift_scratch],
        (parts, weights, tables_t, tmat, lane_order, sign, source_column, incident, image),
        smem_outs=(2,),
    )
    return solution_rows, sensitivity_rows, arnoldi


def solution(mesh):
    fine = Mesh(mesh.devices.reshape(2, 2, 4, 2, 4), ALL_AXES)
    split_rows = P(ALL_AXES)
    return jax.shard_map(
        on_device,
        mesh=fine,
        in_specs=(
            P(ALL_AXES, None),
            P(),
            P(),
            P(),
            P(),
            P(),
            split_rows,
            P(ALL_AXES, None),
            split_rows,
        ),
        out_specs=(P(ALL_AXES, None), P(ALL_AXES, None), P()),
        check_vma=False,
    )
```

time: 1580 us -> 137 us (0.09)
  waiting for transfers between devices: 882 us -> 23.7 us
  blocking collectives: 453 us -> 70.8 us
  other arithmetic: 142 us -> 0.52 us
  matrix products: 60.9 us -> 0 us
    all_gather x3, waiting for transfers between devices: 882 us -> 23.7 us  [the longest x2 13.6 us: exchange(): return lax.all_gather(far, 'co').reshape(2 * FAR * CHUNK, LANES)]
    psum x7 -> x0, blocking collectives: 453 us -> none  [the longest x1 68.7 us: on_device(): lax.psum(jnp.sum(incident * incident), ('grp', 'blk'))]
    all_to_all x0 -> x3, blocking collectives: none -> 70.8 us  [the longest x2 49.2 us: exchange(): far = lax.all_to_all(chunk, FAR_AXES, 0, 0)]
    reduce_sum x10 -> x0, other arithmetic: 69.6 us -> none  [the longest x3 63 us: translate(): jnp.sum(cos_rot * back_real + sin_rot * back_imag, axis=1)]
    another operation x4 -> x0, other arithmetic: 65.6 us -> none
    dot_general x7 -> x0, matrix products: 60.9 us -> none  [the longest x3 37.6 us: translate(): axial_out = jnp.dot(turned, axial_pair, preferred_element_type=jnp.float32)]
  transfers between devices with their start and end apart: 3 -> 4, of which waited for: 3 -> 3; matrix products, arithmetic and copies ran while one was open for 1% -> 1% of each run, Pallas kernels for 0% -> 4%
where the time goes in v1:
time: 137 us; the launch traced here: 136 us
  blocking collectives  70.8 us (52%)
  waiting for transfers between devices  23.7 us (17%)
  local copies, waits for them, and re-layouts  15.6 us (11%)
  between operations  14 us (10%)
  Pallas kernels  11 us (8%)
    all_to_all x2, blocking collectives, exchange(): far = lax.all_to_all(chunk, FAR_AXES, 0, 0)  49.2 us
    all_to_all x1, blocking collectives, on_device(): parts = lax.all_gather(lax.all_to_all(spread, FAR_AXES, 0, 0), 'co')  21.6 us
    unnamed x65, local copies, waits for them, and re-layouts  15.2 us
    all_gather x2, waiting for transfers between devices, exchange(): return lax.all_gather(far, 'co').reshape(2 * FAR * CHUNK, LANES)  13.6 us
    pallas_call x6, Pallas kernels, call(): pl.pallas_call(body, out_shape=[jax.ShapeDtypeStruct(shape, kind) for sha...  11 us
    all_gather x1, waiting for transfers between devices, on_device(): parts = lax.all_gather(lax.all_to_all(spread, FAR_AXES, 0, 0), 'co')  10.1 us
  transfers between devices with their start and end apart: 4, of which 3 were waited for; matrix products, arithmetic and copies ran while one was open for 1% of the time, Pallas kernels for 4%

profile of v1, /device:TPU:1, one launch (start us, length us, event | category | flops | bytes accessed | tf_op | source)
XLA Modules:
  0.0 136.0 jit_solution(12271184494754666615)
XLA Ops:
  7.2 0.7 copy-done.8
  8.0 0.7 copy-done.19
  9.3 0.9 shard_map.148
  10.3 25.4 %all_to_all.15 = f32[64,24,128]{2,1,0:T(8,128)} all-to-all(f32[64,24,128]{2,1,0:T(8,128)S(1)} %get-tuple-element.17), channel_id=1, replica_groups=mesh['xl'=2,'co'=2,'z'=4,'xh'=2,'y'=4] {'xl','z','xh','y'}, dimensions={0} | all-to-all | bytes 1572864 | tf_op jit(solution)/shard_map/all_to_all | solution.py:395
  35.7 0.9 copy.23.probes
  37.0 0.9 copy-done.7
  37.9 1.2 copy-done.23
  39.1 1.0 copy-done.24
  40.1 3.7 %shard_map.149 = (bf16[656,768]{1,0:T(8,128)(2,1)S(1)}, bf16[2,512,512]{2,1,0:T(8,128)(2,1)S(1)}, bf16[2,512,512]{2,1,0:T(8,128)(2,1)S(1)}, bf16[256,512]{1,0:T(8,128)(2,1)S(1)}, f32[8,256]{1,0:T(8,128)S(1)}) custom-call(s32[1,768]{1,0:T(1,128)S(1)} %reshape.26.site, f32[3,768]{1,0:T(4,128)S(1)} %reshape.28.jitter, bf16[480,480]{1,0:T(8,128)(2,1)S(1)} %copy-done.24, ...), custom_call_target="tpu_custom_call" | custom-call | flops 6000000000 | bytes 8000000 | tf_op jit(solution)/shard_map/pallas_call | solution.py:383
  43.8 0.7 copy-done.5
  44.6 2.8 %all-gather.7.cloned.1.call-done = f32[128,24,128]{2,1,0:T(8,128)} async-done(((f32[64,24,128]{2,1,0:T(8,128)}), f32[128,24,128]{2,1,0:T(8,128)}) %all-gather.7.cloned.1.call-update) | async-done | bytes 1572880 | tf_op jit(solution)/shard_map/all_gather | solution.py:396
  47.4 1.4 %copy-done.2 = f32[128,24,128]{2,1,0:T(8,128)S(1)} copy-done((f32[128,24,128]{2,1,0:T(8,128)S(1)}, f32[128,24,128]{2,1,0:T(8,128)}, u32[]{:S(2)}) %copy-start.2) | copy-done | bytes 1572888
  48.8 0.7 copy-done.13
  49.5 0.7 copy-done.16
  50.1 1.5 %shard_map.150 = (f32[64,24,128]{2,1,0:T(8,128)S(1)}, f32[8,512]{1,0:T(8,128)S(1)}, bf16[656,128]{1,0:T(8,128)(2,1)S(1)}, f32[4,512]{1,0:T(4,128)S(1)}) custom-call(f32[3072,128]{1,0:T(8,128)S(1)} %bitcast.10, bf16[656,768]{1,0:T(8,128)(2,1)S(1)} %get-tuple-element.18.pairs, bf16[2,512,512]{2,1,0:T(8,128)(2,1)S(1)} %get-tuple-element.19.tables, ...), custom_call_target="tpu_custom_call" | custom-call | tf_op jit(solution)/shard_map/pallas_call | solution.py:383
  52.2 23.9 %all_to_all.16 = f32[64,24,128]{2,1,0:T(8,128)} all-to-all(f32[64,24,128]{2,1,0:T(8,128)S(1)} %get-tuple-element.22), channel_id=1, replica_groups=mesh['xl'=2,'co'=2,'z'=4,'xh'=2,'y'=4] {'xl','z','xh','y'}, dimensions={0} | all-to-all | bytes 1572864 | tf_op jit(solution)/shard_map/all_to_all | solution.py:395
  76.7 10.8 %all-gather.9.cloned.1.call-done = f32[128,24,128]{2,1,0:T(8,128)} async-done(((f32[64,24,128]{2,1,0:T(8,128)}), f32[128,24,128]{2,1,0:T(8,128)}) %all-gather.9.cloned.1.call-update) | async-done | bytes 1572880 | tf_op jit(solution)/shard_map/all_gather | solution.py:396
  87.5 1.4 %copy-done = f32[128,24,128]{2,1,0:T(8,128)S(1)} copy-done((f32[128,24,128]{2,1,0:T(8,128)S(1)}, f32[128,24,128]{2,1,0:T(8,128)}, u32[]{:S(2)}) %copy-start) | copy-done | bytes 1572888
  88.9 0.9 copy-done.6
  91.9 1.5 %shard_map.152 = f32[4,512]{1,0:T(4,128)S(1)} custom-call(f32[3072,128]{1,0:T(8,128)S(1)} %bitcast.9, bf16[656,768]{1,0:T(8,128)(2,1)S(1)} %get-tuple-element.18.pairs, bf16[2,512,512]{2,1,0:T(8,128)(2,1)S(1)} %get-tuple-element.19.tables, f32[8,256]{1,0:T(8,128)S(1)} %get-tuple-element.20.tmat, f32[8,128]{1,0:T(8,128)S(1)} %get-tuple-element.21.radius, ...), custom_call_target="tpu_custom_call" | custom-call | flops 1000000000 | bytes 8000000 | tf_op jit(solution)/shard_map/pallas_call | solution.py:383
  93.6 21.6 %all_to_all.17 = f32[64,4,512]{2,1,0:T(4,128)} all-to-all(f32[64,4,512]{2,1,0:T(4,128)S(1)} %broadcast_in_dim.11), channel_id=1, replica_groups=mesh['xl'=2,'co'=2,'z'=4,'xh'=2,'y'=4] {'xl','z','xh','y'}, dimensions={0} | all-to-all | bytes 1048576 | tf_op jit(solution)/shard_map/all_to_all | solution.py:484
  115.2 10.1 %all-gather.11.cloned.1.call-done = f32[128,4,512]{2,1,0:T(4,128)} async-done(((f32[64,4,512]{2,1,0:T(4,128)}), f32[128,4,512]{2,1,0:T(4,128)}) %all-gather.11.cloned.1.call-update) | async-done | bytes 1048592 | tf_op jit(solution)/shard_map/all_gather | solution.py:484
  125.4 1.2 copy-done.3
  126.6 2.9 %shard_map.153 = (f32[6,480]{1,0:T(8,128)}, f32[6,480]{1,0:T(8,128)}, f32[4]{0:T(128)}) custom-call(f32[2,64,4,512]{3,2,1,0:T(4,128)S(1)} %bitcast.11, bf16[656,128]{1,0:T(8,128)(2,1)S(1)} %get-tuple-element.29.weights, bf16[2,512,512]{2,1,0:T(8,128)(2,1)S(1)} %get-tuple-element.30.tables_t, f32[8,256]{1,0:T(8,128)S(1)} %get-tuple-element.20.tmat, ...), custom_call_target="tpu_custom_call" | custom-call | tf_op jit(solution)/shard_map/pallas_call | solution.py:383
  (70 shorter events, 4.6 us)
Async XLA Ops:
  7.2 29.8 %copy-start.4 = (s32[512,1]{1,0:T(8,128)S(1)}, s32[512,1]{1,0:T(8,128)}, u32[]{:S(2)}) copy-start(s32[512,1]{1,0:T(8,128)} %constant.13.clone.source_column) | copy-start | bytes 6148
  7.2 40.2 %all-gather.7.cloned.1.call-start = ((), (), s32[]{:S(2)}) async-start(), calls=%async_computation.3 | async-start | bytes 2359296 | tf_op jit(solution)/shard_map/all_gather | solution.py:396
  9.3 26.4 %copy-start.28 = (bf16[256,480]{0,1:T(8,128)(2,1)S(1)}, bf16[256,480]{0,1:T(8,128)(2,1)}, u32[]{:S(2)}) copy-start(bf16[256,480]{0,1:T(8,128)(2,1)} %param.20) | copy-start | bytes 737284
  9.3 27.3 %copy-start.29 = (f32[3,768]{1,0:T(4,128)S(1)}, f32[3,768]{1,0:T(4,128)}, u32[]{:S(2)}) copy-start(f32[3,768]{1,0:T(4,128)} %param.15) | copy-start | bytes 27652
  9.3 27.5 %copy-start.30 = (s32[768]{0:T(1024)S(1)}, s32[768]{0:T(1024)}, u32[]{:S(2)}) copy-start(s32[768]{0:T(1024)} %param.14) | copy-start | bytes 9220
  9.3 27.6 %copy-start.20 = (s32[1,512]{1,0:T(1,128)S(1)}, s32[1,512]{1,0:T(1,128)}, u32[]{:S(2)}) copy-start(s32[1,512]{1,0:T(1,128)} %constant.12.clone.source) | copy-start | bytes 6148
  9.3 27.6 %copy-start.27 = (f32[2,240]{1,0:T(2,128)S(1)}, f32[2,240]{1,0:T(2,128)}, u32[]{:S(2)}) copy-start(f32[2,240]{1,0:T(2,128)} %tmat.1) | copy-start | bytes 5764
  10.3 26.4 %copy-start.25 = (f32[8,512]{1,0:T(8,128)}, f32[8,512]{1,0:T(8,128)S(1)}, u32[]{:S(2)}) copy-start(f32[8,512]{1,0:T(8,128)S(1)} %get-tuple-element.27.base) | copy-start | bytes 49156
  35.7 51.8 %all-gather.9.cloned.1.call-start = ((), (), s32[]{:S(2)}) async-start(), calls=%async_computation.4 | async-start | bytes 2359296 | tf_op jit(solution)/shard_map/all_gather | solution.py:396
  47.4 1.4 %copy-start.2 = (f32[128,24,128]{2,1,0:T(8,128)S(1)}, f32[128,24,128]{2,1,0:T(8,128)}, u32[]{:S(2)}) copy-start(f32[128,24,128]{2,1,0:T(8,128)} %all-gather.7.cloned.1.call-done) | copy-start | bytes 4718596
  76.1 49.2 %all-gather.11.cloned.1.call-start = ((), (), s32[]{:S(2)}) async-start(), calls=%async_computation.5 | async-start | bytes 1572864 | tf_op jit(solution)/shard_map/all_gather | solution.py:484
  87.5 3.9 %copy-start.14 = (s32[1,256]{1,0:T(1,128)S(1)}, s32[1,256]{1,0:T(1,128)}, u32[]{:S(2)}) copy-start(s32[1,256]{1,0:T(1,128)} %constant.14.clone.lane_order) | copy-start | bytes 3076
  87.5 3.9 %copy-start.17 = (f32[1,256]{1,0:T(1,128)S(1)}, f32[1,256]{1,0:T(1,128)}, u32[]{:S(2)}) copy-start(f32[1,256]{1,0:T(1,128)} %constant.15.clone.sign) | copy-start | bytes 3076
  87.5 1.4 %copy-start = (f32[128,24,128]{2,1,0:T(8,128)S(1)}, f32[128,24,128]{2,1,0:T(8,128)}, u32[]{:S(2)}) copy-start(f32[128,24,128]{2,1,0:T(8,128)} %all-gather.9.cloned.1.call-done) | copy-start | bytes 4718596
  90.5 1.4 %copy-start.1 = (f32[128,24,128]{2,1,0:T(8,128)S(1)}, f32[128,24,128]{2,1,0:T(8,128)}, u32[]{:S(2)}) copy-start(f32[128,24,128]{2,1,0:T(8,128)} %all-gather.9.cloned.1.call-done) | copy-start | bytes 4718596
  90.5 1.4 %copy-start.11 = (f32[8,512]{1,0:T(8,128)S(1)}, f32[8,512]{1,0:T(8,128)}, u32[]{:S(2)}) copy-start(f32[8,512]{1,0:T(8,128)} %copy-done.10) | copy-start | bytes 49156
  90.5 1.4 %copy-start.26 = (f32[8,512]{1,0:T(8,128)S(1)}, f32[8,512]{1,0:T(8,128)}, u32[]{:S(2)}) copy-start(f32[8,512]{1,0:T(8,128)} %copy-done.25) | copy-start | bytes 49156
  91.1 2.4 %collective-permute-start = (f32[4,512]{1,0:T(4,128)S(1)}, f32[4,512]{1,0:T(4,128)S(1)}, u32[]{:S(2)}, u32[]{:S(2)}) collective-permute-start(f32[4,512]{1,0:T(4,128)S(1)} %get-tuple-element.26), channel_id=1, source_target_pairs={{0,32},{32,0},{1,33},{33,1},{2,34},{34,2},{3,35},{35,3},{4,36},{36... | collective-permute-start | bytes 24584 | tf_op jit(solution)/shard_map/ppermute | solution.py:473
  91.9 1.5 %copy-start.31 = (pred[512]{0:T(512)(128)(4,1)S(1)}, pred[512]{0:T(512)(128)(4,1)}, u32[]{:S(2)}) copy-start(pred[512]{0:T(512)(128)(4,1)} %and_compare_fusion) | copy-start | bytes 1540
  93.4 31.9 %copy-start.9 = (f32[6,480]{1,0:T(8,128)S(1)}, f32[6,480]{1,0:T(8,128)}, u32[]{:S(2)}) copy-start(f32[6,480]{1,0:T(8,128)} %incident.3) | copy-start | bytes 34564
  93.4 31.9 %copy-start.12 = (f32[8,512]{1,0:T(8,128)S(1)}, f32[8,512]{1,0:T(8,128)}, u32[]{:S(2)}) copy-start(f32[8,512]{1,0:T(8,128)} %copy-done.10) | copy-start | bytes 49156
  93.4 31.9 %copy-start.15 = (s32[1,256]{1,0:T(1,128)S(1)}, s32[1,256]{1,0:T(1,128)}, u32[]{:S(2)}) copy-start(s32[1,256]{1,0:T(1,128)} %constant.14.clone.lane_order) | copy-start | bytes 3076
  93.5 31.9 %copy-start.18 = (f32[1,256]{1,0:T(1,128)S(1)}, f32[1,256]{1,0:T(1,128)}, u32[]{:S(2)}) copy-start(f32[1,256]{1,0:T(1,128)} %constant.15.clone.sign) | copy-start | bytes 3076
  125.4 1.2 copy-start.3
  (12 other events, 9.6 us)
Sparse Core Ops, SparseCore 0:
  35.8 11.5 all-gather.6
  76.2 11.1 all-gather.8
  115.3 9.9 all-gather.10

commit v2 on v1

--- a/solution.py
+++ b/solution.py
@@ -49,18 +49,25 @@
 _SOURCE = np.full((1, FULL), -1, np.int32)
 _SOURCE[0, :HALF] = _SORTED
 _SOURCE[0, WIDE : WIDE + HALF] = _SORTED + HALF
-_LANE_ORDER = np.full((1, WIDE), 99, np.int32)
-_LANE_ORDER[0, :HALF] = _ORDERS[_SORTED]
-_SIGN = np.zeros((1, WIDE), np.float32)
-_SIGN[0, :HALF] = np.sign(_ORDERS[_SORTED])
-
-
-def classes_of(half):
-    part = _LANE_ORDER[0, half * LANES : (half + 1) * LANES]
-    return [int(m) for m in np.unique(part[part < 99])]
-
-
-CLASSES = (classes_of(0), classes_of(1))
+
+
+def spans(half):
+    part = _ORDERS[_SORTED][half * LANES : (half + 1) * LANES]
+    found = []
+    for order in dict.fromkeys(int(m) for m in part):
+        lanes = np.flatnonzero(part == order)
+        found.append((order, int(lanes[0]), int(lanes[-1]) + 1))
+    return found
+
+
+SPANS = (spans(0), spans(1))
+
+
+def by_lane(lane, entries):
+    chosen = entries[-1][0]
+    for value, end in reversed(entries[:-1]):
+        chosen = jnp.where(lane < end, value, chosen)
+    return chosen
 
 
 def dot(a, b):
@@ -76,7 +83,7 @@
     return high, (x - high.astype(F32)).astype(BF)
 
 
-def exact_dot(x, onehot):
+def exact_dot(x, onehot, dot=dot):
     high = x.astype(BF)
     rest = x - high.astype(F32)
     mid = rest.astype(BF)
@@ -89,24 +96,28 @@
     return jnp.where(rows == source, 1.0, 0.0).astype(BF)
 
 
-def onehot_out(source_column):
-    lanes = lax.broadcasted_iota(jnp.int32, (FULL, COEFF), 1)
-    return jnp.where(lanes == source_column, 1.0, 0.0).astype(BF)
-
-
 def own_group():
     return lax.axis_index("xl") * 2 + lax.axis_index("co")
 
 
-def send_body(incident, source, radius, chunk, rows_out, radius_out, lines):
-    value = jnp.concatenate([incident[...], jnp.zeros((ROWS - OWN, COEFF), F32)], axis=0) * SCALE
-    rows = exact_dot(value, onehot_in(source[...]))
+def send_body(incident, source, radius, chunk, rows_out, radius_out, lines, held, held_source, held_radius, sems):
+    copies = [
+        pltpu.make_async_copy(incident, held.at[pl.ds(0, OWN), :], sems.at[0]),
+        pltpu.make_async_copy(source, held_source, sems.at[1]),
+        pltpu.make_async_copy(radius, held_radius, sems.at[2]),
+    ]
+    for copy in copies:
+        copy.start()
+    for copy in copies:
+        copy.wait()
+    value = jnp.concatenate([held[:OWN, :], jnp.zeros((ROWS - OWN, COEFF), F32)], axis=0) * SCALE
+    rows = exact_dot(value, onehot_in(held_source[...]))
     rows_out[...] = rows
     lane = lax.broadcasted_iota(jnp.int32, (ROWS, FULL), 1)
     line = lax.broadcasted_iota(jnp.int32, (ROWS, LANES), 0)
     column = jnp.zeros((ROWS, LANES), F32)
     for r in range(OWN):
-        column = jnp.where(line == r, radius[r], column)
+        column = jnp.where(line == r, held_radius[r], column)
     radius_out[...] = column
     marked = jnp.where(lane == PAD + own_group(), jnp.concatenate([column] * 4, axis=1), rows)
     write_chunks(marked, chunk, lines)
@@ -121,17 +132,23 @@
 
 
 def prepare_body(
-    site, jitter, rotation, axial, probes, tmat, source, source_column,
-    pairs, tables, tables_t, probes_out, tmat_out,
+    site, jitter, rotation, axial, probes, tmat, source,
+    pairs, tables, tables_t, probes_out, tmat_out, inwards_out,
 ):
     own = (
-        (lax.axis_index("co") * 2 + lax.axis_index("xl")) * PER_GROUP
+        lax.axis_index("xl") * PER_GROUP
         + ((lax.axis_index("z") * 2 + lax.axis_index("xh")) * 4 + lax.axis_index("y")) * OWN
     )
     sites = site[...]
-    place_x = (sites & 7).astype(F32) * LATTICE_STEP + jitter[0:1, :]
-    place_y = ((sites >> 3) & 7).astype(F32) * LATTICE_STEP + jitter[1:2, :]
-    place_z = (sites >> 6).astype(F32) * LATTICE_STEP + jitter[2:3, :]
+    core = lax.axis_index("co")
+
+    def own_core_first(place):
+        other = jnp.concatenate([place[:, SPHERES // 2 :], place[:, : SPHERES // 2]], axis=1)
+        return jnp.where(core == 0, place, other)
+
+    place_x = own_core_first((sites & 7).astype(F32) * LATTICE_STEP + jitter[0:1, :])
+    place_y = own_core_first(((sites >> 3) & 7).astype(F32) * LATTICE_STEP + jitter[1:2, :])
+    place_z = own_core_first((sites >> 6).astype(F32) * LATTICE_STEP + jitter[2:3, :])
     lane = lax.broadcasted_iota(jnp.int32, (ROWS, SPHERES), 1)
     line = lax.broadcasted_iota(jnp.int32, (ROWS, SPHERES), 0)
     same = lane == line + own
@@ -170,35 +187,44 @@
             )
 
     inwards = onehot_in(source[...])
-    outwards = onehot_out(source_column[...])
+    inwards_out[...] = inwards
+    outwards = inwards.astype(F32).T.astype(BF)
     turned = dot(outwards, rotation[...]).astype(BF)
     for radial in range(2):
         mixed_high, mixed_low = split(0.5 * dot(turned, axial[radial]))
         tables[radial] = (dot_t(mixed_high, turned) + dot_t(mixed_low, turned)).astype(BF)
         tables_t[radial] = (dot_t(turned, mixed_high) + dot_t(turned, mixed_low)).astype(BF)
-    probes_out[...] = dot(probes[...], inwards).astype(BF)
+    probes_out[...] = dot(outwards, probes[...]).astype(BF)
     tmat_rows = jnp.concatenate([tmat[...], jnp.zeros((ROWS - 2, HALF), F32)], axis=0)
     tmat_out[...] = exact_dot(tmat_rows, inwards[:HALF, :WIDE])
 
 
-def load_rows(gathered, rows):
-    for part in range(4):
-        lines = gathered[pl.ds(part, SPHERES, stride=4), :]
-        rows[:, part * LANES : (part + 1) * LANES] = lines.astype(BF)
-
-
-def group_sums(gathered):
-    groups = []
-    for place in (0, 2, 1, 3):
+def load_rows(near, peer, rows):
+    for which, lines in enumerate((near, peer)):
+        at = pl.ds(which * SPHERES // 2, SPHERES // 2)
+        for part in range(4):
+            value = lines[pl.ds(part, SPHERES // 2, stride=4), :]
+            rows[at, part * LANES : (part + 1) * LANES] = value.astype(BF)
+
+
+def group_sums(near, peer):
+    def total(lines, place):
         parts = []
         for part in range(4):
-            lines = gathered[pl.ds(place * PER_GROUP * 4 + part, PER_GROUP, stride=4), :]
-            parts.append(jnp.sum(lines, axis=0, keepdims=True))
-        groups.append(jnp.concatenate(parts, axis=1))
+            value = lines[pl.ds(place * PER_GROUP * 4 + part, PER_GROUP, stride=4), :]
+            parts.append(jnp.sum(value, axis=0, keepdims=True))
+        return jnp.concatenate(parts, axis=1)
+
+    core = lax.axis_index("co")
+    groups = []
+    for place in range(2):
+        mine, other = total(near, place), total(peer, place)
+        groups.append(jnp.where(core == 0, mine, other))
+        groups.append(jnp.where(core == 0, other, mine))
     return jnp.concatenate(groups, axis=0)
 
 
-def mix(sums, shifted, tables, lane_order, sign):
+def mix(sums, shifted, tables):
     for k in range(1, TOP + 1):
         at_cos, at_sin = pl.ds(k * BLOCK, BLOCK), pl.ds((TOP + k) * BLOCK, BLOCK)
         cos_re, cos_im = sums[at_cos, :WIDE], sums[at_cos, WIDE:]
@@ -212,17 +238,15 @@
         return (k if k >= 0 else TOP - k) * BLOCK
 
     for half in range(2):
-        orders = jnp.broadcast_to(lane_order[:, half * LANES : (half + 1) * LANES], (BLOCK, LANES))
-        masks = [orders == m for m in CLASSES[half]]
+        lane = lax.broadcasted_iota(jnp.int32, (BLOCK, LANES), 1)
 
         def pick(out_order, start):
             columns = slice(start + half * LANES, start + (half + 1) * LANES)
-            value = None
-            for m, mask in zip(CLASSES[half], masks):
-                row = block_of(m - out_order)
-                here = sums[row : row + BLOCK, columns]
-                value = here if value is None else jnp.where(mask, here, value)
-            return value
+            entries = []
+            for order, _, end in SPANS[half]:
+                row = block_of(order - out_order)
+                entries.append((sums[row : row + BLOCK, columns], end))
+            return by_lane(lane, entries)
 
         for out_order in range(ORDER + 1):
             minus_re, minus_im = pick(out_order, 0), pick(out_order, WIDE)
@@ -241,21 +265,24 @@
 
     back = dot(shifted[0], tables[0]) + dot(shifted[1], tables[1])
     parts_re, parts_im = [], []
+    lane = lax.broadcasted_iota(jnp.int32, (ROWS, LANES), 1)
     for half in range(2):
-        columns = slice(half * LANES, (half + 1) * LANES)
-        orders = jnp.abs(jnp.broadcast_to(lane_order[:, columns], (ROWS, LANES)))
-        signs = sign[:, columns]
-        field_re = field_im = None
-        for m in sorted({abs(c) for c in CLASSES[half]}):
+        real = slice(half * LANES, (half + 1) * LANES)
+        imag = slice(WIDE + half * LANES, WIDE + (half + 1) * LANES)
+        entries_re, entries_im = [], []
+        for order, _, end in SPANS[half]:
+            m = abs(order)
             cos_lines = slice(m * BLOCK, m * BLOCK + ROWS)
             sin_lines = slice(m * BLOCK + ROWS, (m + 1) * BLOCK)
-            real, imag = columns, slice(WIDE + half * LANES, WIDE + (half + 1) * LANES)
-            value_re = back[cos_lines, real] + signs * back[sin_lines, imag]
-            value_im = back[cos_lines, imag] - signs * back[sin_lines, real]
-            field_re = value_re if field_re is None else jnp.where(orders == m, value_re, field_re)
-            field_im = value_im if field_im is None else jnp.where(orders == m, value_im, field_im)
-        parts_re.append(field_re)
-        parts_im.append(field_im)
+            value_re, value_im = back[cos_lines, real], back[cos_lines, imag]
+            if order > 0:
+                value_re, value_im = value_re + back[sin_lines, imag], value_im - back[sin_lines, real]
+            if order < 0:
+                value_re, value_im = value_re - back[sin_lines, imag], value_im + back[sin_lines, real]
+            entries_re.append((value_re, end))
+            entries_im.append((value_im, end))
+        parts_re.append(by_lane(lane, entries_re))
+        parts_im.append(by_lane(lane, entries_im))
     return jnp.concatenate(parts_re + parts_im, axis=1)
 
 
@@ -273,33 +300,33 @@
 
 
 def first_body(
-    gathered, pairs, tables, tmat, radius, lane_order, sign,
+    near, peer, pairs, tables, tmat, radius,
     chunk, rows_out, weights_out, totals_out, rows, sums, shifted, lines,
 ):
-    load_rows(gathered, rows)
-    totals_out[...] = group_sums(gathered)
+    load_rows(near, peer, rows)
+    totals_out[...] = group_sums(near, peer)
     sums[...] = dot(pairs[...], rows[...])
     for block in range(BLOCKS):
         k = block if block <= TOP else block - TOP
         at = pl.ds(block * BLOCK, BLOCK)
         value = sums[at, LANES:WIDE]
         weights_out[at, :] = (value if k % 2 == 0 else -value).astype(BF)
-    field = mix(sums, shifted, tables, lane_order, sign)
+    field = mix(sums, shifted, tables)
     image = scatter(field, tmat, radius[...])
     rows_out[...] = image
     write_chunks(image, chunk, lines)
 
 
-def gradient_body(gathered, totals_first, probes, probe_group, keep, send):
-    totals = jnp.concatenate([totals_first[...], group_sums(gathered)], axis=0)
+def gradient_body(near, peer, totals_first, probes, probe_group, keep, send):
+    totals = jnp.concatenate([totals_first[...], group_sums(near, peer)], axis=0)
     lane = lax.broadcasted_iota(jnp.int32, (2 * GROUPS, FULL), 1)
     totals = jnp.where((lane & (WIDE - 1)) < HALF, totals, 0.0)
     total_high, total_low = split(totals)
-    values = dot_t(total_high, probes[...]) + dot_t(total_low, probes[...])
+    values = dot(total_high, probes[...]) + dot(total_low, probes[...])
     line = lax.broadcasted_iota(jnp.int32, (2 * GROUPS, PROBES_OWN), 0)
     values = jnp.where((line & (GROUPS - 1)) == probe_group[...], values, 0.0)
     value_high, value_low = split(values)
-    gradient = dot(value_high, probes[...]) + dot(value_low, probes[...])
+    gradient = dot_t(value_high, probes[...]) + dot_t(value_low, probes[...])
     core = lax.axis_index("co")
     first, second = gradient[:GROUPS], gradient[GROUPS:]
     keep[...] = jnp.where(core == 0, first, second)
@@ -307,12 +334,12 @@
 
 
 def second_body(
-    gathered, pairs, tables, tmat, radius, lane_order, sign, base, image,
+    near, peer, pairs, tables, tmat, radius, base, image,
     scalars, rows, sums, shifted,
 ):
-    load_rows(gathered, rows)
+    load_rows(near, peer, rows)
     sums[...] = dot(pairs[...], rows[...])
-    field = mix(sums, shifted, tables, lane_order, sign)
+    field = mix(sums, shifted, tables)
     last = scatter(field, tmat, radius[...])
     zero, one = base[...], image[...]
     line = lax.broadcasted_iota(jnp.int32, (GROUPS, FULL), 0)
@@ -325,11 +352,12 @@
 
 
 def finish_body(
-    parts, weights, tables_t, tmat, lane_order, sign, source_column, incident, image,
+    near, peer, weights, tables_t, tmat, inwards, incident, image,
     solution_out, sensitivity_out, arnoldi_out, places, sums, shifted,
 ):
-    first = jnp.sum(parts[0], axis=0)
-    second = jnp.sum(parts[1], axis=0)
+    mine, other = jnp.sum(near[...], axis=0), jnp.sum(peer[...], axis=0)
+    core = lax.axis_index("co")
+    first, second = jnp.where(core == 0, mine, other), jnp.where(core == 0, other, mine)
     scal = (first + second)[0:1, :]
     g00, s01, s11, s02, s12, s22 = [scal[:, PAD + i : PAD + i + 1] for i in range(6)]
     g01, g11, g02, g12, g22 = s01 / g00, s11 / g00, s02 / g00, s12 / g00, s22 / g00
@@ -363,7 +391,7 @@
     places[at, :WIDE] = real * grad_re + imag * grad_im
     places[at, WIDE:] = real * grad_im - imag * grad_re
     sums[...] = dot(weights[...], places[...].astype(BF))
-    field = mix(sums, shifted, tables_t, lane_order, sign)
+    field = mix(sums, shifted, tables_t)
     group = own_group()
     own = jnp.zeros((1, FULL), F32)
     for g in range(GROUPS):
@@ -371,29 +399,35 @@
     lane = lax.broadcasted_iota(jnp.int32, (1, FULL), 1)
     own = jnp.where((lane & (WIDE - 1)) < HALF, own, 0.0)
     both = jnp.concatenate([image[...], own - field], axis=0)
-    result = exact_dot(both, onehot_out(source_column[...]))
+    result = exact_dot(both, inwards[...], dot_t)
     image_rows = result[:OWN]
     solution_out[...] = for_base * incident[...] + (for_image / SCALE) * image_rows
     sensitivity_out[...] = result[ROWS : ROWS + OWN]
 
 
-def call(body, outs, scratch=(), operands=(), smem=(), smem_outs=(), cost=None):
-    vmem = pl.BlockSpec(memory_space=pltpu.VMEM)
-    scalar = pl.BlockSpec(memory_space=pltpu.SMEM)
+def call(body, outs, scratch=(), operands=(), spaces=None, smem_outs=(), cost=None):
+    spaces = spaces or {}
     return pl.pallas_call(
         body,
         out_shape=[jax.ShapeDtypeStruct(shape, kind) for shape, kind in outs],
-        in_specs=[scalar if i in smem else vmem for i in range(len(operands))],
-        out_specs=[scalar if i in smem_outs else vmem for i in range(len(outs))],
+        in_specs=[pl.BlockSpec(memory_space=spaces.get(i, pltpu.VMEM)) for i in range(len(operands))],
+        out_specs=[
+            pl.BlockSpec(memory_space=pltpu.SMEM if i in smem_outs else pltpu.VMEM) for i in range(len(outs))
+        ],
         scratch_shapes=list(scratch),
-        compiler_params=pltpu.CompilerParams(vmem_limit_bytes=40 * 1024 * 1024),
+        compiler_params=pltpu.CompilerParams(vmem_limit_bytes=16 * 1024 * 1024),
         cost_estimate=cost,
     )(*operands)
 
 
+def swap_cores(array):
+    return lax.ppermute(array, "co", [(0, 1), (1, 0)])
+
+
 def exchange(chunk):
-    far = lax.all_to_all(chunk, FAR_AXES, 0, 0)
-    return lax.all_gather(far, "co").reshape(2 * FAR * CHUNK, LANES)
+    near = lax.all_to_all(chunk, FAR_AXES, 0, 0)
+    peer = swap_cores(near)
+    return near.reshape(FAR * CHUNK, LANES), peer.reshape(FAR * CHUNK, LANES)
 
 
 def on_device(
@@ -408,41 +442,44 @@
     probe_group,
 ):
     source = jnp.asarray(_SOURCE)
-    source_column = jnp.asarray(_SOURCE.reshape(FULL, 1))
-    lane_order = jnp.asarray(_LANE_ORDER)
-    sign = jnp.asarray(_SIGN)
-
+    line_scratch = pltpu.VMEM((4 * ROWS, LANES), F32)
     chunk, base, radius = call(
         send_body,
         [((FAR, CHUNK, LANES), F32), ((ROWS, FULL), F32), ((ROWS, LANES), F32)],
-        [pltpu.VMEM((4 * ROWS, LANES), F32)],
+        [
+            line_scratch,
+            pltpu.VMEM((ROWS, COEFF), F32),
+            pltpu.VMEM((1, FULL), jnp.int32),
+            pltpu.SMEM((OWN,), F32),
+            pltpu.SemaphoreType.DMA((3,)),
+        ],
         (incident, source, radius_factor),
-        smem=(2,),
-    )
-    gathered_base = exchange(chunk)
+        {0: pl.ANY, 1: pl.ANY, 2: pl.ANY},
+    )
+    near, peer = exchange(chunk)
 
     def by_core(array):
         lead = array.shape[:-1]
         return jnp.swapaxes(array.reshape(lead + (2, 2, PER_GROUP)), -3, -2).reshape(lead + (SPHERES,))
 
-    pairs, tables, tables_t, probes, tmat = call(
+    pairs, tables, tables_t, probes, tmat, inwards = call(
         prepare_body,
         [
             ((BLOCKS * BLOCK, SPHERES), BF),
             ((2, FULL, FULL), BF),
             ((2, FULL, FULL), BF),
-            ((PROBES_OWN, FULL), BF),
+            ((FULL, PROBES_OWN), BF),
             ((ROWS, WIDE), F32),
+            ((COEFF, FULL), BF),
         ],
         operands=(
             by_core(sphere_site[None, :]),
             by_core(jitter),
             rotation_table,
             axial_tables,
-            probe_field,
+            probe_field.T,
             tmatrix,
             source,
-            source_column,
         ),
         cost=pl.CostEstimate(flops=6_000_000_000, bytes_accessed=8_000_000, transcendentals=20_000),
     )
@@ -450,7 +487,6 @@
     row_scratch = pltpu.VMEM((SPHERES, FULL), BF)
     sum_scratch = pltpu.VMEM((BLOCKS * BLOCK, FULL), F32)
     shift_scratch = pltpu.VMEM((2, (ORDER + 1) * BLOCK, FULL), BF)
-    line_scratch = pltpu.VMEM((4 * ROWS, LANES), F32)
 
     chunk, image, weights, totals_first = call(
         first_body,
@@ -461,32 +497,33 @@
             ((GROUPS, FULL), F32),
         ],
         [row_scratch, sum_scratch, shift_scratch, line_scratch],
-        (gathered_base, pairs, tables, tmat, radius, lane_order, sign),
-    )
-    gathered_image = exchange(chunk)
+        (near, peer, pairs, tables, tmat, radius),
+    )
+    near, peer = exchange(chunk)
 
     keep, send = call(
         gradient_body,
         [((GROUPS, FULL), F32), ((GROUPS, FULL), F32)],
-        operands=(gathered_image, totals_first, probes, probe_group.reshape(1, PROBES_OWN)),
-    )
-    received = lax.ppermute(send, "co", [(0, 1), (1, 0)])
+        operands=(near, peer, totals_first, probes, probe_group.reshape(1, PROBES_OWN)),
+    )
+    received = swap_cores(send)
     (scalars,) = call(
         second_body,
         [((GROUPS, FULL), F32)],
         [row_scratch, sum_scratch, shift_scratch],
-        (gathered_image, pairs, tables, tmat, radius, lane_order, sign, base, image),
+        (near, peer, pairs, tables, tmat, radius, base, image),
         cost=pl.CostEstimate(flops=1_000_000_000, bytes_accessed=8_000_000, transcendentals=0),
     )
-    lane = jnp.arange(FULL, dtype=jnp.int32)
+    lane = lax.broadcasted_iota(jnp.int32, (GROUPS, FULL), 1)
     share = jnp.where((lane & (WIDE - 1)) < HALF, keep + received, scalars)
     spread = jnp.broadcast_to(share[None], (FAR, GROUPS, FULL))
-    parts = lax.all_gather(lax.all_to_all(spread, FAR_AXES, 0, 0), "co")
+    near = lax.all_to_all(spread, FAR_AXES, 0, 0)
+    peer = swap_cores(near)
     solution_rows, sensitivity_rows, arnoldi = call(
         finish_body,
         [((OWN, COEFF), F32), ((OWN, COEFF), F32), ((4,), F32)],
         [pltpu.VMEM((LANES, FULL), F32), sum_scratch, shift_scratch],
-        (parts, weights, tables_t, tmat, lane_order, sign, source_column, incident, image),
+        (near, peer, weights, tables_t, tmat, inwards, incident, image),
         smem_outs=(2,),
     )
     return solution_rows, sensitivity_rows, arnoldi

time: 137 us -> 89.4 us (0.65)
  waiting for transfers between devices: 23.7 us -> 3.45 us
  between operations: 14 us -> 0.75 us
  local copies, waits for them, and re-layouts: 15.6 us -> 5.32 us
  blocking collectives: 70.8 us -> 61.5 us
  starting transfers between devices: 0.35 us -> 7.32 us
    all_gather x3 -> x0, waiting for transfers between devices: 23.7 us -> none  [the longest x2 13.6 us: exchange(): return lax.all_gather(far, 'co').reshape(2 * FAR * CHUNK, LANES)]
    unnamed x65 -> x24, local copies, waits for them, and re-layouts: 15.2 us -> 4.89 us
    all_to_all x3, blocking collectives: 70.8 us -> 61.5 us  [the longest x2 44.6 us: exchange(): near = lax.all_to_all(chunk, FAR_AXES, 0, 0)]
    ppermute x1 -> x4, starting transfers between devices: 0.23 us -> 7.32 us  [swap_cores(): return lax.ppermute(array, 'co', [(0, 1), (1, 0)])]
    ppermute x1 -> x4, waiting for transfers between devices: 0.01 us -> 3.45 us  [swap_cores(): return lax.ppermute(array, 'co', [(0, 1), (1, 0)])]
  transfers between devices with their start and end apart: 4 -> 4, of which waited for: 3 -> 2; matrix products, arithmetic and copies ran while one was open for 1% -> 0% of each run, Pallas kernels for 4% -> 6%
where the time goes in v2:
time: 89.4 us; the launch traced here: 89 us
  blocking collectives  61.5 us (69%)
  Pallas kernels  10.7 us (12%)
  starting transfers between devices  7.32 us (8%)
  local copies, waits for them, and re-layouts  5.32 us (6%)
  waiting for transfers between devices  3.45 us (4%)
    all_to_all x2, blocking collectives, exchange(): near = lax.all_to_all(chunk, FAR_AXES, 0, 0)  44.6 us
    all_to_all x1, blocking collectives, on_device(): near = lax.all_to_all(spread, FAR_AXES, 0, 0)  16.9 us
    pallas_call x6, Pallas kernels, call(): pl.pallas_call(body, out_shape=[jax.ShapeDtypeStruct(shape, kind) for sha...  10.7 us
    ppermute x4, starting transfers between devices, swap_cores(): return lax.ppermute(array, 'co', [(0, 1), (1, 0)])  7.32 us
    unnamed x24, local copies, waits for them, and re-layouts  4.89 us
    ppermute x4, waiting for transfers between devices, swap_cores(): return lax.ppermute(array, 'co', [(0, 1), (1, 0)])  3.45 us
  transfers between devices with their start and end apart: 4, of which 2 were waited for; matrix products, arithmetic and copies ran while one was open for 0% of the time, Pallas kernels for 6%

profile of v2, /device:TPU:1, one launch (start us, length us, event | category | flops | bytes accessed | tf_op | source)
XLA Modules:
  0.0 89.0 jit_solution(3635816781768993300)
XLA Ops:
  0.6 0.7 copy-done
  1.4 0.7 copy-done.2
  2.0 0.7 copy-done.5
  2.7 1.0 %shard_map.121 = (f32[64,24,128]{2,1,0:T(8,128)S(1)}, f32[8,512]{1,0:T(8,128)S(1)}, f32[8,128]{1,0:T(8,128)S(1)}) custom-call(f32[6,480]{1,0:T(8,128)S(1)} %copy-done, s32[1,512]{1,0:T(1,128)S(1)} %copy-done.2, f32[6]{0:T(128)S(1)} %copy-done.5), custom_call_target="tpu_custom_call" | custom-call | tf_op jit(solution)/shard_map/pallas_call | solution.py:410
  3.7 25.4 %all_to_all.15 = f32[64,24,128]{2,1,0:T(8,128)S(1)} all-to-all(f32[64,24,128]{2,1,0:T(8,128)S(1)} %get-tuple-element.18), channel_id=1, replica_groups=mesh['xl'=2,'co'=2,'z'=4,'xh'=2,'y'=4] {'xl','z','xh','y'}, dimensions={0} | all-to-all | bytes 1572864 | tf_op jit(solution)/shard_map/all_to_all | solution.py:428
  29.1 2.9 %collective-permute-start = (f32[64,24,128]{2,1,0:T(8,128)S(1)}, f32[64,24,128]{2,1,0:T(8,128)S(1)}, u32[]{:S(2)}, u32[]{:S(2)}) collective-permute-start(f32[64,24,128]{2,1,0:T(8,128)S(1)} %all_to_all.15), channel_id=1, source_target_pairs={{0,32},{32,0},{1,33},{33,1},{2,34},{34,2},{3,35},{35,3},{4,36},{36... | collective-permute-start | bytes 2359304 | tf_op jit(solution)/shard_map/ppermute | solution.py:424
  31.9 0.1 reshape.34
  32.1 0.1 reshape.35.jitter
  32.1 0.6 copy-done.11
  32.9 0.6 copy-done.3
  33.5 0.9 %copy-done.8 = bf16[256,480]{0,1:T(8,128)(2,1)S(1)} copy-done((bf16[256,480]{0,1:T(8,128)(2,1)S(1)}, bf16[256,480]{0,1:T(8,128)(2,1)}, u32[]{:S(2)}) %copy-start.8) | copy-done | bytes 245784
  34.5 3.6 %shard_map.122 = (bf16[656,768]{1,0:T(8,128)(2,1)S(1)}, bf16[2,512,512]{2,1,0:T(8,128)(2,1)S(1)}, bf16[2,512,512]{2,1,0:T(8,128)(2,1)S(1)}, bf16[512,256]{1,0:T(...) custom-call(s32[1,768]{1,0:T(1,128)S(1)} %reshape.33.site, f32[3,768]{1,0:T(4,128)S(1)} %reshape.35.jitter, ...), custom_call_target="tpu_custom_call" | custom-call | flops 6000000000 | bytes 8000000 | tf_op jit(solution)/shard_map/pallas_call | solution.py:410
  38.1 1.4 %shard_map.123 = (f32[64,24,128]{2,1,0:T(8,128)S(1)}, f32[8,512]{1,0:T(8,128)S(1)}, bf16[656,128]{1,0:T(8,128)(2,1)S(1)}, f32[4,512]{1,0:T(4,128)S(1)}) custom-call(f32[1536,128]{1,0:T(8,128)S(1)} %bitcast.12, f32[1536,128]{1,0:T(8,128)S(1)} %bitcast.15, bf16[656,768]{1,0:T(8,128)(2,1)S(1)} %get-tuple-element.19.pairs, ...), custom_call_target="tpu_custom_call" | custom-call | tf_op jit(solution)/shard_map/pallas_call | solution.py:410
  39.5 19.2 %all_to_all.16 = f32[64,24,128]{2,1,0:T(8,128)S(1)} all-to-all(f32[64,24,128]{2,1,0:T(8,128)S(1)} %get-tuple-element.23), channel_id=1, replica_groups=mesh['xl'=2,'co'=2,'z'=4,'xh'=2,'y'=4] {'xl','z','xh','y'}, dimensions={0} | all-to-all | bytes 1572864 | tf_op jit(solution)/shard_map/all_to_all | solution.py:428
  58.8 1.9 %collective-permute-start.1 = (f32[64,24,128]{2,1,0:T(8,128)S(1)}, f32[64,24,128]{2,1,0:T(8,128)S(1)}, u32[]{:S(2)}, u32[]{:S(2)}) collective-permute-start(f32[64,24,128]{2,1,0:T(8,128)S(1)} %all_to_all.16), channel_id=1, source_target_pairs={{0,32},{32,0},{1,33},{33,1},{2,34},{34,2},{3,35},{35,3},{4,36},{36... | collective-permute-start | bytes 2359304 | tf_op jit(solution)/shard_map/ppermute | solution.py:424
  60.6 1.9 %collective-permute-done.1 = f32[64,24,128]{2,1,0:T(8,128)S(1)} collective-permute-done((f32[64,24,128]{2,1,0:T(8,128)S(1)}, f32[64,24,128]{2,1,0:T(8,128)S(1)}, u32[]{:S(2)}, u32[]{:S(2)}) %collective-permute-start.1) | collective-permute-done | bytes 786464 | tf_op jit(solution)/shard_map/ppermute | solution.py:424
  62.5 0.7 copy-done.4
  63.2 0.6 shard_map.124
  63.8 0.4 collective-permute-start.2
  64.2 1.5 %shard_map.125 = f32[4,512]{1,0:T(4,128)S(1)} custom-call(f32[1536,128]{1,0:T(8,128)S(1)} %bitcast.11, f32[1536,128]{1,0:T(8,128)S(1)} %bitcast.14, bf16[656,768]{1,0:T(8,128)(2,1)S(1)} %get-tuple-element.19.pairs, bf16[2,512,512]{2,1,0:T(8,128)(2,1)S(1)} %get-tuple-element.20.tables, f32[8,256]{1,0:T(8,128)S(1)} %get-tuple-element.21.tmat, ...), custom_call_target="tpu_custom_call" | custom-call | flops 1000000000 | bytes 8000000 | tf_op jit(solution)/shard_map/pallas_call | solution.py:410
  65.8 16.9 %all_to_all.17.near = f32[64,4,512]{2,1,0:T(4,128)S(1)} all-to-all(f32[64,4,512]{2,1,0:T(4,128)S(1)} %broadcast_in_dim.2), channel_id=1, replica_groups=mesh['xl'=2,'co'=2,'z'=4,'xh'=2,'y'=4] {'xl','z','xh','y'}, dimensions={0} | all-to-all | bytes 1048576 | tf_op jit(solution)/shard_map/all_to_all | solution.py:520
  82.6 2.2 %collective-permute-start.3 = (f32[64,4,512]{2,1,0:T(4,128)S(1)}, f32[64,4,512]{2,1,0:T(4,128)S(1)}, u32[]{:S(2)}, u32[]{:S(2)}) collective-permute-start(f32[64,4,512]{2,1,0:T(4,128)S(1)} %all_to_all.17.near), channel_id=1, source_target_pairs={{0,32},{32,0},{1,33},{33,1},{2,34},{34,2},{3,35},{35,3},{4,36},{36... | collective-permute-start | bytes 1572872 | tf_op jit(solution)/shard_map/ppermute | solution.py:424
  84.8 1.5 %collective-permute-done.3.peer = f32[64,4,512]{2,1,0:T(4,128)S(1)} collective-permute-done((f32[64,4,512]{2,1,0:T(4,128)S(1)}, f32[64,4,512]{2,1,0:T(4,128)S(1)}, u32[]{:S(2)}, u32[]{:S(2)}) %collective-permute-start.3) | collective-permute-done | bytes 524320 | tf_op jit(solution)/shard_map/ppermute | solution.py:424
  86.3 2.6 %shard_map.126 = (f32[6,480]{1,0:T(8,128)}, f32[6,480]{1,0:T(8,128)}, f32[4]{0:T(128)}) custom-call(f32[64,4,512]{2,1,0:T(4,128)S(1)} %all_to_all.17.near, f32[64,4,512]{2,1,0:T(4,128)S(1)} %collective-permute-done.3.peer, bf16[656,128]{1,0:T(8,128)(2,1)S(1)} %get-tuple-element.30.weights, bf16[2,512,512]{2,1,0:T(8,128)(2,1)S(1)} %get-tuple-element.31.tables_t, ...), custom_call_target="tpu_custom_call" | custom-call | tf_op jit(solution)/shard_map/pallas_call | solution.py:410
  (26 shorter events, 0.3 us)
Async XLA Ops:
  0.6 0.7 copy-start
  1.4 0.7 copy-start.2
  2.0 0.7 copy-start.5
  2.7 30.2 %copy-start.6 = (bf16[2,480,480]{2,1,0:T(8,128)(2,1)S(1)}, bf16[2,480,480]{2,1,0:T(8,128)(2,1)}, u32[]{:S(2)}) copy-start(bf16[2,480,480]{2,1,0:T(8,128)(2,1)} %axial.1) | copy-start | bytes 2764804
  3.7 28.3 %copy-start.10 = (f32[3,768]{1,0:T(4,128)S(1)}, f32[3,768]{1,0:T(4,128)}, u32[]{:S(2)}) copy-start(f32[3,768]{1,0:T(4,128)} %param.12) | copy-start | bytes 27652
  3.7 29.3 %copy-start.7 = (bf16[480,480]{1,0:T(8,128)(2,1)S(1)}, bf16[480,480]{1,0:T(8,128)(2,1)}, u32[]{:S(2)}) copy-start(bf16[480,480]{1,0:T(8,128)(2,1)} %rotation.1) | copy-start | bytes 1382404
  29.1 9.1 %collective-permute-start = (f32[64,24,128]{2,1,0:T(8,128)S(1)}, f32[64,24,128]{2,1,0:T(8,128)S(1)}, u32[]{:S(2)}, u32[]{:S(2)}) collective-permute-start(f32[64,24,128]{2,1,0:T(8,128)S(1)} %all_to_all.15), channel_id=1, source_target_pairs={{0,32},{32,0},{1,33},{33,1},{2,34},{34,2},{3,35},{35,3},{4,36},{36... | collective-permute-start | bytes 2359304 | tf_op jit(solution)/shard_map/ppermute | solution.py:424
  32.0 0.7 copy-start.11
  32.8 0.7 copy-start.3
  32.8 0.7 copy-start.9
  33.5 0.9 %copy-start.8 = (bf16[256,480]{0,1:T(8,128)(2,1)S(1)}, bf16[256,480]{0,1:T(8,128)(2,1)}, u32[]{:S(2)}) copy-start(bf16[256,480]{0,1:T(8,128)(2,1)} %param.17) | copy-start | bytes 737284
  58.8 3.8 %collective-permute-start.1 = (f32[64,24,128]{2,1,0:T(8,128)S(1)}, f32[64,24,128]{2,1,0:T(8,128)S(1)}, u32[]{:S(2)}, u32[]{:S(2)}) collective-permute-start(f32[64,24,128]{2,1,0:T(8,128)S(1)} %all_to_all.16), channel_id=1, source_target_pairs={{0,32},{32,0},{1,33},{33,1},{2,34},{34,2},{3,35},{35,3},{4,36},{36... | collective-permute-start | bytes 2359304 | tf_op jit(solution)/shard_map/ppermute | solution.py:424
  62.5 0.7 copy-start.4
  63.8 1.9 %collective-permute-start.2 = (f32[4,512]{1,0:T(4,128)S(1)}, f32[4,512]{1,0:T(4,128)S(1)}, u32[]{:S(2)}, u32[]{:S(2)}) collective-permute-start(f32[4,512]{1,0:T(4,128)S(1)} %get-tuple-element.27), channel_id=1, source_target_pairs={{0,32},{32,0},{1,33},{33,1},{2,34},{34,2},{3,35},{35,3},{4,36},{36... | collective-permute-start | bytes 24584 | tf_op jit(solution)/shard_map/ppermute | solution.py:424
  65.7 20.6 %copy-start.1 = (f32[6,480]{1,0:T(8,128)S(1)}, f32[6,480]{1,0:T(8,128)}, u32[]{:S(2)}) copy-start(f32[6,480]{1,0:T(8,128)} %incident.3) | copy-start | bytes 34564
  82.6 3.7 %collective-permute-start.3 = (f32[64,4,512]{2,1,0:T(4,128)S(1)}, f32[64,4,512]{2,1,0:T(4,128)S(1)}, u32[]{:S(2)}, u32[]{:S(2)}) collective-permute-start(f32[64,4,512]{2,1,0:T(4,128)S(1)} %all_to_all.17.near), channel_id=1, source_target_pairs={{0,32},{32,0},{1,33},{33,1},{2,34},{34,2},{3,35},{35,3},{4,36},{36... | collective-permute-start | bytes 1572872 | tf_op jit(solution)/shard_map/ppermute | solution.py:424

commit v3 on v2

--- a/solution.py
+++ b/solution.py
@@ -78,17 +78,20 @@
     return lax.dot_general(a, b, (((1,), (1,)), ((), ())), preferred_element_type=F32)
 
 
-def split(x):
-    high = x.astype(BF)
-    return high, (x - high.astype(F32)).astype(BF)
-
-
-def exact_dot(x, onehot, dot=dot):
-    high = x.astype(BF)
-    rest = x - high.astype(F32)
-    mid = rest.astype(BF)
-    low = (rest - mid.astype(F32)).astype(BF)
-    return dot(high, onehot) + dot(mid, onehot) + dot(low, onehot)
+def fine_dot(x, y, dot=dot, parts=3):
+    rows = x.shape[0]
+    padded = -(-rows // 16) * 16
+    if padded > rows:
+        x = jnp.concatenate([x, jnp.zeros((padded - rows, x.shape[1]), F32)], axis=0)
+    terms = []
+    for _ in range(parts):
+        terms.append(x.astype(BF))
+        x = x - terms[-1].astype(F32)
+    product = dot(jnp.concatenate(terms, axis=0), y)
+    total = product[:rows]
+    for part in range(1, parts):
+        total = total + product[part * padded : part * padded + rows]
+    return total
 
 
 def onehot_in(source):
@@ -100,27 +103,10 @@
     return lax.axis_index("xl") * 2 + lax.axis_index("co")
 
 
-def send_body(incident, source, radius, chunk, rows_out, radius_out, lines, held, held_source, held_radius, sems):
-    copies = [
-        pltpu.make_async_copy(incident, held.at[pl.ds(0, OWN), :], sems.at[0]),
-        pltpu.make_async_copy(source, held_source, sems.at[1]),
-        pltpu.make_async_copy(radius, held_radius, sems.at[2]),
-    ]
-    for copy in copies:
-        copy.start()
-    for copy in copies:
-        copy.wait()
-    value = jnp.concatenate([held[:OWN, :], jnp.zeros((ROWS - OWN, COEFF), F32)], axis=0) * SCALE
-    rows = exact_dot(value, onehot_in(held_source[...]))
-    rows_out[...] = rows
-    lane = lax.broadcasted_iota(jnp.int32, (ROWS, FULL), 1)
-    line = lax.broadcasted_iota(jnp.int32, (ROWS, LANES), 0)
-    column = jnp.zeros((ROWS, LANES), F32)
-    for r in range(OWN):
-        column = jnp.where(line == r, held_radius[r], column)
-    radius_out[...] = column
-    marked = jnp.where(lane == PAD + own_group(), jnp.concatenate([column] * 4, axis=1), rows)
-    write_chunks(marked, chunk, lines)
+def send_body(incident, chunk, lines):
+    value = jnp.concatenate([incident[...], jnp.zeros((ROWS - OWN, COEFF), F32)], axis=0) * SCALE
+    value = jnp.concatenate([value, jnp.zeros((ROWS, FULL - COEFF), F32)], axis=1)
+    write_chunks(value, chunk, lines)
 
 
 def write_chunks(rows, chunk, lines):
@@ -132,8 +118,8 @@
 
 
 def prepare_body(
-    site, jitter, rotation, axial, probes, tmat, source,
-    pairs, tables, tables_t, probes_out, tmat_out, inwards_out,
+    site, jitter, rotation, axial, probe_group, tmat, source, incident, radius,
+    pairs, tables, seen_out, tmat_out, inwards_out, base_out, radius_out,
 ):
     own = (
         lax.axis_index("xl") * PER_GROUP
@@ -191,40 +177,47 @@
     outwards = inwards.astype(F32).T.astype(BF)
     turned = dot(outwards, rotation[...]).astype(BF)
     for radial in range(2):
-        mixed_high, mixed_low = split(0.5 * dot(turned, axial[radial]))
-        tables[radial] = (dot_t(mixed_high, turned) + dot_t(mixed_low, turned)).astype(BF)
-        tables_t[radial] = (dot_t(turned, mixed_high) + dot_t(turned, mixed_low)).astype(BF)
-    probes_out[...] = dot(outwards, probes[...]).astype(BF)
+        tables[radial] = fine_dot(0.5 * dot(turned, axial[radial]), turned, dot_t, 2).astype(BF)
+    line = lax.broadcasted_iota(jnp.int32, (GROUPS, PROBES_OWN), 0)
+    seen_out[...] = jnp.where(line == probe_group[...], 1.0, 0.0)
     tmat_rows = jnp.concatenate([tmat[...], jnp.zeros((ROWS - 2, HALF), F32)], axis=0)
-    tmat_out[...] = exact_dot(tmat_rows, inwards[:HALF, :WIDE])
-
-
-def load_rows(near, peer, rows):
-    for which, lines in enumerate((near, peer)):
-        at = pl.ds(which * SPHERES // 2, SPHERES // 2)
-        for part in range(4):
-            value = lines[pl.ds(part, SPHERES // 2, stride=4), :]
-            rows[at, part * LANES : (part + 1) * LANES] = value.astype(BF)
-
-
-def group_sums(near, peer):
-    def total(lines, place):
+    tmat_out[...] = fine_dot(tmat_rows, inwards[:HALF, :WIDE])
+    value = jnp.concatenate([incident[...], jnp.zeros((ROWS - OWN, COEFF), F32)], axis=0) * SCALE
+    base_out[...] = fine_dot(value, inwards)
+    line = lax.broadcasted_iota(jnp.int32, (ROWS, LANES), 0)
+    column = jnp.zeros((ROWS, LANES), F32)
+    for r in range(OWN):
+        column = jnp.where(line == r, radius[r], column)
+    radius_out[...] = column
+
+
+def load_rows(lines):
+    parts = [lines[pl.ds(part, SPHERES // 2, stride=4), :].astype(BF) for part in range(4)]
+    return jnp.concatenate(parts, axis=1)
+
+
+def half_sums(lines):
+    groups = []
+    for place in range(2):
         parts = []
         for part in range(4):
             value = lines[pl.ds(place * PER_GROUP * 4 + part, PER_GROUP, stride=4), :]
             parts.append(jnp.sum(value, axis=0, keepdims=True))
-        return jnp.concatenate(parts, axis=1)
-
+        groups.append(jnp.concatenate(parts, axis=1))
+    return jnp.concatenate(groups, axis=0)
+
+
+def all_groups(mine, other):
     core = lax.axis_index("co")
-    groups = []
-    for place in range(2):
-        mine, other = total(near, place), total(peer, place)
-        groups.append(jnp.where(core == 0, mine, other))
-        groups.append(jnp.where(core == 0, other, mine))
-    return jnp.concatenate(groups, axis=0)
-
-
-def mix(sums, shifted, tables):
+    first, second = jnp.where(core == 0, mine, other), jnp.where(core == 0, other, mine)
+    return jnp.concatenate([first[0:1], second[0:1], first[1:2], second[1:2]], axis=0)
+
+
+def order_body(near_in, pairs, near_out):
+    del near_in, pairs, near_out
+
+
+def mix(sums, shifted, tables, dot=dot):
     for k in range(1, TOP + 1):
         at_cos, at_sin = pl.ds(k * BLOCK, BLOCK), pl.ds((TOP + k) * BLOCK, BLOCK)
         cos_re, cos_im = sums[at_cos, :WIDE], sums[at_cos, WIDE:]
@@ -300,45 +293,50 @@
 
 
 def first_body(
-    near, peer, pairs, tables, tmat, radius,
-    chunk, rows_out, weights_out, totals_out, rows, sums, shifted, lines,
+    near, peer, pairs, inwards, tables, tmat, radius,
+    chunk, rows_out, totals_out, sums, shifted, lines,
 ):
-    load_rows(near, peer, rows)
-    totals_out[...] = group_sums(near, peer)
-    sums[...] = dot(pairs[...], rows[...])
+    totals_out[...] = all_groups(half_sums(near), half_sums(peer))
+    rows = jnp.concatenate([load_rows(near), load_rows(peer)], axis=0)[:, :COEFF]
+    sums[...] = dot(pairs[...], dot(rows, inwards[...]).astype(BF))
+    field = mix(sums, shifted, tables)
+    image = scatter(field, tmat, radius[...])
+    rows_out[...] = image
+    lane = lax.broadcasted_iota(jnp.int32, (ROWS, FULL), 1)
+    marked = jnp.where(lane == PAD + own_group(), jnp.concatenate([radius[...]] * 4, axis=1), image)
+    write_chunks(marked, chunk, lines)
+
+
+def gradient_of(totals, probes, seen):
+    lane = lax.broadcasted_iota(jnp.int32, totals.shape, 1)
+    totals = jnp.where((lane & (WIDE - 1)) < HALF, totals, 0.0)
+    values = fine_dot(totals, probes[...], parts=2) * seen[...]
+    return fine_dot(values, probes[...], dot_t, 2)
+
+
+def first_gradient_body(totals, inwards, probes, seen, gradient_out, probes_out):
+    outwards = inwards[...].astype(F32).T.astype(BF)
+    probes_out[...] = dot(outwards, probes[...]).astype(BF)
+    gradient_out[...] = gradient_of(fine_dot(totals[:, :COEFF], inwards[...]), probes_out, seen)
+
+
+def second_gradient_body(near, peer, first, probes, seen, keep, send):
+    second = gradient_of(all_groups(half_sums(near), half_sums(peer)), probes, seen)
+    core = lax.axis_index("co")
+    keep[...] = jnp.where(core == 0, first[...], second)
+    send[...] = jnp.where(core == 0, second, first[...])
+
+
+def second_body(
+    near, peer, pairs, tables, tmat, radius, base, image,
+    scalars, weights_out, sums, shifted,
+):
+    sums[...] = dot(pairs[...], jnp.concatenate([load_rows(near), load_rows(peer)], axis=0))
     for block in range(BLOCKS):
         k = block if block <= TOP else block - TOP
         at = pl.ds(block * BLOCK, BLOCK)
         value = sums[at, LANES:WIDE]
         weights_out[at, :] = (value if k % 2 == 0 else -value).astype(BF)
-    field = mix(sums, shifted, tables)
-    image = scatter(field, tmat, radius[...])
-    rows_out[...] = image
-    write_chunks(image, chunk, lines)
-
-
-def gradient_body(near, peer, totals_first, probes, probe_group, keep, send):
-    totals = jnp.concatenate([totals_first[...], group_sums(near, peer)], axis=0)
-    lane = lax.broadcasted_iota(jnp.int32, (2 * GROUPS, FULL), 1)
-    totals = jnp.where((lane & (WIDE - 1)) < HALF, totals, 0.0)
-    total_high, total_low = split(totals)
-    values = dot(total_high, probes[...]) + dot(total_low, probes[...])
-    line = lax.broadcasted_iota(jnp.int32, (2 * GROUPS, PROBES_OWN), 0)
-    values = jnp.where((line & (GROUPS - 1)) == probe_group[...], values, 0.0)
-    value_high, value_low = split(values)
-    gradient = dot_t(value_high, probes[...]) + dot_t(value_low, probes[...])
-    core = lax.axis_index("co")
-    first, second = gradient[:GROUPS], gradient[GROUPS:]
-    keep[...] = jnp.where(core == 0, first, second)
-    send[...] = jnp.where(core == 0, second, first)
-
-
-def second_body(
-    near, peer, pairs, tables, tmat, radius, base, image,
-    scalars, rows, sums, shifted,
-):
-    load_rows(near, peer, rows)
-    sums[...] = dot(pairs[...], rows[...])
     field = mix(sums, shifted, tables)
     last = scatter(field, tmat, radius[...])
     zero, one = base[...], image[...]
@@ -352,7 +350,7 @@
 
 
 def finish_body(
-    near, peer, weights, tables_t, tmat, inwards, incident, image,
+    near, peer, weights, tables, tmat, inwards, incident, image,
     solution_out, sensitivity_out, arnoldi_out, places, sums, shifted,
 ):
     mine, other = jnp.sum(near[...], axis=0), jnp.sum(peer[...], axis=0)
@@ -391,7 +389,7 @@
     places[at, :WIDE] = real * grad_re + imag * grad_im
     places[at, WIDE:] = real * grad_im - imag * grad_re
     sums[...] = dot(weights[...], places[...].astype(BF))
-    field = mix(sums, shifted, tables_t)
+    field = mix(sums, shifted, tables, dot_t)
     group = own_group()
     own = jnp.zeros((1, FULL), F32)
     for g in range(GROUPS):
@@ -399,24 +397,23 @@
     lane = lax.broadcasted_iota(jnp.int32, (1, FULL), 1)
     own = jnp.where((lane & (WIDE - 1)) < HALF, own, 0.0)
     both = jnp.concatenate([image[...], own - field], axis=0)
-    result = exact_dot(both, inwards[...], dot_t)
+    result = fine_dot(both, inwards[...], dot_t)
     image_rows = result[:OWN]
     solution_out[...] = for_base * incident[...] + (for_image / SCALE) * image_rows
     sensitivity_out[...] = result[ROWS : ROWS + OWN]
 
 
-def call(body, outs, scratch=(), operands=(), spaces=None, smem_outs=(), cost=None):
-    spaces = spaces or {}
+def call(body, outs, scratch=(), operands=(), spaces=None, out_spaces=None, cost=None, aliases=None):
+    spaces, out_spaces = spaces or {}, out_spaces or {}
     return pl.pallas_call(
         body,
         out_shape=[jax.ShapeDtypeStruct(shape, kind) for shape, kind in outs],
         in_specs=[pl.BlockSpec(memory_space=spaces.get(i, pltpu.VMEM)) for i in range(len(operands))],
-        out_specs=[
-            pl.BlockSpec(memory_space=pltpu.SMEM if i in smem_outs else pltpu.VMEM) for i in range(len(outs))
-        ],
+        out_specs=[pl.BlockSpec(memory_space=out_spaces.get(i, pltpu.VMEM)) for i in range(len(outs))],
         scratch_shapes=list(scratch),
         compiler_params=pltpu.CompilerParams(vmem_limit_bytes=16 * 1024 * 1024),
         cost_estimate=cost,
+        input_output_aliases=aliases or {},
     )(*operands)
 
 
@@ -424,10 +421,8 @@
     return lax.ppermute(array, "co", [(0, 1), (1, 0)])
 
 
-def exchange(chunk):
-    near = lax.all_to_all(chunk, FAR_AXES, 0, 0)
-    peer = swap_cores(near)
-    return near.reshape(FAR * CHUNK, LANES), peer.reshape(FAR * CHUNK, LANES)
+def as_lines(chunk):
+    return chunk.reshape(FAR * CHUNK, LANES)
 
 
 def on_device(
@@ -441,78 +436,76 @@
     probe_field,
     probe_group,
 ):
-    source = jnp.asarray(_SOURCE)
     line_scratch = pltpu.VMEM((4 * ROWS, LANES), F32)
-    chunk, base, radius = call(
-        send_body,
-        [((FAR, CHUNK, LANES), F32), ((ROWS, FULL), F32), ((ROWS, LANES), F32)],
-        [
-            line_scratch,
-            pltpu.VMEM((ROWS, COEFF), F32),
-            pltpu.VMEM((1, FULL), jnp.int32),
-            pltpu.SMEM((OWN,), F32),
-            pltpu.SemaphoreType.DMA((3,)),
-        ],
-        (incident, source, radius_factor),
-        {0: pl.ANY, 1: pl.ANY, 2: pl.ANY},
-    )
-    near, peer = exchange(chunk)
+    sum_scratch = pltpu.VMEM((BLOCKS * BLOCK, FULL), F32)
+    shift_scratch = pltpu.VMEM((2, (ORDER + 1) * BLOCK, FULL), BF)
+    rows_shape = ((ROWS, FULL), F32)
+    chunk_shape = ((FAR, CHUNK, LANES), F32)
+    gradient_shape = ((GROUPS, FULL), F32)
+    half_cost = pl.CostEstimate(flops=8_000_000_000, bytes_accessed=4_000_000, transcendentals=0)
+
+    (chunk,) = call(send_body, [chunk_shape], [line_scratch], (incident,))
 
     def by_core(array):
         lead = array.shape[:-1]
         return jnp.swapaxes(array.reshape(lead + (2, 2, PER_GROUP)), -3, -2).reshape(lead + (SPHERES,))
 
-    pairs, tables, tables_t, probes, tmat, inwards = call(
+    pairs, tables, seen, tmat, inwards, base, radius = call(
         prepare_body,
         [
             ((BLOCKS * BLOCK, SPHERES), BF),
             ((2, FULL, FULL), BF),
-            ((2, FULL, FULL), BF),
-            ((FULL, PROBES_OWN), BF),
+            ((GROUPS, PROBES_OWN), F32),
             ((ROWS, WIDE), F32),
             ((COEFF, FULL), BF),
+            rows_shape,
+            ((ROWS, LANES), F32),
         ],
         operands=(
             by_core(sphere_site[None, :]),
             by_core(jitter),
             rotation_table,
             axial_tables,
-            probe_field.T,
+            probe_group.reshape(1, PROBES_OWN),
             tmatrix,
-            source,
+            jnp.asarray(_SOURCE),
+            incident,
+            radius_factor,
         ),
-        cost=pl.CostEstimate(flops=6_000_000_000, bytes_accessed=8_000_000, transcendentals=20_000),
-    )
-
-    row_scratch = pltpu.VMEM((SPHERES, FULL), BF)
-    sum_scratch = pltpu.VMEM((BLOCKS * BLOCK, FULL), F32)
-    shift_scratch = pltpu.VMEM((2, (ORDER + 1) * BLOCK, FULL), BF)
-
-    chunk, image, weights, totals_first = call(
+        spaces={8: pltpu.SMEM},
+        cost=pl.CostEstimate(flops=8_000_000_000, bytes_accessed=8_000_000, transcendentals=20_000),
+    )
+
+    near = lax.all_to_all(chunk, FAR_AXES, 0, 0)
+    (near,) = call(order_body, [chunk_shape], operands=(near, pairs), spaces={1: pl.ANY}, aliases={0: 0})
+    chunk, image, totals = call(
         first_body,
-        [
-            ((FAR, CHUNK, LANES), F32),
-            ((ROWS, FULL), F32),
-            ((BLOCKS * BLOCK, LANES), BF),
-            ((GROUPS, FULL), F32),
-        ],
-        [row_scratch, sum_scratch, shift_scratch, line_scratch],
-        (near, peer, pairs, tables, tmat, radius),
-    )
-    near, peer = exchange(chunk)
-
+        [chunk_shape, rows_shape, gradient_shape],
+        [sum_scratch, shift_scratch, line_scratch],
+        (as_lines(near), as_lines(swap_cores(near)), pairs, inwards, tables, tmat, radius),
+    )
+
+    gradient, probes = call(
+        first_gradient_body,
+        [gradient_shape, ((FULL, PROBES_OWN), BF)],
+        operands=(totals, inwards, probe_field.T, seen),
+        cost=half_cost,
+    )
+
+    near = lax.all_to_all(chunk, FAR_AXES, 0, 0)
+    near, peer = as_lines(near), as_lines(swap_cores(near))
     keep, send = call(
-        gradient_body,
-        [((GROUPS, FULL), F32), ((GROUPS, FULL), F32)],
-        operands=(near, peer, totals_first, probes, probe_group.reshape(1, PROBES_OWN)),
+        second_gradient_body,
+        [gradient_shape, gradient_shape],
+        operands=(near, peer, gradient, probes, seen),
     )
     received = swap_cores(send)
-    (scalars,) = call(
+    scalars, weights = call(
         second_body,
-        [((GROUPS, FULL), F32)],
-        [row_scratch, sum_scratch, shift_scratch],
+        [gradient_shape, ((BLOCKS * BLOCK, LANES), BF)],
+        [sum_scratch, shift_scratch],
         (near, peer, pairs, tables, tmat, radius, base, image),
-        cost=pl.CostEstimate(flops=1_000_000_000, bytes_accessed=8_000_000, transcendentals=0),
+        cost=half_cost,
     )
     lane = lax.broadcasted_iota(jnp.int32, (GROUPS, FULL), 1)
     share = jnp.where((lane & (WIDE - 1)) < HALF, keep + received, scalars)
@@ -523,8 +516,8 @@
         finish_body,
         [((OWN, COEFF), F32), ((OWN, COEFF), F32), ((4,), F32)],
         [pltpu.VMEM((LANES, FULL), F32), sum_scratch, shift_scratch],
-        (near, peer, weights, tables_t, tmat, inwards, incident, image),
-        smem_outs=(2,),
+        (near, peer, weights, tables, tmat, inwards, incident, image),
+        out_spaces={2: pltpu.SMEM},
     )
     return solution_rows, sensitivity_rows, arnoldi
 

time: 89.4 us -> 83.3 us (0.932)
  blocking collectives: 61.5 us -> 35.3 us
  starting transfers between devices: 7.32 us -> 20.4 us
  waiting for transfers between devices: 3.45 us -> 11.3 us
    all_to_all x2 -> x1, blocking collectives: 44.6 us -> 18.7 us  [on_device(): near = lax.all_to_all(chunk, FAR_AXES, 0, 0)]
    all_to_all x0 -> x1, starting transfers between devices: none -> 12.1 us  [on_device(): near = lax.all_to_all(chunk, FAR_AXES, 0, 0)]
    all_to_all x0 -> x1, waiting for transfers between devices: none -> 6.61 us  [on_device(): near = lax.all_to_all(chunk, FAR_AXES, 0, 0)]
    ppermute x4, waiting for transfers between devices: 3.45 us -> 4.67 us  [swap_cores(): return lax.ppermute(array, 'co', [(0, 1), (1, 0)])]
    ppermute x4, starting transfers between devices: 7.32 us -> 8.26 us  [swap_cores(): return lax.ppermute(array, 'co', [(0, 1), (1, 0)])]
    unnamed x24 -> x22, local copies, waits for them, and re-layouts: 4.89 us -> 4.23 us
    pallas_call x6 -> x8, Pallas kernels: 10.7 us -> 10.5 us  [call(): pl.pallas_call(body, out_shape=[jax.ShapeDtypeStruct(shape, kind) for sha...]
  transfers between devices with their start and end apart: 4 -> 5, of which waited for: 2 -> 4; matrix products, arithmetic and copies ran while one was open for 0% -> 0% of each run, Pallas kernels for 6% -> 6%
where the time goes in v3:
time: 83.3 us; the launch traced here: 82.8 us
  blocking collectives  35.3 us (42%)
  starting transfers between devices  20.4 us (24%)
  waiting for transfers between devices  11.3 us (14%)
  Pallas kernels  10.5 us (13%)
  local copies, waits for them, and re-layouts  4.66 us (6%)
    all_to_all x1, blocking collectives, on_device(): near = lax.all_to_all(chunk, FAR_AXES, 0, 0)  18.7 us
    all_to_all x1, blocking collectives, on_device(): near = lax.all_to_all(spread, FAR_AXES, 0, 0)  16.6 us
    all_to_all x1, starting transfers between devices, on_device(): near = lax.all_to_all(chunk, FAR_AXES, 0, 0)  12.1 us
    pallas_call x8, Pallas kernels, call(): pl.pallas_call(body, out_shape=[jax.ShapeDtypeStruct(shape, kind) for sha...  10.5 us
    ppermute x4, starting transfers between devices, swap_cores(): return lax.ppermute(array, 'co', [(0, 1), (1, 0)])  8.26 us
    all_to_all x1, waiting for transfers between devices, on_device(): near = lax.all_to_all(chunk, FAR_AXES, 0, 0)  6.61 us
    ppermute x4, waiting for transfers between devices, swap_cores(): return lax.ppermute(array, 'co', [(0, 1), (1, 0)])  4.67 us
    unnamed x22, local copies, waits for them, and re-layouts  4.23 us
  transfers between devices with their start and end apart: 5, of which 4 were waited for; matrix products, arithmetic and copies ran while one was open for 0% of the time, Pallas kernels for 6%

profile of v3, /device:TPU:1, one launch (start us, length us, event | category | flops | bytes accessed | tf_op | source)
XLA Modules:
  0.0 82.8 jit_solution(6004635086825126324)
XLA Ops:
  0.6 0.7 copy-done
  1.4 0.9 %shard_map.121 = f32[64,24,128]{2,1,0:T(8,128)} custom-call(f32[6,480]{1,0:T(8,128)S(1)} %copy-done), custom_call_target="tpu_custom_call" | custom-call | tf_op jit(solution)/shard_map/pallas_call | solution.py:408
  2.3 12.1 %all-to-all-start = ((f32[64,24,128]{2,1,0:T(8,128)}), f32[64,24,128]{2,1,0:T(8,128)S(1)}, u32[]{:S(2)}, u32[]{:S(2)}) async-start(f32[64,24,128]{2,1,0:T(8,128)} %shard_map.121), calls=%async_computation | async-start | bytes 1572864 | tf_op jit(solution)/shard_map/all_to_all | solution.py:479
  14.4 0.1 reshape.32
  14.6 0.6 copy-done.10
  15.4 0.5 copy-done.1
  16.1 1.2 %copy-done.2 = bf16[2,480,480]{2,1,0:T(8,128)(2,1)S(1)} copy-done((bf16[2,480,480]{2,1,0:T(8,128)(2,1)S(1)}, bf16[2,480,480]{2,1,0:T(8,128)(2,1)}, u32[]{:S(2)}) %copy-start.2) | copy-done | bytes 921624
  17.3 1.0 %copy-done.3 = bf16[480,480]{1,0:T(8,128)(2,1)S(1)} copy-done((bf16[480,480]{1,0:T(8,128)(2,1)S(1)}, bf16[480,480]{1,0:T(8,128)(2,1)}, u32[]{:S(2)}) %copy-start.3) | copy-done | bytes 460824
  18.3 3.0 %shard_map.122 = (bf16[656,768]{1,0:T(8,128)(2,1)S(1)}, bf16[2,512,512]{2,1,0:T(8,128)(2,1)S(1)}, f32[4,256]{1,0:T(4,128)S(1)}, f32[8,256]{1,0:T(8,128)S(1)}, bf...) custom-call(s32[1,768]{1,0:T(1,128)S(1)} %reshape.31.site, f32[3,768]{1,0:T(4,128)S(1)} %reshape.33.jitter, ...), custom_call_target="tpu_custom_call" | custom-call | flops 8000000000 | bytes 8000000 | tf_op jit(solution)/shard_map/pallas_call | solution.py:408
  21.3 6.6 %all-to-all-done.near_in = f32[64,24,128]{2,1,0:T(8,128)S(1)} async-done(((f32[64,24,128]{2,1,0:T(8,128)}), f32[64,24,128]{2,1,0:T(8,128)S(1)}, u32[]{:S(2)}, u32[]{:S(2)}) %all-to-all-start) | async-done | bytes 786464 | tf_op jit(solution)/shard_map/all_to_all | solution.py:479
  27.9 2.9 %collective-permute-start = (f32[64,24,128]{2,1,0:T(8,128)S(1)}, f32[64,24,128]{2,1,0:T(8,128)S(1)}, u32[]{:S(2)}, u32[]{:S(2)}) collective-permute-start(f32[64,24,128]{2,1,0:T(8,128)S(1)} %shard_map.123), channel_id=1, source_target_pairs={{0,32},{32,0},{1,33},{33,1},{2,34},{34,2},{3,35},{35,3},{4,36},{36... | collective-permute-start | bytes 2359304 | tf_op jit(solution)/shard_map/ppermute | solution.py:421
  30.8 1.9 %collective-permute-done = f32[64,24,128]{2,1,0:T(8,128)S(1)} collective-permute-done((f32[64,24,128]{2,1,0:T(8,128)S(1)}, f32[64,24,128]{2,1,0:T(8,128)S(1)}, u32[]{:S(2)}, u32[]{:S(2)}) %collective-permute-start) | collective-permute-done | bytes 786464 | tf_op jit(solution)/shard_map/ppermute | solution.py:421
  32.7 1.7 %shard_map.124 = (f32[64,24,128]{2,1,0:T(8,128)S(1)}, f32[8,512]{1,0:T(8,128)S(1)}, f32[4,512]{1,0:T(4,128)S(1)}) custom-call(f32[1536,128]{1,0:T(8,128)S(1)} %bitcast.10, f32[1536,128]{1,0:T(8,128)S(1)} %bitcast.15, bf16[656,768]{1,0:T(8,128)(2,1)S(1)} %get-tuple-element.19.pairs, bf16[480,512]{1,0:T(8,128)(2,1)S(1)} %get-tuple-element.20.inwards, ...), custom_call_target="tpu_custom_call" | custom-call | tf_op jit(solution)/shard_map/pallas_call | solution.py:408
  34.4 18.7 %all_to_all.15 = f32[64,24,128]{2,1,0:T(8,128)S(1)} all-to-all(f32[64,24,128]{2,1,0:T(8,128)S(1)} %get-tuple-element.24), channel_id=1, replica_groups=mesh['xl'=2,'co'=2,'z'=4,'xh'=2,'y'=4] {'xl','z','xh','y'}, dimensions={0} | all-to-all | bytes 1572864 | tf_op jit(solution)/shard_map/all_to_all | solution.py:495
  53.1 2.8 %collective-permute-start.1 = (f32[64,24,128]{2,1,0:T(8,128)S(1)}, f32[64,24,128]{2,1,0:T(8,128)S(1)}, u32[]{:S(2)}, u32[]{:S(2)}) collective-permute-start(f32[64,24,128]{2,1,0:T(8,128)S(1)} %all_to_all.15), channel_id=1, source_target_pairs={{0,32},{32,0},{1,33},{33,1},{2,34},{34,2},{3,35},{35,3},{4,36},{36... | collective-permute-start | bytes 2359304 | tf_op jit(solution)/shard_map/ppermute | solution.py:421
  55.9 0.7 shard_map.125
  56.5 1.2 %collective-permute-done.1 = f32[64,24,128]{2,1,0:T(8,128)S(1)} collective-permute-done((f32[64,24,128]{2,1,0:T(8,128)S(1)}, f32[64,24,128]{2,1,0:T(8,128)S(1)}, u32[]{:S(2)}, u32[]{:S(2)}) %collective-permute-start.1) | collective-permute-done | bytes 786464 | tf_op jit(solution)/shard_map/ppermute | solution.py:421
  57.8 0.4 shard_map.126
  58.1 0.4 collective-permute-start.2
  58.5 1.4 %shard_map.127 = (f32[4,512]{1,0:T(4,128)S(1)}, bf16[656,128]{1,0:T(8,128)(2,1)S(1)}) custom-call(f32[1536,128]{1,0:T(8,128)S(1)} %bitcast.12, f32[1536,128]{1,0:T(8,128)S(1)} %bitcast.14, bf16[656,768]{1,0:T(8,128)(2,1)S(1)} %get-tuple-element.19.pairs, bf16[2,512,512]{2,1,0:T(8,128)(2,1)S(1)} %get-tuple-element.21.tables, ...), custom_call_target="tpu_custom_call" | custom-call | flops 8000000000 | bytes 4000000 | tf_op jit(solution)/shard_map/pallas_call | solution.py:408
  60.0 16.6 %all_to_all.16.near = f32[64,4,512]{2,1,0:T(4,128)S(1)} all-to-all(f32[64,4,512]{2,1,0:T(4,128)S(1)} %broadcast_in_dim.2), channel_id=1, replica_groups=mesh['xl'=2,'co'=2,'z'=4,'xh'=2,'y'=4] {'xl','z','xh','y'}, dimensions={0} | all-to-all | bytes 1048576 | tf_op jit(solution)/shard_map/all_to_all | solution.py:513
  76.6 2.2 %collective-permute-start.3 = (f32[64,4,512]{2,1,0:T(4,128)S(1)}, f32[64,4,512]{2,1,0:T(4,128)S(1)}, u32[]{:S(2)}, u32[]{:S(2)}) collective-permute-start(f32[64,4,512]{2,1,0:T(4,128)S(1)} %all_to_all.16.near), channel_id=1, source_target_pairs={{0,32},{32,0},{1,33},{33,1},{2,34},{34,2},{3,35},{35,3},{4,36},{36... | collective-permute-start | bytes 1572872 | tf_op jit(solution)/shard_map/ppermute | solution.py:421
  78.8 1.5 %collective-permute-done.3.peer = f32[64,4,512]{2,1,0:T(4,128)S(1)} collective-permute-done((f32[64,4,512]{2,1,0:T(4,128)S(1)}, f32[64,4,512]{2,1,0:T(4,128)S(1)}, u32[]{:S(2)}, u32[]{:S(2)}) %collective-permute-start.3) | collective-permute-done | bytes 524320 | tf_op jit(solution)/shard_map/ppermute | solution.py:421
  80.3 2.5 %shard_map.128 = (f32[6,480]{1,0:T(8,128)}, f32[6,480]{1,0:T(8,128)}, f32[4]{0:T(128)}) custom-call(f32[64,4,512]{2,1,0:T(4,128)S(1)} %all_to_all.16.near, f32[64,4,512]{2,1,0:T(4,128)S(1)} %collective-permute-done.3.peer, bf16[656,128]{1,0:T(8,128)(2,1)S(1)} %get-tuple-element.34.weights, bf16[2,512,512]{2,1,0:T(8,128)(2,1)S(1)} %get-tuple-element.21.tables, ...), custom_call_target="tpu_custom_call" | custom-call | tf_op jit(solution)/shard_map/pallas_call | solution.py:408
  (27 shorter events, 0.5 us)
Async XLA Ops:
  0.6 0.7 copy-start
  2.3 12.1 %copy-start.9 = (f32[3,768]{1,0:T(4,128)S(1)}, f32[3,768]{1,0:T(4,128)}, u32[]{:S(2)}) copy-start(f32[3,768]{1,0:T(4,128)} %param.12) | copy-start | bytes 27652
  2.3 25.6 %all-to-all-start = ((f32[64,24,128]{2,1,0:T(8,128)}), f32[64,24,128]{2,1,0:T(8,128)S(1)}, u32[]{:S(2)}, u32[]{:S(2)}) async-start(f32[64,24,128]{2,1,0:T(8,128)} %shard_map.121), calls=%async_computation | async-start | bytes 1572864 | tf_op jit(solution)/shard_map/all_to_all | solution.py:479
  14.5 0.7 copy-start.10
  15.2 0.7 copy-start.1
  15.3 0.7 copy-start.5
  15.3 0.7 copy-start.8
  15.4 0.7 copy-start.6
  15.4 0.7 copy-start.7
  16.1 1.2 %copy-start.2 = (bf16[2,480,480]{2,1,0:T(8,128)(2,1)S(1)}, bf16[2,480,480]{2,1,0:T(8,128)(2,1)}, u32[]{:S(2)}) copy-start(bf16[2,480,480]{2,1,0:T(8,128)(2,1)} %axial.1) | copy-start | bytes 2764804
  17.3 1.0 %copy-start.3 = (bf16[480,480]{1,0:T(8,128)(2,1)S(1)}, bf16[480,480]{1,0:T(8,128)(2,1)}, u32[]{:S(2)}) copy-start(bf16[480,480]{1,0:T(8,128)(2,1)} %rotation.1) | copy-start | bytes 1382404
  27.9 4.8 %collective-permute-start = (f32[64,24,128]{2,1,0:T(8,128)S(1)}, f32[64,24,128]{2,1,0:T(8,128)S(1)}, u32[]{:S(2)}, u32[]{:S(2)}) collective-permute-start(f32[64,24,128]{2,1,0:T(8,128)S(1)} %shard_map.123), channel_id=1, source_target_pairs={{0,32},{32,0},{1,33},{33,1},{2,34},{34,2},{3,35},{35,3},{4,36},{36... | collective-permute-start | bytes 2359304 | tf_op jit(solution)/shard_map/ppermute | solution.py:421
  34.4 21.5 %copy-start.4 = (bf16[256,480]{0,1:T(8,128)(2,1)S(1)}, bf16[256,480]{0,1:T(8,128)(2,1)}, u32[]{:S(2)}) copy-start(bf16[256,480]{0,1:T(8,128)(2,1)} %param.17) | copy-start | bytes 737284
  53.1 4.7 %collective-permute-start.1 = (f32[64,24,128]{2,1,0:T(8,128)S(1)}, f32[64,24,128]{2,1,0:T(8,128)S(1)}, u32[]{:S(2)}, u32[]{:S(2)}) collective-permute-start(f32[64,24,128]{2,1,0:T(8,128)S(1)} %all_to_all.15), channel_id=1, source_target_pairs={{0,32},{32,0},{1,33},{33,1},{2,34},{34,2},{3,35},{35,3},{4,36},{36... | collective-permute-start | bytes 2359304 | tf_op jit(solution)/shard_map/ppermute | solution.py:421
  58.1 1.8 %collective-permute-start.2 = (f32[4,512]{1,0:T(4,128)S(1)}, f32[4,512]{1,0:T(4,128)S(1)}, u32[]{:S(2)}, u32[]{:S(2)}) collective-permute-start(f32[4,512]{1,0:T(4,128)S(1)} %get-tuple-element.30), channel_id=1, source_target_pairs={{0,32},{32,0},{1,33},{33,1},{2,34},{34,2},{3,35},{35,3},{4,36},{36... | collective-permute-start | bytes 24584 | tf_op jit(solution)/shard_map/ppermute | solution.py:421
  76.6 3.7 %collective-permute-start.3 = (f32[64,4,512]{2,1,0:T(4,128)S(1)}, f32[64,4,512]{2,1,0:T(4,128)S(1)}, u32[]{:S(2)}, u32[]{:S(2)}) collective-permute-start(f32[64,4,512]{2,1,0:T(4,128)S(1)} %all_to_all.16.near), channel_id=1, source_target_pairs={{0,32},{32,0},{1,33},{33,1},{2,34},{34,2},{3,35},{35,3},{4,36},{36... | collective-permute-start | bytes 1572872 | tf_op jit(solution)/shard_map/ppermute | solution.py:421

commit v4 on v3

--- a/solution.py
+++ b/solution.py
@@ -30,6 +30,10 @@
 FAR = 64
 SCALE = 2.0**-14
 PAD = HALF
+SHARE = 2 * FULL // LANES
+SCALAR_LINE = 2
+PIECE_LINES = (6, 7)
+SLICE_LINES = (3, 7)
 BF = jnp.bfloat16
 F32 = jnp.float32
 
@@ -114,12 +118,12 @@
         lines[pl.ds(part, ROWS, stride=4), :] = rows[:, part * LANES : (part + 1) * LANES]
     once = lines[:CHUNK, :]
     for far in range(FAR):
-        chunk[far] = once
+        chunk[far * CHUNK : (far + 1) * CHUNK, :] = once
 
 
 def prepare_body(
-    site, jitter, rotation, axial, probe_group, tmat, source, incident, radius,
-    pairs, tables, seen_out, tmat_out, inwards_out, base_out, radius_out,
+    site, jitter, rotation, axial, probes, probe_group, tmat, source, incident, radius,
+    pairs, tables, probes_out, seen_out, tmat_out, inwards_out, outwards_out, base_out, radius_out,
 ):
     own = (
         lax.axis_index("xl") * PER_GROUP
@@ -175,6 +179,8 @@
     inwards = onehot_in(source[...])
     inwards_out[...] = inwards
     outwards = inwards.astype(F32).T.astype(BF)
+    outwards_out[...] = outwards
+    probes_out[...] = dot(outwards, probes[...]).astype(BF)
     turned = dot(outwards, rotation[...]).astype(BF)
     for radial in range(2):
         tables[radial] = fine_dot(0.5 * dot(turned, axial[radial]), turned, dot_t, 2).astype(BF)
@@ -293,43 +299,79 @@
 
 
 def first_body(
-    near, peer, pairs, inwards, tables, tmat, radius,
-    chunk, rows_out, totals_out, sums, shifted, lines,
+    near, peer, pairs, inwards, tables, tmat, radius, plain_probes, probes, seen,
+    chunk, rows_out, sums, shifted, lines,
 ):
-    totals_out[...] = all_groups(half_sums(near), half_sums(peer))
     rows = jnp.concatenate([load_rows(near), load_rows(peer)], axis=0)[:, :COEFF]
     sums[...] = dot(pairs[...], dot(rows, inwards[...]).astype(BF))
+    totals = all_groups(half_sums(near), half_sums(peer))[:, :COEFF]
+    gradient = gradient_of(totals, plain_probes, probes, seen)
     field = mix(sums, shifted, tables)
     image = scatter(field, tmat, radius[...])
     rows_out[...] = image
     lane = lax.broadcasted_iota(jnp.int32, (ROWS, FULL), 1)
     marked = jnp.where(lane == PAD + own_group(), jnp.concatenate([radius[...]] * 4, axis=1), image)
     write_chunks(marked, chunk, lines)
-
-
-def gradient_of(totals, probes, seen):
+    for piece in range(2):
+        line = SLICE_LINES[piece]
+        chunk[pl.ds(line, FAR, stride=CHUNK), :] = lines[line : line + 1, :] + slices(gradient, piece)
+
+
+def piece_mask(piece):
+    lane = lax.broadcasted_iota(jnp.int32, (FAR, FULL), 1)
+    far = lax.broadcasted_iota(jnp.int32, (FAR, FULL), 0)
+    return (lane >> 4) == ((far & (FAR // GROUPS - 1)) * 2 + piece)
+
+
+def slices(gradient, piece):
+    rows = [jnp.broadcast_to(gradient[g : g + 1, :], (FAR // GROUPS, FULL)) for g in range(GROUPS)]
+    rows = jnp.where(piece_mask(piece), jnp.concatenate(rows, axis=0), 0.0)
+    lane = lax.broadcasted_iota(jnp.int32, (FULL, LANES), 1)
+    source = lax.broadcasted_iota(jnp.int32, (FULL, LANES), 0)
+    fold = jnp.where(lane - (LANES - 16) == (source & 15), 1.0, 0.0).astype(BF)
+    return fine_dot(rows, fold, parts=2)
+
+
+def unslice(parts):
+    lane = lax.broadcasted_iota(jnp.int32, (LANES, FULL), 1)
+    source = lax.broadcasted_iota(jnp.int32, (LANES, FULL), 0)
+    spread = jnp.where(source - (LANES - 16) == (lane & 15), 1.0, 0.0).astype(BF)
+    both = fine_dot(jnp.concatenate(parts, axis=0), spread, parts=2)
+    total = jnp.where(piece_mask(0), both[:FAR], jnp.where(piece_mask(1), both[FAR:], 0.0))
+    each = FAR // GROUPS
+    return jnp.concatenate(
+        [jnp.sum(total[g * each : (g + 1) * each], axis=0, keepdims=True) for g in range(GROUPS)], axis=0
+    )
+
+
+def gradient_of(totals, from_probes, to_probes, seen):
+    values = fine_dot(totals, from_probes[...], parts=2) * seen[...]
+    return fine_dot(values, to_probes[...], dot_t, 2)
+
+
+def to_lines(rows):
+    return jnp.concatenate([rows[:, part * LANES : (part + 1) * LANES] for part in range(4)], axis=0)
+
+
+def from_lines(lines):
+    each = lines.shape[0] // 4
+    return jnp.concatenate([lines[part * each : (part + 1) * each, :] for part in range(4)], axis=1)
+
+
+def second_gradient_body(near, peer, probes, seen, keep, send):
+    totals = all_groups(half_sums(near), half_sums(peer))
     lane = lax.broadcasted_iota(jnp.int32, totals.shape, 1)
     totals = jnp.where((lane & (WIDE - 1)) < HALF, totals, 0.0)
-    values = fine_dot(totals, probes[...], parts=2) * seen[...]
-    return fine_dot(values, probes[...], dot_t, 2)
-
-
-def first_gradient_body(totals, inwards, probes, seen, gradient_out, probes_out):
-    outwards = inwards[...].astype(F32).T.astype(BF)
-    probes_out[...] = dot(outwards, probes[...]).astype(BF)
-    gradient_out[...] = gradient_of(fine_dot(totals[:, :COEFF], inwards[...]), probes_out, seen)
-
-
-def second_gradient_body(near, peer, first, probes, seen, keep, send):
-    second = gradient_of(all_groups(half_sums(near), half_sums(peer)), probes, seen)
+    gradient = gradient_of(totals, probes, probes, seen)
     core = lax.axis_index("co")
-    keep[...] = jnp.where(core == 0, first[...], second)
-    send[...] = jnp.where(core == 0, second, first[...])
+    low, high = to_lines(gradient[:2]), to_lines(gradient[2:])
+    keep[...] = jnp.where(core == 0, low, high)
+    send[...] = jnp.where(core == 0, high, low)
 
 
 def second_body(
     near, peer, pairs, tables, tmat, radius, base, image,
-    scalars, weights_out, sums, shifted,
+    extra, weights_out, sums, shifted,
 ):
     sums[...] = dot(pairs[...], jnp.concatenate([load_rows(near), load_rows(peer)], axis=0))
     for block in range(BLOCKS):
@@ -340,25 +382,39 @@
     field = mix(sums, shifted, tables)
     last = scatter(field, tmat, radius[...])
     zero, one = base[...], image[...]
-    line = lax.broadcasted_iota(jnp.int32, (GROUPS, FULL), 0)
-    lane = lax.broadcasted_iota(jnp.int32, (GROUPS, FULL), 1)
-    out = jnp.zeros((GROUPS, FULL), F32)
+    line = lax.broadcasted_iota(jnp.int32, (SHARE, LANES), 0)
+    lane = lax.broadcasted_iota(jnp.int32, (SHARE, LANES), 1)
+    out = jnp.zeros((SHARE, LANES), F32)
     pairs_of = ((zero, zero), (zero, one), (one, one), (zero, last), (one, last), (last, last))
     for index, (a, b) in enumerate(pairs_of):
-        out = jnp.where((line == 0) & (lane == PAD + index), jnp.sum(a * b), out)
-    scalars[...] = out
+        out = jnp.where((line == SCALAR_LINE) & (lane == PAD - LANES + index), jnp.sum(a * b), out)
+    for piece in range(2):
+        value = jnp.sum(near[pl.ds(SLICE_LINES[piece], FAR, stride=CHUNK), :], axis=0, keepdims=True)
+        out = jnp.where((line == PIECE_LINES[piece]) & (lane >= LANES - 16), value, out)
+    extra[...] = out
+
+
+def sum_body(near, out):
+    total = near[pl.ds(0, SHARE), :]
+    for far in range(1, FAR):
+        total = total + near[pl.ds(far * SHARE, SHARE), :]
+    out[:SHARE, :] = total
+    pieces = [near[pl.ds(PIECE_LINES[piece], FAR, stride=SHARE), :] for piece in range(2)]
+    out[SHARE:, :] = to_lines(unslice(pieces))
 
 
 def finish_body(
-    near, peer, weights, tables, tmat, inwards, incident, image,
+    near, peer, weights, tables, tmat, outwards, incident, image,
     solution_out, sensitivity_out, arnoldi_out, places, sums, shifted,
 ):
-    mine, other = jnp.sum(near[...], axis=0), jnp.sum(peer[...], axis=0)
+    scal = near[SCALAR_LINE : SCALAR_LINE + 1, :] + peer[SCALAR_LINE : SCALAR_LINE + 1, :]
+    scal = scal / scal[:, PAD - LANES : PAD - LANES + 1]
+    g01, g11, g02, g12, g22 = [scal[:, PAD - LANES + i : PAD - LANES + i + 1] for i in range(1, 6)]
     core = lax.axis_index("co")
-    first, second = jnp.where(core == 0, mine, other), jnp.where(core == 0, other, mine)
-    scal = (first + second)[0:1, :]
-    g00, s01, s11, s02, s12, s22 = [scal[:, PAD + i : PAD + i + 1] for i in range(6)]
-    g01, g11, g02, g12, g22 = s01 / g00, s11 / g00, s02 / g00, s12 / g00, s22 / g00
+    first = from_lines(near[SHARE:, :] + peer[SHARE:, :])
+    mine, other = from_lines(near[:SHARE, :]), from_lines(peer[:SHARE, :])
+    low, high = jnp.where(core == 0, mine, other), jnp.where(core == 0, other, mine)
+    second = jnp.concatenate([low, high], axis=0)
     diag_first = 1.0 + g01
     below_sq = g11 - g01 * g01
     below_first = jnp.sqrt(below_sq)
@@ -397,7 +453,7 @@
     lane = lax.broadcasted_iota(jnp.int32, (1, FULL), 1)
     own = jnp.where((lane & (WIDE - 1)) < HALF, own, 0.0)
     both = jnp.concatenate([image[...], own - field], axis=0)
-    result = fine_dot(both, inwards[...], dot_t)
+    result = fine_dot(both, outwards[...])
     image_rows = result[:OWN]
     solution_out[...] = for_base * incident[...] + (for_image / SCALE) * image_rows
     sensitivity_out[...] = result[ROWS : ROWS + OWN]
@@ -421,8 +477,9 @@
     return lax.ppermute(array, "co", [(0, 1), (1, 0)])
 
 
-def as_lines(chunk):
-    return chunk.reshape(FAR * CHUNK, LANES)
+def spread_far(lines):
+    parts = lines.reshape(FAR, lines.shape[0] // FAR, LANES)
+    return lax.all_to_all(parts, FAR_AXES, 0, 0).reshape(lines.shape)
 
 
 def on_device(
@@ -440,8 +497,8 @@
     sum_scratch = pltpu.VMEM((BLOCKS * BLOCK, FULL), F32)
     shift_scratch = pltpu.VMEM((2, (ORDER + 1) * BLOCK, FULL), BF)
     rows_shape = ((ROWS, FULL), F32)
-    chunk_shape = ((FAR, CHUNK, LANES), F32)
-    gradient_shape = ((GROUPS, FULL), F32)
+    chunk_shape = ((FAR * CHUNK, LANES), F32)
+    share_shape = ((SHARE, LANES), F32)
     half_cost = pl.CostEstimate(flops=8_000_000_000, bytes_accessed=4_000_000, transcendentals=0)
 
     (chunk,) = call(send_body, [chunk_shape], [line_scratch], (incident,))
@@ -450,14 +507,17 @@
         lead = array.shape[:-1]
         return jnp.swapaxes(array.reshape(lead + (2, 2, PER_GROUP)), -3, -2).reshape(lead + (SPHERES,))
 
-    pairs, tables, seen, tmat, inwards, base, radius = call(
+    plain_probes = probe_field.T
+    pairs, tables, probes, seen, tmat, inwards, outwards, base, radius = call(
         prepare_body,
         [
             ((BLOCKS * BLOCK, SPHERES), BF),
             ((2, FULL, FULL), BF),
+            ((FULL, PROBES_OWN), BF),
             ((GROUPS, PROBES_OWN), F32),
             ((ROWS, WIDE), F32),
             ((COEFF, FULL), BF),
+            ((FULL, COEFF), BF),
             rows_shape,
             ((ROWS, LANES), F32),
         ],
@@ -466,57 +526,46 @@
             by_core(jitter),
             rotation_table,
             axial_tables,
+            plain_probes,
             probe_group.reshape(1, PROBES_OWN),
             tmatrix,
             jnp.asarray(_SOURCE),
             incident,
             radius_factor,
         ),
-        spaces={8: pltpu.SMEM},
+        spaces={9: pltpu.SMEM},
         cost=pl.CostEstimate(flops=8_000_000_000, bytes_accessed=8_000_000, transcendentals=20_000),
     )
 
-    near = lax.all_to_all(chunk, FAR_AXES, 0, 0)
+    near = spread_far(chunk)
     (near,) = call(order_body, [chunk_shape], operands=(near, pairs), spaces={1: pl.ANY}, aliases={0: 0})
-    chunk, image, totals = call(
+    chunk, image = call(
         first_body,
-        [chunk_shape, rows_shape, gradient_shape],
+        [chunk_shape, rows_shape],
         [sum_scratch, shift_scratch, line_scratch],
-        (as_lines(near), as_lines(swap_cores(near)), pairs, inwards, tables, tmat, radius),
-    )
-
-    gradient, probes = call(
-        first_gradient_body,
-        [gradient_shape, ((FULL, PROBES_OWN), BF)],
-        operands=(totals, inwards, probe_field.T, seen),
-        cost=half_cost,
-    )
-
-    near = lax.all_to_all(chunk, FAR_AXES, 0, 0)
-    near, peer = as_lines(near), as_lines(swap_cores(near))
-    keep, send = call(
-        second_gradient_body,
-        [gradient_shape, gradient_shape],
-        operands=(near, peer, gradient, probes, seen),
-    )
+        (near, swap_cores(near), pairs, inwards, tables, tmat, radius, plain_probes, probes, seen),
+    )
+
+    near = spread_far(chunk)
+    peer = swap_cores(near)
+    keep, send = call(second_gradient_body, [share_shape, share_shape], operands=(near, peer, probes, seen))
     received = swap_cores(send)
-    scalars, weights = call(
+    extra, weights = call(
         second_body,
-        [gradient_shape, ((BLOCKS * BLOCK, LANES), BF)],
+        [share_shape, ((BLOCKS * BLOCK, LANES), BF)],
         [sum_scratch, shift_scratch],
         (near, peer, pairs, tables, tmat, radius, base, image),
         cost=half_cost,
     )
-    lane = lax.broadcasted_iota(jnp.int32, (GROUPS, FULL), 1)
-    share = jnp.where((lane & (WIDE - 1)) < HALF, keep + received, scalars)
-    spread = jnp.broadcast_to(share[None], (FAR, GROUPS, FULL))
-    near = lax.all_to_all(spread, FAR_AXES, 0, 0)
+    share = keep + received + extra
+    near = spread_far(jnp.broadcast_to(share[None], (FAR, SHARE, LANES)).reshape(FAR * SHARE, LANES))
+    (near,) = call(sum_body, [((SHARE + GROUPS * 4, LANES), F32)], operands=(near,))
     peer = swap_cores(near)
     solution_rows, sensitivity_rows, arnoldi = call(
         finish_body,
         [((OWN, COEFF), F32), ((OWN, COEFF), F32), ((4,), F32)],
         [pltpu.VMEM((LANES, FULL), F32), sum_scratch, shift_scratch],
-        (near, peer, weights, tables, tmat, inwards, incident, image),
+        (near, peer, weights, tables, tmat, outwards, incident, image),
         out_spaces={2: pltpu.SMEM},
     )
     return solution_rows, sensitivity_rows, arnoldi

time: 83.3 us -> 80.5 us (0.966)
  blocking collectives: 35.3 us -> 33.2 us
  waiting for transfers between devices: 11.3 us -> 9.54 us
  local copies, waits for them, and re-layouts: 4.66 us -> 6.15 us
    all_to_all x2, blocking collectives: 35.3 us -> 33.2 us  [spread_far(): return lax.all_to_all(parts, FAR_AXES, 0, 0).reshape(lines.shape)]
    all_to_all x1, waiting for transfers between devices: 6.61 us -> 4.88 us  [spread_far(): return lax.all_to_all(parts, FAR_AXES, 0, 0).reshape(lines.shape)]
    unnamed x22 -> x30, local copies, waits for them, and re-layouts: 4.23 us -> 5.78 us
where the time goes in v4:
time: 80.5 us; the launch traced here: 79.9 us
  blocking collectives  33.2 us (41%)
  starting transfers between devices  20.1 us (25%)
  Pallas kernels  10.2 us (13%)
  waiting for transfers between devices  9.54 us (12%)
  local copies, waits for them, and re-layouts  6.15 us (8%)
    all_to_all x2, blocking collectives, spread_far(): return lax.all_to_all(parts, FAR_AXES, 0, 0).reshape(lines.shape)  33.2 us
    all_to_all x1, starting transfers between devices, spread_far(): return lax.all_to_all(parts, FAR_AXES, 0, 0).reshape(lines.shape)  12.1 us
    pallas_call x8, Pallas kernels, call(): pl.pallas_call(body, out_shape=[jax.ShapeDtypeStruct(shape, kind) for sha...  10.2 us
    ppermute x4, starting transfers between devices, swap_cores(): return lax.ppermute(array, 'co', [(0, 1), (1, 0)])  7.99 us
    unnamed x30, local copies, waits for them, and re-layouts  5.78 us
    all_to_all x1, waiting for transfers between devices, spread_far(): return lax.all_to_all(parts, FAR_AXES, 0, 0).reshape(lines.shape)  4.88 us
    ppermute x4, waiting for transfers between devices, swap_cores(): return lax.ppermute(array, 'co', [(0, 1), (1, 0)])  4.66 us
  transfers between devices with their start and end apart: 5, of which 4 were waited for; matrix products, arithmetic and copies ran while one was open for 0% of the time, Pallas kernels for 6%

profile of v4, /device:TPU:1, one launch (start us, length us, event | category | flops | bytes accessed | tf_op | source)
XLA Modules:
  0.0 79.9 jit_solution(8155291824440196837)
XLA Ops:
  0.6 0.7 copy-done.5
  1.4 0.9 %shard_map.121 = f32[1536,128]{1,0:T(8,128)} custom-call(f32[6,480]{1,0:T(8,128)S(1)} %copy-done.5), custom_call_target="tpu_custom_call" | custom-call | tf_op jit(solution)/shard_map/pallas_call | solution.py:464
  2.3 12.1 %all-to-all-start = ((f32[64,24,128]{2,1,0:T(8,128)}), f32[64,24,128]{2,1,0:T(8,128)S(1)}, u32[]{:S(2)}, u32[]{:S(2)}) async-start(f32[64,24,128]{2,1,0:T(8,128)} %bitcast), calls=%async_computation | async-start | bytes 1572864 | tf_op jit(solution)/shard_map/all_to_all | solution.py:482
  14.6 0.5 copy-done.13
  15.3 0.6 copy-done.6
  16.0 1.2 %copy-done.7 = bf16[2,480,480]{2,1,0:T(8,128)(2,1)S(1)} copy-done((bf16[2,480,480]{2,1,0:T(8,128)(2,1)S(1)}, bf16[2,480,480]{2,1,0:T(8,128)(2,1)}, u32[]{:S(2)}) %copy-start.7) | copy-done | bytes 921624
  17.2 1.0 %copy-done.8 = bf16[480,480]{1,0:T(8,128)(2,1)S(1)} copy-done((bf16[480,480]{1,0:T(8,128)(2,1)S(1)}, bf16[480,480]{1,0:T(8,128)(2,1)}, u32[]{:S(2)}) %copy-start.8) | copy-done | bytes 460824
  18.3 3.1 %shard_map.122 = (bf16[656,768]{1,0:T(8,128)(2,1)S(1)}, bf16[2,512,512]{2,1,0:T(8,128)(2,1)S(1)}, bf16[512,256]{1,0:T(8,128)(2,1)S(1)}, f32[4,256]{1,0:T(4,128)S...) custom-call(s32[1,768]{1,0:T(1,128)S(1)} %reshape.36.site, ...), custom_call_target="tpu_custom_call" | custom-call | flops 8000000000 | bytes 8000000 | tf_op jit(solution)/shard_map/pallas_call | solution.py:464
  21.4 0.8 copy-done
  22.2 0.8 copy-done.2
  23.0 4.9 %all-to-all-done = f32[64,24,128]{2,1,0:T(8,128)S(1)} async-done(((f32[64,24,128]{2,1,0:T(8,128)}), f32[64,24,128]{2,1,0:T(8,128)S(1)}, u32[]{:S(2)}, u32[]{:S(2)}) %all-to-all-start) | async-done | bytes 786464 | tf_op jit(solution)/shard_map/all_to_all | solution.py:482
  27.9 2.9 %collective-permute-start = (f32[1536,128]{1,0:T(8,128)S(1)}, f32[1536,128]{1,0:T(8,128)S(1)}, u32[]{:S(2)}, u32[]{:S(2)}) collective-permute-start(f32[1536,128]{1,0:T(8,128)S(1)} %shard_map.123.near), channel_id=1, source_target_pairs={{0,32},{32,0},{1,33},{33,1},{2,34},{34,2},{3,35},{35,3},{4,36},{36... | collective-permute-start | bytes 2359304 | tf_op jit(solution)/shard_map/ppermute | solution.py:477
  30.8 1.9 %collective-permute-done.peer = f32[1536,128]{1,0:T(8,128)S(1)} collective-permute-done((f32[1536,128]{1,0:T(8,128)S(1)}, f32[1536,128]{1,0:T(8,128)S(1)}, u32[]{:S(2)}, u32[]{:S(2)}) %collective-permute-start) | collective-permute-done | bytes 786464 | tf_op jit(solution)/shard_map/ppermute | solution.py:477
  32.7 1.9 %shard_map.124 = (f32[1536,128]{1,0:T(8,128)S(1)}, f32[8,512]{1,0:T(8,128)S(1)}) custom-call(f32[1536,128]{1,0:T(8,128)S(1)} %shard_map.123.near, f32[1536,128]{1,0:T(8,128)S(1)} %collective-permute-done.peer, bf16[656,768]{1,0:T(8,128)(2,1)S(1)} %get-tuple-element.18.pairs, bf16[480,512]{1,0:T(8,128)(2,1)S(1)} %copy-done.3, ...), custom_call_target="tpu_custom_call" | custom-call | tf_op jit(solution)/shard_map/pallas_call | solution.py:464
  34.6 18.6 %all_to_all.15 = f32[64,24,128]{2,1,0:T(8,128)S(1)} all-to-all(f32[64,24,128]{2,1,0:T(8,128)S(1)} %bitcast.16), channel_id=1, replica_groups=mesh['xl'=2,'co'=2,'z'=4,'xh'=2,'y'=4] {'xl','z','xh','y'}, dimensions={0} | all-to-all | bytes 1572864 | tf_op jit(solution)/shard_map/all_to_all | solution.py:482
  53.1 2.8 %collective-permute-start.1 = (f32[1536,128]{1,0:T(8,128)S(1)}, f32[1536,128]{1,0:T(8,128)S(1)}, u32[]{:S(2)}, u32[]{:S(2)}) collective-permute-start(f32[1536,128]{1,0:T(8,128)S(1)} %bitcast.12), channel_id=1, source_target_pairs={{0,32},{32,0},{1,33},{33,1},{2,34},{34,2},{3,35},{35,3},{4,36},{36... | collective-permute-start | bytes 2359304 | tf_op jit(solution)/shard_map/ppermute | solution.py:477
  55.9 1.9 %collective-permute-done.1.peer = f32[1536,128]{1,0:T(8,128)S(1)} collective-permute-done((f32[1536,128]{1,0:T(8,128)S(1)}, f32[1536,128]{1,0:T(8,128)S(1)}, u32[]{:S(2)}, u32[]{:S(2)}) %collective-permute-start.1) | collective-permute-done | bytes 786464 | tf_op jit(solution)/shard_map/ppermute | solution.py:477
  57.8 0.4 shard_map.125
  58.2 0.4 collective-permute-start.2
  58.6 1.4 %shard_map.126 = (f32[8,128]{1,0:T(8,128)S(1)}, bf16[656,128]{1,0:T(8,128)(2,1)S(1)}) custom-call(f32[1536,128]{1,0:T(8,128)S(1)} %bitcast.14, f32[1536,128]{1,0:T(8,128)S(1)} %collective-permute-done.1.peer, bf16[656,768]{1,0:T(8,128)(2,1)S(1)} %get-tuple-element.18.pairs, bf16[2,512,512]{2,1,0:T(8,128)(2,1)S(1)} %get-tuple-element.20.tables, ...), custom_call_target="tpu_custom_call" | custom-call | flops 8000000000 | bytes 4000000 | tf_op jit(solution)/shard_map/pallas_call | solution.py:464
  60.0 14.6 %all_to_all.16 = f32[64,8,128]{2,1,0:T(8,128)S(1)} all-to-all(f32[64,8,128]{2,1,0:T(8,128)S(1)} %broadcast_in_dim.2), channel_id=1, replica_groups=mesh['xl'=2,'co'=2,'z'=4,'xh'=2,'y'=4] {'xl','z','xh','y'}, dimensions={0} | all-to-all | bytes 524288 | tf_op jit(solution)/shard_map/all_to_all | solution.py:482
  74.8 1.9 %collective-permute-start.3 = (f32[24,128]{1,0:T(8,128)S(1)}, f32[24,128]{1,0:T(8,128)S(1)}, u32[]{:S(2)}, u32[]{:S(2)}) collective-permute-start(f32[24,128]{1,0:T(8,128)S(1)} %shard_map.127.near), channel_id=1, source_target_pairs={{0,32},{32,0},{1,33},{33,1},{2,34},{34,2},{3,35},{35,3},{4,36},{36... | collective-permute-start | bytes 36872 | tf_op jit(solution)/shard_map/ppermute | solution.py:477
  76.8 0.8 %collective-permute-done.3.peer = f32[24,128]{1,0:T(8,128)S(1)} collective-permute-done((f32[24,128]{1,0:T(8,128)S(1)}, f32[24,128]{1,0:T(8,128)S(1)}, u32[]{:S(2)}, u32[]{:S(2)}) %collective-permute-start.3) | collective-permute-done | bytes 12320 | tf_op jit(solution)/shard_map/ppermute | solution.py:477
  77.6 2.3 %shard_map.128 = (f32[6,480]{1,0:T(8,128)}, f32[6,480]{1,0:T(8,128)}, f32[4]{0:T(128)}) custom-call(f32[24,128]{1,0:T(8,128)S(1)} %shard_map.127.near, f32[24,128]{1,0:T(8,128)S(1)} %collective-permute-done.3.peer, bf16[656,128]{1,0:T(8,128)(2,1)S(1)} %get-tuple-element.31.weights, bf16[2,512,512]{2,1,0:T(8,128)(2,1)S(1)} %get-tuple-element.20.tables, ...), custom_call_target="tpu_custom_call" | custom-call | tf_op jit(solution)/shard_map/pallas_call | solution.py:464
  (34 shorter events, 0.8 us)
Async XLA Ops:
  0.6 0.7 copy-start.5
  2.3 12.1 %copy-start.14 = (s32[768]{0:T(1024)S(1)}, s32[768]{0:T(1024)}, u32[]{:S(2)}) copy-start(s32[768]{0:T(1024)} %param.11) | copy-start | bytes 9220
  2.3 13.0 %copy-start.4 = (bf16[256,480]{0,1:T(8,128)(2,1)S(1)}, bf16[256,480]{0,1:T(8,128)(2,1)}, u32[]{:S(2)}) copy-start(bf16[256,480]{0,1:T(8,128)(2,1)} %param.17) | copy-start | bytes 737284
  2.3 25.6 %all-to-all-start = ((f32[64,24,128]{2,1,0:T(8,128)}), f32[64,24,128]{2,1,0:T(8,128)S(1)}, u32[]{:S(2)}, u32[]{:S(2)}) async-start(f32[64,24,128]{2,1,0:T(8,128)} %bitcast), calls=%async_computation | async-start | bytes 1572864 | tf_op jit(solution)/shard_map/all_to_all | solution.py:482
  14.4 0.7 copy-start.13
  15.2 0.7 copy-start.6
  15.2 0.7 copy-start.12
  15.3 0.7 copy-start.9
  15.3 0.7 copy-start.10
  15.3 0.7 copy-start.11
  16.0 1.2 %copy-start.7 = (bf16[2,480,480]{2,1,0:T(8,128)(2,1)S(1)}, bf16[2,480,480]{2,1,0:T(8,128)(2,1)}, u32[]{:S(2)}) copy-start(bf16[2,480,480]{2,1,0:T(8,128)(2,1)} %axial.1) | copy-start | bytes 2764804
  17.2 1.0 %copy-start.8 = (bf16[480,480]{1,0:T(8,128)(2,1)S(1)}, bf16[480,480]{1,0:T(8,128)(2,1)}, u32[]{:S(2)}) copy-start(bf16[480,480]{1,0:T(8,128)(2,1)} %rotation.1) | copy-start | bytes 1382404
  21.4 0.8 %copy-start = (bf16[512,480]{1,0:T(8,128)(2,1)}, bf16[512,480]{1,0:T(8,128)(2,1)S(1)}, u32[]{:S(2)}) copy-start(bf16[512,480]{1,0:T(8,128)(2,1)S(1)} %get-tuple-element.32.outwards) | copy-start | bytes 1474564
  22.2 0.8 copy-start.2
  27.9 4.8 %copy-start.3 = (bf16[480,512]{1,0:T(8,128)(2,1)S(1)}, bf16[480,512]{1,0:T(8,128)(2,1)}, u32[]{:S(2)}) copy-start(bf16[480,512]{1,0:T(8,128)(2,1)} %copy-done.2) | copy-start | bytes 1474564
  27.9 4.8 %collective-permute-start = (f32[1536,128]{1,0:T(8,128)S(1)}, f32[1536,128]{1,0:T(8,128)S(1)}, u32[]{:S(2)}, u32[]{:S(2)}) collective-permute-start(f32[1536,128]{1,0:T(8,128)S(1)} %shard_map.123.near), channel_id=1, source_target_pairs={{0,32},{32,0},{1,33},{33,1},{2,34},{34,2},{3,35},{35,3},{4,36},{36... | collective-permute-start | bytes 2359304 | tf_op jit(solution)/shard_map/ppermute | solution.py:477
  53.1 4.7 %collective-permute-start.1 = (f32[1536,128]{1,0:T(8,128)S(1)}, f32[1536,128]{1,0:T(8,128)S(1)}, u32[]{:S(2)}, u32[]{:S(2)}) collective-permute-start(f32[1536,128]{1,0:T(8,128)S(1)} %bitcast.12), channel_id=1, source_target_pairs={{0,32},{32,0},{1,33},{33,1},{2,34},{34,2},{3,35},{35,3},{4,36},{36... | collective-permute-start | bytes 2359304 | tf_op jit(solution)/shard_map/ppermute | solution.py:477
  58.2 1.8 %collective-permute-start.2 = (f32[8,128]{1,0:T(8,128)S(1)}, f32[8,128]{1,0:T(8,128)S(1)}, u32[]{:S(2)}, u32[]{:S(2)}) collective-permute-start(f32[8,128]{1,0:T(8,128)S(1)} %get-tuple-element.27), channel_id=1, source_target_pairs={{0,32},{32,0},{1,33},{33,1},{2,34},{34,2},{3,35},{35,3},{4,36},{36... | collective-permute-start | bytes 12296 | tf_op jit(solution)/shard_map/ppermute | solution.py:477
  60.0 17.6 %copy-start.1 = (bf16[512,480]{1,0:T(8,128)(2,1)S(1)}, bf16[512,480]{1,0:T(8,128)(2,1)}, u32[]{:S(2)}) copy-start(bf16[512,480]{1,0:T(8,128)(2,1)} %copy-done) | copy-start | bytes 1474564
  74.8 2.8 %collective-permute-start.3 = (f32[24,128]{1,0:T(8,128)S(1)}, f32[24,128]{1,0:T(8,128)S(1)}, u32[]{:S(2)}, u32[]{:S(2)}) collective-permute-start(f32[24,128]{1,0:T(8,128)S(1)} %shard_map.127.near), channel_id=1, source_target_pairs={{0,32},{32,0},{1,33},{33,1},{2,34},{34,2},{3,35},{35,3},{4,36},{36... | collective-permute-start | bytes 36872 | tf_op jit(solution)/shard_map/ppermute | solution.py:477

commit v5 on v4

--- a/solution.py
+++ b/solution.py
@@ -32,6 +32,7 @@
 PAD = HALF
 SHARE = 2 * FULL // LANES
 SCALAR_LINE = 2
+SCALARS = SHARE + 4 * GROUPS
 PIECE_LINES = (6, 7)
 SLICE_LINES = (3, 7)
 BF = jnp.bfloat16
@@ -123,7 +124,7 @@
 
 def prepare_body(
     site, jitter, rotation, axial, probes, probe_group, tmat, source, incident, radius,
-    pairs, tables, probes_out, seen_out, tmat_out, inwards_out, outwards_out, base_out, radius_out,
+    pairs, tables, probes_out, seen_out, tmat_out, inwards_out, base_out, radius_out,
 ):
     own = (
         lax.axis_index("xl") * PER_GROUP
@@ -179,7 +180,6 @@
     inwards = onehot_in(source[...])
     inwards_out[...] = inwards
     outwards = inwards.astype(F32).T.astype(BF)
-    outwards_out[...] = outwards
     probes_out[...] = dot(outwards, probes[...]).astype(BF)
     turned = dot(outwards, rotation[...]).astype(BF)
     for radial in range(2):
@@ -221,6 +221,11 @@
 
 def order_body(near_in, pairs, near_out):
     del near_in, pairs, near_out
+
+
+def near_body(near, inwards, rows_out, totals_out):
+    rows_out[...] = dot(load_rows(near)[:, :COEFF], inwards[...]).astype(BF)
+    totals_out[...] = half_sums(near)
 
 
 def mix(sums, shifted, tables, dot=dot):
@@ -299,12 +304,12 @@
 
 
 def first_body(
-    near, peer, pairs, inwards, tables, tmat, radius, plain_probes, probes, seen,
+    near_rows, near_totals, peer, pairs, inwards, tables, tmat, radius, plain_probes, probes, seen,
     chunk, rows_out, sums, shifted, lines,
 ):
-    rows = jnp.concatenate([load_rows(near), load_rows(peer)], axis=0)[:, :COEFF]
-    sums[...] = dot(pairs[...], dot(rows, inwards[...]).astype(BF))
-    totals = all_groups(half_sums(near), half_sums(peer))[:, :COEFF]
+    rows = dot(load_rows(peer)[:, :COEFF], inwards[...]).astype(BF)
+    sums[...] = dot(pairs[...], jnp.concatenate([near_rows[...], rows], axis=0))
+    totals = all_groups(near_totals[...], half_sums(peer))[:, :COEFF]
     gradient = gradient_of(totals, plain_probes, probes, seen)
     field = mix(sums, shifted, tables)
     image = scatter(field, tmat, radius[...])
@@ -384,10 +389,16 @@
     zero, one = base[...], image[...]
     line = lax.broadcasted_iota(jnp.int32, (SHARE, LANES), 0)
     lane = lax.broadcasted_iota(jnp.int32, (SHARE, LANES), 1)
-    out = jnp.zeros((SHARE, LANES), F32)
     pairs_of = ((zero, zero), (zero, one), (one, one), (zero, last), (one, last), (last, last))
-    for index, (a, b) in enumerate(pairs_of):
-        out = jnp.where((line == SCALAR_LINE) & (lane == PAD - LANES + index), jnp.sum(a * b), out)
+    sums_of = []
+    for a, b in pairs_of:
+        product = a * b
+        parts = [product[:, part * LANES : (part + 1) * LANES] for part in range(4)]
+        sums_of.append(jnp.sum((parts[0] + parts[1]) + (parts[2] + parts[3]), axis=0, keepdims=True))
+    stacked = jnp.concatenate(sums_of + [jnp.zeros((SHARE - 6, LANES), F32)], axis=0)
+    column = jnp.sum(stacked, axis=1, keepdims=True)
+    row = jnp.sum(jnp.where(lane - (PAD - LANES) == line, column, 0.0), axis=0, keepdims=True)
+    out = jnp.where(line == SCALAR_LINE, row, 0.0)
     for piece in range(2):
         value = jnp.sum(near[pl.ds(SLICE_LINES[piece], FAR, stride=CHUNK), :], axis=0, keepdims=True)
         out = jnp.where((line == PIECE_LINES[piece]) & (lane >= LANES - 16), value, out)
@@ -400,42 +411,48 @@
         total = total + near[pl.ds(far * SHARE, SHARE), :]
     out[:SHARE, :] = total
     pieces = [near[pl.ds(PIECE_LINES[piece], FAR, stride=SHARE), :] for piece in range(2)]
-    out[SHARE:, :] = to_lines(unslice(pieces))
+    out[SHARE:SCALARS, :] = to_lines(unslice(pieces))
+    line = total[SCALAR_LINE : SCALAR_LINE + 1, :]
+    for index in range(6):
+        at = PAD - LANES + index
+        out[SCALARS + index : SCALARS + index + 1, :] = jnp.broadcast_to(line[:, at : at + 1], (1, LANES))
 
 
 def finish_body(
-    near, peer, weights, tables, tmat, outwards, incident, image,
+    near, peer, weights, tables, tmat, inwards, incident, image,
     solution_out, sensitivity_out, arnoldi_out, places, sums, shifted,
 ):
-    scal = near[SCALAR_LINE : SCALAR_LINE + 1, :] + peer[SCALAR_LINE : SCALAR_LINE + 1, :]
-    scal = scal / scal[:, PAD - LANES : PAD - LANES + 1]
-    g01, g11, g02, g12, g22 = [scal[:, PAD - LANES + i : PAD - LANES + i + 1] for i in range(1, 6)]
+    g00, g01, g11, g02, g12, g22 = [near[at : at + 1, :] + peer[at : at + 1, :] for at in range(SCALARS, SCALARS + 6)]
+    scale = 1.0 / g00
+    g01, g11, g02, g12, g22 = g01 * scale, g11 * scale, g02 * scale, g12 * scale, g22 * scale
     core = lax.axis_index("co")
-    first = from_lines(near[SHARE:, :] + peer[SHARE:, :])
+    first = from_lines(near[SHARE:SCALARS, :] + peer[SHARE:SCALARS, :])
     mine, other = from_lines(near[:SHARE, :]), from_lines(peer[:SHARE, :])
     low, high = jnp.where(core == 0, mine, other), jnp.where(core == 0, other, mine)
     second = jnp.concatenate([low, high], axis=0)
     diag_first = 1.0 + g01
     below_sq = g11 - g01 * g01
+    inverse = 1.0 / below_sq
+    upper = g02 - g01 * g01
+    shift = g12 - g01 * (g11 + g02 - g01 * g01)
+    norm_sq = g22 - g01 * (2.0 * g12 - g01 * g11)
+    cross = diag_first * upper + below_sq + shift
+    gram_first = diag_first * diag_first + below_sq
+    gram_second = (below_sq + 2.0 * shift + norm_sq) * inverse
+    cross_scaled = cross * inverse
+    determinant = gram_first * gram_second - cross * cross_scaled
+    for_image = (upper - diag_first * (1.0 + shift * inverse)) / determinant
+    for_base = (diag_first * gram_second - upper * cross_scaled) / determinant - for_image * g01
     below_first = jnp.sqrt(below_sq)
-    upper_second = (g02 - g01 * g01) / below_first
-    shift_second = (g12 - g01 * g11 - g01 * g02 + g01 * g01 * g01) / below_sq
+    shift_second = shift * inverse
     diag_second = 1.0 + shift_second
-    norm_sq = (g22 - 2.0 * g01 * g12 + g01 * g01 * g11) / below_sq
-    rest_second = norm_sq - upper_second * upper_second - shift_second * shift_second
-    gram_first = diag_first * diag_first + below_sq
-    gram_cross = diag_first * upper_second + below_first * diag_second
-    gram_second = upper_second * upper_second + diag_second * diag_second + rest_second
-    determinant = gram_first * gram_second - gram_cross * gram_cross
-    step_first = (diag_first * gram_second - upper_second * gram_cross) / determinant
-    step_second = (gram_first * upper_second - gram_cross * diag_first) / determinant
-    for_image = step_second / below_first
-    for_base = step_first - for_image * g01
+    rest_second = (norm_sq - upper * upper) * inverse - shift_second * shift_second
     arnoldi_out[0] = diag_first[0, 0]
     arnoldi_out[1] = below_first[0, 0]
     arnoldi_out[2] = diag_second[0, 0]
     arnoldi_out[3] = rest_second[0, 0]
 
+    for_base, for_image = [jnp.concatenate([part] * 4, axis=1) for part in (for_base, for_image)]
     factor = COEFF * GROUPS / PROBES / SCALE / float(np.sqrt(np.float32(PER_GROUP)))
     gradient = (for_base * first + for_image * second) * factor
     real, imag = tmat[0:1, :], tmat[1:2, :]
@@ -453,9 +470,9 @@
     lane = lax.broadcasted_iota(jnp.int32, (1, FULL), 1)
     own = jnp.where((lane & (WIDE - 1)) < HALF, own, 0.0)
     both = jnp.concatenate([image[...], own - field], axis=0)
-    result = fine_dot(both, outwards[...])
+    result = fine_dot(both, inwards[...], dot_t)
     image_rows = result[:OWN]
-    solution_out[...] = for_base * incident[...] + (for_image / SCALE) * image_rows
+    solution_out[...] = for_base[:, :COEFF] * incident[...] + (for_image[:, :COEFF] / SCALE) * image_rows
     sensitivity_out[...] = result[ROWS : ROWS + OWN]
 
 
@@ -508,7 +525,7 @@
         return jnp.swapaxes(array.reshape(lead + (2, 2, PER_GROUP)), -3, -2).reshape(lead + (SPHERES,))
 
     plain_probes = probe_field.T
-    pairs, tables, probes, seen, tmat, inwards, outwards, base, radius = call(
+    pairs, tables, probes, seen, tmat, inwards, base, radius = call(
         prepare_body,
         [
             ((BLOCKS * BLOCK, SPHERES), BF),
@@ -517,7 +534,6 @@
             ((GROUPS, PROBES_OWN), F32),
             ((ROWS, WIDE), F32),
             ((COEFF, FULL), BF),
-            ((FULL, COEFF), BF),
             rows_shape,
             ((ROWS, LANES), F32),
         ],
@@ -539,11 +555,17 @@
 
     near = spread_far(chunk)
     (near,) = call(order_body, [chunk_shape], operands=(near, pairs), spaces={1: pl.ANY}, aliases={0: 0})
+    near_rows, near_totals = call(
+        near_body,
+        [((SPHERES // 2, FULL), BF), ((2, FULL), F32)],
+        operands=(near, inwards),
+        cost=half_cost,
+    )
     chunk, image = call(
         first_body,
         [chunk_shape, rows_shape],
         [sum_scratch, shift_scratch, line_scratch],
-        (near, swap_cores(near), pairs, inwards, tables, tmat, radius, plain_probes, probes, seen),
+        (near_rows, near_totals, swap_cores(near), pairs, inwards, tables, tmat, radius, plain_probes, probes, seen),
     )
 
     near = spread_far(chunk)
@@ -559,13 +581,13 @@
     )
     share = keep + received + extra
     near = spread_far(jnp.broadcast_to(share[None], (FAR, SHARE, LANES)).reshape(FAR * SHARE, LANES))
-    (near,) = call(sum_body, [((SHARE + GROUPS * 4, LANES), F32)], operands=(near,))
+    (near,) = call(sum_body, [((SCALARS + 8, LANES), F32)], operands=(near,))
     peer = swap_cores(near)
     solution_rows, sensitivity_rows, arnoldi = call(
         finish_body,
         [((OWN, COEFF), F32), ((OWN, COEFF), F32), ((4,), F32)],
         [pltpu.VMEM((LANES, FULL), F32), sum_scratch, shift_scratch],
-        (near, peer, weights, tables, tmat, outwards, incident, image),
+        (near, peer, weights, tables, tmat, inwards, incident, image),
         out_spaces={2: pltpu.SMEM},
     )
     return solution_rows, sensitivity_rows, arnoldi

time: 80.5 us -> 79.6 us (0.989)
    pallas_call x8 -> x9, Pallas kernels: 10.2 us -> 9.8 us  [call(): pl.pallas_call(body, out_shape=[jax.ShapeDtypeStruct(shape, kind) for sha...]
    unnamed x30 -> x28, local copies, waits for them, and re-layouts: 5.78 us -> 5.84 us
where the time goes in v5:
time: 79.6 us; the launch traced here: 79 us
  blocking collectives  33 us (41%)
  starting transfers between devices  20.1 us (25%)
  Pallas kernels  9.8 us (12%)
  waiting for transfers between devices  9.14 us (11%)
  local copies, waits for them, and re-layouts  6.21 us (8%)
    all_to_all x2, blocking collectives, spread_far(): return lax.all_to_all(parts, FAR_AXES, 0, 0).reshape(lines.shape)  33 us
    all_to_all x1, starting transfers between devices, spread_far(): return lax.all_to_all(parts, FAR_AXES, 0, 0).reshape(lines.shape)  12.1 us
    pallas_call x9, Pallas kernels, call(): pl.pallas_call(body, out_shape=[jax.ShapeDtypeStruct(shape, kind) for sha...  9.8 us
    ppermute x4, starting transfers between devices, swap_cores(): return lax.ppermute(array, 'co', [(0, 1), (1, 0)])  7.99 us
    unnamed x28, local copies, waits for them, and re-layouts  5.84 us
    all_to_all x1, waiting for transfers between devices, spread_far(): return lax.all_to_all(parts, FAR_AXES, 0, 0).reshape(lines.shape)  4.84 us
    ppermute x4, waiting for transfers between devices, swap_cores(): return lax.ppermute(array, 'co', [(0, 1), (1, 0)])  4.3 us
  transfers between devices with their start and end apart: 5, of which 4 were waited for; matrix products, arithmetic and copies ran while one was open for 0% of the time, Pallas kernels for 6%

profile of v5, /device:TPU:1, one launch (start us, length us, event | category | flops | bytes accessed | tf_op | source)
XLA Modules:
  0.0 79.0 jit_solution(7402894030305937848)
XLA Ops:
  0.6 0.7 copy-done.4
  1.4 0.9 %shard_map.121 = f32[1536,128]{1,0:T(8,128)} custom-call(f32[6,480]{1,0:T(8,128)S(1)} %copy-done.4), custom_call_target="tpu_custom_call" | custom-call | tf_op jit(solution)/shard_map/pallas_call | solution.py:481
  2.3 12.1 %all-to-all-start = ((f32[64,24,128]{2,1,0:T(8,128)}), f32[64,24,128]{2,1,0:T(8,128)S(1)}, u32[]{:S(2)}, u32[]{:S(2)}) async-start(f32[64,24,128]{2,1,0:T(8,128)} %bitcast), calls=%async_computation | async-start | bytes 1572864 | tf_op jit(solution)/shard_map/all_to_all | solution.py:499
  14.6 0.5 copy-done.12
  15.3 0.6 copy-done.5
  16.0 0.9 %copy-done.2 = bf16[256,480]{0,1:T(8,128)(2,1)S(1)} copy-done((bf16[256,480]{0,1:T(8,128)(2,1)S(1)}, bf16[256,480]{0,1:T(8,128)(2,1)}, u32[]{:S(2)}) %copy-start.2) | copy-done | bytes 245784
  17.0 1.2 %copy-done.6 = bf16[2,480,480]{2,1,0:T(8,128)(2,1)S(1)} copy-done((bf16[2,480,480]{2,1,0:T(8,128)(2,1)S(1)}, bf16[2,480,480]{2,1,0:T(8,128)(2,1)}, u32[]{:S(2)}) %copy-start.6) | copy-done | bytes 921624
  18.2 1.0 %copy-done.7 = bf16[480,480]{1,0:T(8,128)(2,1)S(1)} copy-done((bf16[480,480]{1,0:T(8,128)(2,1)S(1)}, bf16[480,480]{1,0:T(8,128)(2,1)}, u32[]{:S(2)}) %copy-start.7) | copy-done | bytes 460824
  19.2 3.1 %shard_map.122 = (bf16[656,768]{1,0:T(8,128)(2,1)S(1)}, bf16[2,512,512]{2,1,0:T(8,128)(2,1)S(1)}, bf16[512,256]{1,0:T(8,128)(2,1)S(1)}, f32[4,256]{1,0:T(4,128)S...) custom-call(s32[1,768]{1,0:T(1,128)S(1)} %reshape.36.site, ...), custom_call_target="tpu_custom_call" | custom-call | flops 8000000000 | bytes 8000000 | tf_op jit(solution)/shard_map/pallas_call | solution.py:481
  22.3 0.7 copy-done
  23.0 4.8 %all-to-all-done = f32[64,24,128]{2,1,0:T(8,128)S(1)} async-done(((f32[64,24,128]{2,1,0:T(8,128)}), f32[64,24,128]{2,1,0:T(8,128)S(1)}, u32[]{:S(2)}, u32[]{:S(2)}) %all-to-all-start) | async-done | bytes 786464 | tf_op jit(solution)/shard_map/all_to_all | solution.py:499
  27.9 2.9 %collective-permute-start = (f32[1536,128]{1,0:T(8,128)S(1)}, f32[1536,128]{1,0:T(8,128)S(1)}, u32[]{:S(2)}, u32[]{:S(2)}) collective-permute-start(f32[1536,128]{1,0:T(8,128)S(1)} %shard_map.123.near), channel_id=1, source_target_pairs={{0,32},{32,0},{1,33},{33,1},{2,34},{34,2},{3,35},{35,3},{4,36},{36... | collective-permute-start | bytes 2359304 | tf_op jit(solution)/shard_map/ppermute | solution.py:494
  31.1 1.5 %collective-permute-done.peer = f32[1536,128]{1,0:T(8,128)S(1)} collective-permute-done((f32[1536,128]{1,0:T(8,128)S(1)}, f32[1536,128]{1,0:T(8,128)S(1)}, u32[]{:S(2)}, u32[]{:S(2)}) %collective-permute-start) | collective-permute-done | bytes 786464 | tf_op jit(solution)/shard_map/ppermute | solution.py:494
  32.7 1.7 %shard_map.125 = (f32[1536,128]{1,0:T(8,128)S(1)}, f32[8,512]{1,0:T(8,128)S(1)}) custom-call(bf16[384,512]{1,0:T(8,128)(2,1)S(1)} %get-tuple-element.21.near_rows, f32[2,512]{1,0:T(2,128)S(1)} %get-tuple-element.22.near_totals, f32[1536,128]{1,0:T(8,128)S(1)} %collective-permute-done.peer, bf16[656,768]{1,0:T(8,128)(2,1)S(1)} %get-tuple-element.19.pairs, ...), custom_call_target="tpu_custom_call" | custom-call | tf_op jit(solution)/shard_map/pallas_call | solution.py:481
  34.4 18.6 %all_to_all.15 = f32[64,24,128]{2,1,0:T(8,128)S(1)} all-to-all(f32[64,24,128]{2,1,0:T(8,128)S(1)} %bitcast.16), channel_id=1, replica_groups=mesh['xl'=2,'co'=2,'z'=4,'xh'=2,'y'=4] {'xl','z','xh','y'}, dimensions={0} | all-to-all | bytes 1572864 | tf_op jit(solution)/shard_map/all_to_all | solution.py:499
  52.9 2.8 %collective-permute-start.1 = (f32[1536,128]{1,0:T(8,128)S(1)}, f32[1536,128]{1,0:T(8,128)S(1)}, u32[]{:S(2)}, u32[]{:S(2)}) collective-permute-start(f32[1536,128]{1,0:T(8,128)S(1)} %bitcast.11), channel_id=1, source_target_pairs={{0,32},{32,0},{1,33},{33,1},{2,34},{34,2},{3,35},{35,3},{4,36},{36... | collective-permute-start | bytes 2359304 | tf_op jit(solution)/shard_map/ppermute | solution.py:494
  55.7 1.9 %collective-permute-done.1.peer = f32[1536,128]{1,0:T(8,128)S(1)} collective-permute-done((f32[1536,128]{1,0:T(8,128)S(1)}, f32[1536,128]{1,0:T(8,128)S(1)}, u32[]{:S(2)}, u32[]{:S(2)}) %collective-permute-start.1) | collective-permute-done | bytes 786464 | tf_op jit(solution)/shard_map/ppermute | solution.py:494
  57.6 0.4 shard_map.126
  58.0 0.4 collective-permute-start.2
  58.4 1.3 %shard_map.127 = (f32[8,128]{1,0:T(8,128)S(1)}, bf16[656,128]{1,0:T(8,128)(2,1)S(1)}) custom-call(f32[1536,128]{1,0:T(8,128)S(1)} %bitcast.13, f32[1536,128]{1,0:T(8,128)S(1)} %collective-permute-done.1.peer, bf16[656,768]{1,0:T(8,128)(2,1)S(1)} %get-tuple-element.19.pairs, bf16[2,512,512]{2,1,0:T(8,128)(2,1)S(1)} %get-tuple-element.23.tables, ...), custom_call_target="tpu_custom_call" | custom-call | flops 8000000000 | bytes 4000000 | tf_op jit(solution)/shard_map/pallas_call | solution.py:481
  59.7 14.5 %all_to_all.16 = f32[64,8,128]{2,1,0:T(8,128)S(1)} all-to-all(f32[64,8,128]{2,1,0:T(8,128)S(1)} %broadcast_in_dim.2), channel_id=1, replica_groups=mesh['xl'=2,'co'=2,'z'=4,'xh'=2,'y'=4] {'xl','z','xh','y'}, dimensions={0} | all-to-all | bytes 524288 | tf_op jit(solution)/shard_map/all_to_all | solution.py:499
  74.5 1.9 %collective-permute-start.3 = (f32[32,128]{1,0:T(8,128)S(1)}, f32[32,128]{1,0:T(8,128)S(1)}, u32[]{:S(2)}, u32[]{:S(2)}) collective-permute-start(f32[32,128]{1,0:T(8,128)S(1)} %shard_map.128.near), channel_id=1, source_target_pairs={{0,32},{32,0},{1,33},{33,1},{2,34},{34,2},{3,35},{35,3},{4,36},{36... | collective-permute-start | bytes 49160 | tf_op jit(solution)/shard_map/ppermute | solution.py:494
  76.4 0.8 %collective-permute-done.3.peer = f32[32,128]{1,0:T(8,128)S(1)} collective-permute-done((f32[32,128]{1,0:T(8,128)S(1)}, f32[32,128]{1,0:T(8,128)S(1)}, u32[]{:S(2)}, u32[]{:S(2)}) %collective-permute-start.3) | collective-permute-done | bytes 16416 | tf_op jit(solution)/shard_map/ppermute | solution.py:494
  77.2 1.8 %shard_map.129 = (f32[6,480]{1,0:T(8,128)}, f32[6,480]{1,0:T(8,128)}, f32[4]{0:T(128)}) custom-call(f32[32,128]{1,0:T(8,128)S(1)} %shard_map.128.near, f32[32,128]{1,0:T(8,128)S(1)} %collective-permute-done.3.peer, bf16[656,128]{1,0:T(8,128)(2,1)S(1)} %get-tuple-element.34.weights, bf16[2,512,512]{2,1,0:T(8,128)(2,1)S(1)} %get-tuple-element.23.tables, ...), custom_call_target="tpu_custom_call" | custom-call | tf_op jit(solution)/shard_map/pallas_call | solution.py:481
  (33 shorter events, 1.1 us)
Async XLA Ops:
  0.6 0.7 copy-start.4
  2.3 12.1 %copy-start.13 = (s32[768]{0:T(1024)S(1)}, s32[768]{0:T(1024)}, u32[]{:S(2)}) copy-start(s32[768]{0:T(1024)} %param.11) | copy-start | bytes 9220
  2.3 25.6 %all-to-all-start = ((f32[64,24,128]{2,1,0:T(8,128)}), f32[64,24,128]{2,1,0:T(8,128)S(1)}, u32[]{:S(2)}, u32[]{:S(2)}) async-start(f32[64,24,128]{2,1,0:T(8,128)} %bitcast), calls=%async_computation | async-start | bytes 1572864 | tf_op jit(solution)/shard_map/all_to_all | solution.py:499
  14.4 0.7 copy-start.12
  15.2 0.7 copy-start.5
  15.2 0.7 copy-start.11
  15.3 0.7 copy-start.8
  15.3 0.7 copy-start.9
  15.3 0.7 copy-start.10
  16.0 0.9 %copy-start.2 = (bf16[256,480]{0,1:T(8,128)(2,1)S(1)}, bf16[256,480]{0,1:T(8,128)(2,1)}, u32[]{:S(2)}) copy-start(bf16[256,480]{0,1:T(8,128)(2,1)} %param.17) | copy-start | bytes 737284
  17.0 1.2 %copy-start.6 = (bf16[2,480,480]{2,1,0:T(8,128)(2,1)S(1)}, bf16[2,480,480]{2,1,0:T(8,128)(2,1)}, u32[]{:S(2)}) copy-start(bf16[2,480,480]{2,1,0:T(8,128)(2,1)} %axial.1) | copy-start | bytes 2764804
  18.2 1.0 %copy-start.7 = (bf16[480,480]{1,0:T(8,128)(2,1)S(1)}, bf16[480,480]{1,0:T(8,128)(2,1)}, u32[]{:S(2)}) copy-start(bf16[480,480]{1,0:T(8,128)(2,1)} %rotation.1) | copy-start | bytes 1382404
  22.3 0.7 copy-start
  27.9 4.8 %collective-permute-start = (f32[1536,128]{1,0:T(8,128)S(1)}, f32[1536,128]{1,0:T(8,128)S(1)}, u32[]{:S(2)}, u32[]{:S(2)}) collective-permute-start(f32[1536,128]{1,0:T(8,128)S(1)} %shard_map.123.near), channel_id=1, source_target_pairs={{0,32},{32,0},{1,33},{33,1},{2,34},{34,2},{3,35},{35,3},{4,36},{36... | collective-permute-start | bytes 2359304 | tf_op jit(solution)/shard_map/ppermute | solution.py:494
  30.8 1.9 %copy-start.1 = (bf16[512,256]{1,0:T(8,128)(2,1)S(1)}, bf16[512,256]{1,0:T(8,128)(2,1)}, u32[]{:S(2)}) copy-start(bf16[512,256]{1,0:T(8,128)(2,1)} %copy-done) | copy-start | bytes 786436
  30.8 1.9 %copy-start.3 = (bf16[256,480]{0,1:T(8,128)(2,1)S(1)}, bf16[256,480]{0,1:T(8,128)(2,1)}, u32[]{:S(2)}) copy-start(bf16[256,480]{0,1:T(8,128)(2,1)} %param.17) | copy-start | bytes 737284
  52.9 4.7 %collective-permute-start.1 = (f32[1536,128]{1,0:T(8,128)S(1)}, f32[1536,128]{1,0:T(8,128)S(1)}, u32[]{:S(2)}, u32[]{:S(2)}) collective-permute-start(f32[1536,128]{1,0:T(8,128)S(1)} %bitcast.11), channel_id=1, source_target_pairs={{0,32},{32,0},{1,33},{33,1},{2,34},{34,2},{3,35},{35,3},{4,36},{36... | collective-permute-start | bytes 2359304 | tf_op jit(solution)/shard_map/ppermute | solution.py:494
  58.0 1.7 %collective-permute-start.2 = (f32[8,128]{1,0:T(8,128)S(1)}, f32[8,128]{1,0:T(8,128)S(1)}, u32[]{:S(2)}, u32[]{:S(2)}) collective-permute-start(f32[8,128]{1,0:T(8,128)S(1)} %get-tuple-element.30), channel_id=1, source_target_pairs={{0,32},{32,0},{1,33},{33,1},{2,34},{34,2},{3,35},{35,3},{4,36},{36... | collective-permute-start | bytes 12296 | tf_op jit(solution)/shard_map/ppermute | solution.py:494
  74.5 2.8 %collective-permute-start.3 = (f32[32,128]{1,0:T(8,128)S(1)}, f32[32,128]{1,0:T(8,128)S(1)}, u32[]{:S(2)}, u32[]{:S(2)}) collective-permute-start(f32[32,128]{1,0:T(8,128)S(1)} %shard_map.128.near), channel_id=1, source_target_pairs={{0,32},{32,0},{1,33},{33,1},{2,34},{34,2},{3,35},{35,3},{4,36},{36... | collective-permute-start | bytes 49160 | tf_op jit(solution)/shard_map/ppermute | solution.py:494

commit v6 on v5

--- a/solution.py
+++ b/solution.py
@@ -30,6 +30,7 @@
 FAR = 64
 SCALE = 2.0**-14
 PAD = HALF
+SIN_ROWS = (ORDER + 2) * ROWS
 SHARE = 2 * FULL // LANES
 SCALAR_LINE = 2
 SCALARS = SHARE + 4 * GROUPS
@@ -49,30 +50,8 @@
     return np.concatenate([orders, orders]).astype(np.int32)
 
 
-_ORDERS = order_table(ORDER)
-_SORTED = np.lexsort((_ORDERS, np.abs(_ORDERS)))
-_SOURCE = np.full((1, FULL), -1, np.int32)
-_SOURCE[0, :HALF] = _SORTED
-_SOURCE[0, WIDE : WIDE + HALF] = _SORTED + HALF
-
-
-def spans(half):
-    part = _ORDERS[_SORTED][half * LANES : (half + 1) * LANES]
-    found = []
-    for order in dict.fromkeys(int(m) for m in part):
-        lanes = np.flatnonzero(part == order)
-        found.append((order, int(lanes[0]), int(lanes[-1]) + 1))
-    return found
-
-
-SPANS = (spans(0), spans(1))
-
-
-def by_lane(lane, entries):
-    chosen = entries[-1][0]
-    for value, end in reversed(entries[:-1]):
-        chosen = jnp.where(lane < end, value, chosen)
-    return chosen
+_ORDERS = np.zeros((1, WIDE), np.int32)
+_ORDERS[0, :HALF] = order_table(ORDER)
 
 
 def dot(a, b):
@@ -99,9 +78,15 @@
     return total
 
 
-def onehot_in(source):
-    rows = lax.broadcasted_iota(jnp.int32, (COEFF, FULL), 0)
-    return jnp.where(rows == source, 1.0, 0.0).astype(BF)
+def padded(x, axis):
+    zeros = jnp.zeros((x.shape[0], WIDE - HALF) if axis else (WIDE - HALF, x.shape[1]), x.dtype)
+    low, high = (x[:, :HALF], x[:, HALF:]) if axis else (x[:HALF, :], x[HALF:, :])
+    return jnp.concatenate([low, zeros, high, zeros], axis=axis)
+
+
+def own_rows(incident):
+    value = jnp.concatenate([incident[...], jnp.zeros((ROWS - OWN, COEFF), F32)], axis=0) * SCALE
+    return padded(value, 1)
 
 
 def own_group():
@@ -109,9 +94,7 @@
 
 
 def send_body(incident, chunk, lines):
-    value = jnp.concatenate([incident[...], jnp.zeros((ROWS - OWN, COEFF), F32)], axis=0) * SCALE
-    value = jnp.concatenate([value, jnp.zeros((ROWS, FULL - COEFF), F32)], axis=1)
-    write_chunks(value, chunk, lines)
+    write_chunks(own_rows(incident), chunk, lines)
 
 
 def write_chunks(rows, chunk, lines):
@@ -123,8 +106,8 @@
 
 
 def prepare_body(
-    site, jitter, rotation, axial, probes, probe_group, tmat, source, incident, radius,
-    pairs, tables, probes_out, seen_out, tmat_out, inwards_out, base_out, radius_out,
+    site, jitter, rotation, axial, probes, probe_group, tmat, orders, incident, radius,
+    pairs, tables, probes_out, seen_out, tmat_out, orders_out, base_out, radius_out,
 ):
     own = (
         lax.axis_index("xl") * PER_GROUP
@@ -177,19 +160,16 @@
                 sin_k * cos_one + cos_k * sin_one,
             )
 
-    inwards = onehot_in(source[...])
-    inwards_out[...] = inwards
-    outwards = inwards.astype(F32).T.astype(BF)
-    probes_out[...] = dot(outwards, probes[...]).astype(BF)
-    turned = dot(outwards, rotation[...]).astype(BF)
+    probes_out[...] = padded(probes[...], 0)
+    turned = padded(rotation[...], 0)
     for radial in range(2):
         tables[radial] = fine_dot(0.5 * dot(turned, axial[radial]), turned, dot_t, 2).astype(BF)
     line = lax.broadcasted_iota(jnp.int32, (GROUPS, PROBES_OWN), 0)
     seen_out[...] = jnp.where(line == probe_group[...], 1.0, 0.0)
-    tmat_rows = jnp.concatenate([tmat[...], jnp.zeros((ROWS - 2, HALF), F32)], axis=0)
-    tmat_out[...] = fine_dot(tmat_rows, inwards[:HALF, :WIDE])
-    value = jnp.concatenate([incident[...], jnp.zeros((ROWS - OWN, COEFF), F32)], axis=0) * SCALE
-    base_out[...] = fine_dot(value, inwards)
+    tmat_rows = jnp.concatenate([tmat[...], jnp.zeros((2, WIDE - HALF), F32)], axis=1)
+    tmat_out[...] = jnp.concatenate([tmat_rows, jnp.zeros((ROWS - 2, WIDE), F32)], axis=0)
+    orders_out[...] = jnp.broadcast_to(orders[...], (ROWS, WIDE))
+    base_out[...] = own_rows(incident)
     line = lax.broadcasted_iota(jnp.int32, (ROWS, LANES), 0)
     column = jnp.zeros((ROWS, LANES), F32)
     for r in range(OWN):
@@ -223,70 +203,87 @@
     del near_in, pairs, near_out
 
 
-def near_body(near, inwards, rows_out, totals_out):
-    rows_out[...] = dot(load_rows(near)[:, :COEFF], inwards[...]).astype(BF)
+def first_near_body(near, pairs, sums_out, totals_out):
+    sums_out[...] = dot(pairs[:, : SPHERES // 2], load_rows(near))
     totals_out[...] = half_sums(near)
 
 
-def mix(sums, shifted, tables, dot=dot):
-    for k in range(1, TOP + 1):
-        at_cos, at_sin = pl.ds(k * BLOCK, BLOCK), pl.ds((TOP + k) * BLOCK, BLOCK)
-        cos_re, cos_im = sums[at_cos, :WIDE], sums[at_cos, WIDE:]
-        sin_re, sin_im = sums[at_sin, :WIDE], sums[at_sin, WIDE:]
-        sums[at_cos, :WIDE] = cos_re - sin_im
-        sums[at_cos, WIDE:] = cos_im + sin_re
-        sums[at_sin, :WIDE] = cos_re + sin_im
-        sums[at_sin, WIDE:] = cos_im - sin_re
-
-    def block_of(k):
-        return (k if k >= 0 else TOP - k) * BLOCK
-
+def second_near_body(near, pairs, probes, seen, sums_out, gradient_out):
+    sums_out[...] = dot(pairs[:, : SPHERES // 2], load_rows(near))
+    gradient_out[...] = half_gradient(near, probes, seen, lax.axis_index("co"))
+
+
+def half_gradient(lines, probes, seen, core):
+    totals = half_sums(lines)
+    lane = lax.broadcasted_iota(jnp.int32, totals.shape, 1)
+    totals = jnp.where((lane & (WIDE - 1)) < HALF, totals, 0.0)
+    first, second = seen[0:2, :], seen[2:4, :]
+    mask = jnp.concatenate(
+        [jnp.where(core == 0, part[0:1], part[1:2]) for part in (first, second)], axis=0
+    )
+    return gradient_of(totals, probes, mask)
+
+
+def by_order(values, bits):
+    for bit, mask in zip((16, 8, 4, 2, 1), bits):
+        count = TOP + bit
+        values = [
+            jnp.where(mask, values[j + bit], values[j]) if j + bit < len(values) else values[j]
+            for j in range(count)
+        ]
+    return values
+
+
+def mix(sums, shifted, tables, orders, dot=dot):
+    zeros = jnp.zeros((ROWS, LANES), F32)
     for half in range(2):
-        lane = lax.broadcasted_iota(jnp.int32, (BLOCK, LANES), 1)
-
-        def pick(out_order, start):
-            columns = slice(start + half * LANES, start + (half + 1) * LANES)
-            entries = []
-            for order, _, end in SPANS[half]:
-                row = block_of(order - out_order)
-                entries.append((sums[row : row + BLOCK, columns], end))
-            return by_lane(lane, entries)
-
-        for out_order in range(ORDER + 1):
-            minus_re, minus_im = pick(out_order, 0), pick(out_order, WIDE)
-            if out_order:
-                plus_re, plus_im = pick(-out_order, 0), pick(-out_order, WIDE)
-            else:
-                plus_re, plus_im = minus_re, minus_im
-            cos_part = (minus_re + plus_re, minus_im + plus_im)
-            sin_part = (plus_im - minus_im, minus_re - plus_re)
-            for which, start in ((0, 0), (1, WIDE)):
-                columns = slice(start + half * LANES, start + (half + 1) * LANES)
-                for radial in range(2):
-                    lines = slice(radial * ROWS, (radial + 1) * ROWS)
-                    value = jnp.concatenate([cos_part[which][lines], sin_part[which][lines]], axis=0)
-                    shifted[radial, out_order * BLOCK : (out_order + 1) * BLOCK, columns] = value.astype(BF)
+        code = orders[:, half * LANES : (half + 1) * LANES] + ORDER
+        bits = [(code & bit) != 0 for bit in (16, 8, 4, 2, 1)]
+        real = slice(half * LANES, (half + 1) * LANES)
+        imag = slice(WIDE + half * LANES, WIDE + (half + 1) * LANES)
+        for radial in range(2):
+
+            def load(block, columns):
+                at = block * BLOCK + radial * ROWS
+                return sums[at : at + ROWS, columns]
+
+            for is_imag, columns, others in ((0, real, imag), (1, imag, real)):
+                plus, minus = [load(0, columns)], []
+                for k in range(1, TOP + 1):
+                    cos_sum, sin_sum = load(k, columns), load(TOP + k, others)
+                    plus.append(cos_sum + sin_sum if is_imag else cos_sum - sin_sum)
+                    minus.append(cos_sum - sin_sum if is_imag else cos_sum + sin_sum)
+                chosen = by_order(minus[::-1] + plus, bits)
+                cos_part, sin_part = [], []
+                for m in range(ORDER + 1):
+                    ahead, behind = chosen[ORDER - m], chosen[ORDER + m]
+                    cos_part.append(ahead + behind)
+                    sin_part.append(behind - ahead if is_imag else ahead - behind)
+                cos_part.append(zeros)
+                for m in range(0, ORDER + 1, 2):
+                    value = jnp.concatenate(cos_part[m : m + 2], axis=0)
+                    shifted[radial, m * ROWS : (m + 2) * ROWS, columns] = value.astype(BF)
+                for m in range(1, ORDER + 1, 2):
+                    value = jnp.concatenate(sin_part[m : m + 2], axis=0)
+                    at = SIN_ROWS + (m - 1) * ROWS
+                    shifted[radial, at : at + 2 * ROWS, others] = value.astype(BF)
 
     back = dot(shifted[0], tables[0]) + dot(shifted[1], tables[1])
     parts_re, parts_im = [], []
-    lane = lax.broadcasted_iota(jnp.int32, (ROWS, LANES), 1)
     for half in range(2):
         real = slice(half * LANES, (half + 1) * LANES)
         imag = slice(WIDE + half * LANES, WIDE + (half + 1) * LANES)
-        entries_re, entries_im = [], []
-        for order, _, end in SPANS[half]:
-            m = abs(order)
-            cos_lines = slice(m * BLOCK, m * BLOCK + ROWS)
-            sin_lines = slice(m * BLOCK + ROWS, (m + 1) * BLOCK)
-            value_re, value_im = back[cos_lines, real], back[cos_lines, imag]
-            if order > 0:
-                value_re, value_im = value_re + back[sin_lines, imag], value_im - back[sin_lines, real]
-            if order < 0:
-                value_re, value_im = value_re - back[sin_lines, imag], value_im + back[sin_lines, real]
-            entries_re.append((value_re, end))
-            entries_im.append((value_im, end))
-        parts_re.append(by_lane(lane, entries_re))
-        parts_im.append(by_lane(lane, entries_im))
+        order = orders[:, real]
+        size = jnp.abs(order)
+        sign = jnp.where(order > 0, 1.0, -1.0)
+        field_re, field_im = back[0:ROWS, real], back[0:ROWS, imag]
+        for m in range(1, ORDER + 1):
+            cos_lines = slice(m * ROWS, (m + 1) * ROWS)
+            sin_lines = slice(SIN_ROWS + (m - 1) * ROWS, SIN_ROWS + m * ROWS)
+            field_re = jnp.where(size == m, back[cos_lines, real] + sign * back[sin_lines, imag], field_re)
+            field_im = jnp.where(size == m, back[cos_lines, imag] - sign * back[sin_lines, real], field_im)
+        parts_re.append(field_re)
+        parts_im.append(field_im)
     return jnp.concatenate(parts_re + parts_im, axis=1)
 
 
@@ -304,14 +301,12 @@
 
 
 def first_body(
-    near_rows, near_totals, peer, pairs, inwards, tables, tmat, radius, plain_probes, probes, seen,
+    near_sums, near_totals, peer, pairs, tables, tmat, radius, orders, probes, seen,
     chunk, rows_out, sums, shifted, lines,
 ):
-    rows = dot(load_rows(peer)[:, :COEFF], inwards[...]).astype(BF)
-    sums[...] = dot(pairs[...], jnp.concatenate([near_rows[...], rows], axis=0))
-    totals = all_groups(near_totals[...], half_sums(peer))[:, :COEFF]
-    gradient = gradient_of(totals, plain_probes, probes, seen)
-    field = mix(sums, shifted, tables)
+    sums[...] = near_sums[...] + dot(pairs[:, SPHERES // 2 :], load_rows(peer))
+    gradient = gradient_of(all_groups(near_totals[...], half_sums(peer)), probes, seen[...])
+    field = mix(sums, shifted, tables, orders)
     image = scatter(field, tmat, radius[...])
     rows_out[...] = image
     lane = lax.broadcasted_iota(jnp.int32, (ROWS, FULL), 1)
@@ -349,9 +344,9 @@
     )
 
 
-def gradient_of(totals, from_probes, to_probes, seen):
-    values = fine_dot(totals, from_probes[...], parts=2) * seen[...]
-    return fine_dot(values, to_probes[...], dot_t, 2)
+def gradient_of(totals, probes, seen):
+    values = fine_dot(totals, probes[...], parts=2) * seen
+    return fine_dot(values, probes[...], dot_t, 2)
 
 
 def to_lines(rows):
@@ -363,28 +358,21 @@
     return jnp.concatenate([lines[part * each : (part + 1) * each, :] for part in range(4)], axis=1)
 
 
-def second_gradient_body(near, peer, probes, seen, keep, send):
-    totals = all_groups(half_sums(near), half_sums(peer))
-    lane = lax.broadcasted_iota(jnp.int32, totals.shape, 1)
-    totals = jnp.where((lane & (WIDE - 1)) < HALF, totals, 0.0)
-    gradient = gradient_of(totals, probes, probes, seen)
-    core = lax.axis_index("co")
-    low, high = to_lines(gradient[:2]), to_lines(gradient[2:])
-    keep[...] = jnp.where(core == 0, low, high)
-    send[...] = jnp.where(core == 0, high, low)
+def second_gradient_body(peer, probes, seen, send):
+    send[...] = to_lines(half_gradient(peer, probes, seen, 1 - lax.axis_index("co")))
 
 
 def second_body(
-    near, peer, pairs, tables, tmat, radius, base, image,
+    near, near_sums, near_gradient, peer, pairs, tables, tmat, radius, orders, base, image,
     extra, weights_out, sums, shifted,
 ):
-    sums[...] = dot(pairs[...], jnp.concatenate([load_rows(near), load_rows(peer)], axis=0))
+    sums[...] = near_sums[...] + dot(pairs[:, SPHERES // 2 :], load_rows(peer))
     for block in range(BLOCKS):
         k = block if block <= TOP else block - TOP
         at = pl.ds(block * BLOCK, BLOCK)
         value = sums[at, LANES:WIDE]
         weights_out[at, :] = (value if k % 2 == 0 else -value).astype(BF)
-    field = mix(sums, shifted, tables)
+    field = mix(sums, shifted, tables, orders)
     last = scatter(field, tmat, radius[...])
     zero, one = base[...], image[...]
     line = lax.broadcasted_iota(jnp.int32, (SHARE, LANES), 0)
@@ -402,7 +390,7 @@
     for piece in range(2):
         value = jnp.sum(near[pl.ds(SLICE_LINES[piece], FAR, stride=CHUNK), :], axis=0, keepdims=True)
         out = jnp.where((line == PIECE_LINES[piece]) & (lane >= LANES - 16), value, out)
-    extra[...] = out
+    extra[...] = out + to_lines(near_gradient[...])
 
 
 def sum_body(near, out):
@@ -419,7 +407,7 @@
 
 
 def finish_body(
-    near, peer, weights, tables, tmat, inwards, incident, image,
+    near, peer, weights, tables, tmat, orders, incident, image,
     solution_out, sensitivity_out, arnoldi_out, places, sums, shifted,
 ):
     g00, g01, g11, g02, g12, g22 = [near[at : at + 1, :] + peer[at : at + 1, :] for at in range(SCALARS, SCALARS + 6)]
@@ -428,8 +416,8 @@
     core = lax.axis_index("co")
     first = from_lines(near[SHARE:SCALARS, :] + peer[SHARE:SCALARS, :])
     mine, other = from_lines(near[:SHARE, :]), from_lines(peer[:SHARE, :])
-    low, high = jnp.where(core == 0, mine, other), jnp.where(core == 0, other, mine)
-    second = jnp.concatenate([low, high], axis=0)
+    even, odd = jnp.where(core == 0, mine, other), jnp.where(core == 0, other, mine)
+    second = jnp.concatenate([even[0:1], odd[0:1], even[1:2], odd[1:2]], axis=0)
     diag_first = 1.0 + g01
     below_sq = g11 - g01 * g01
     inverse = 1.0 / below_sq
@@ -462,18 +450,20 @@
     places[at, :WIDE] = real * grad_re + imag * grad_im
     places[at, WIDE:] = real * grad_im - imag * grad_re
     sums[...] = dot(weights[...], places[...].astype(BF))
-    field = mix(sums, shifted, tables, dot_t)
+    field = mix(sums, shifted, tables, orders, dot_t)
     group = own_group()
     own = jnp.zeros((1, FULL), F32)
     for g in range(GROUPS):
         own = jnp.where(group == g, gradient[g : g + 1, :], own)
     lane = lax.broadcasted_iota(jnp.int32, (1, FULL), 1)
     own = jnp.where((lane & (WIDE - 1)) < HALF, own, 0.0)
-    both = jnp.concatenate([image[...], own - field], axis=0)
-    result = fine_dot(both, inwards[...], dot_t)
-    image_rows = result[:OWN]
+    image_rows = unpadded(image[...])
     solution_out[...] = for_base[:, :COEFF] * incident[...] + (for_image[:, :COEFF] / SCALE) * image_rows
-    sensitivity_out[...] = result[ROWS : ROWS + OWN]
+    sensitivity_out[...] = unpadded(own - field)
+
+
+def unpadded(rows):
+    return jnp.concatenate([rows[:OWN, :HALF], rows[:OWN, WIDE : WIDE + HALF]], axis=1)
 
 
 def call(body, outs, scratch=(), operands=(), spaces=None, out_spaces=None, cost=None, aliases=None):
@@ -524,8 +514,7 @@
         lead = array.shape[:-1]
         return jnp.swapaxes(array.reshape(lead + (2, 2, PER_GROUP)), -3, -2).reshape(lead + (SPHERES,))
 
-    plain_probes = probe_field.T
-    pairs, tables, probes, seen, tmat, inwards, base, radius = call(
+    pairs, tables, probes, seen, tmat, orders, base, radius = call(
         prepare_body,
         [
             ((BLOCKS * BLOCK, SPHERES), BF),
@@ -533,7 +522,7 @@
             ((FULL, PROBES_OWN), BF),
             ((GROUPS, PROBES_OWN), F32),
             ((ROWS, WIDE), F32),
-            ((COEFF, FULL), BF),
+            ((ROWS, WIDE), jnp.int32),
             rows_shape,
             ((ROWS, LANES), F32),
         ],
@@ -542,10 +531,10 @@
             by_core(jitter),
             rotation_table,
             axial_tables,
-            plain_probes,
+            probe_field.T,
             probe_group.reshape(1, PROBES_OWN),
             tmatrix,
-            jnp.asarray(_SOURCE),
+            jnp.asarray(_ORDERS),
             incident,
             radius_factor,
         ),
@@ -555,31 +544,38 @@
 
     near = spread_far(chunk)
     (near,) = call(order_body, [chunk_shape], operands=(near, pairs), spaces={1: pl.ANY}, aliases={0: 0})
-    near_rows, near_totals = call(
-        near_body,
-        [((SPHERES // 2, FULL), BF), ((2, FULL), F32)],
-        operands=(near, inwards),
+    sums_shape = ((BLOCKS * BLOCK, FULL), F32)
+    near_sums, near_totals = call(
+        first_near_body,
+        [sums_shape, ((2, FULL), F32)],
+        operands=(near, pairs),
         cost=half_cost,
     )
     chunk, image = call(
         first_body,
         [chunk_shape, rows_shape],
         [sum_scratch, shift_scratch, line_scratch],
-        (near_rows, near_totals, swap_cores(near), pairs, inwards, tables, tmat, radius, plain_probes, probes, seen),
+        (near_sums, near_totals, swap_cores(near), pairs, tables, tmat, radius, orders, probes, seen),
     )
 
     near = spread_far(chunk)
     peer = swap_cores(near)
-    keep, send = call(second_gradient_body, [share_shape, share_shape], operands=(near, peer, probes, seen))
+    near_sums, near_gradient = call(
+        second_near_body,
+        [sums_shape, ((2, FULL), F32)],
+        operands=(near, pairs, probes, seen),
+        cost=half_cost,
+    )
+    (send,) = call(second_gradient_body, [share_shape], operands=(peer, probes, seen))
     received = swap_cores(send)
     extra, weights = call(
         second_body,
         [share_shape, ((BLOCKS * BLOCK, LANES), BF)],
         [sum_scratch, shift_scratch],
-        (near, peer, pairs, tables, tmat, radius, base, image),
+        (near, near_sums, near_gradient, peer, pairs, tables, tmat, radius, orders, base, image),
         cost=half_cost,
     )
-    share = keep + received + extra
+    share = received + extra
     near = spread_far(jnp.broadcast_to(share[None], (FAR, SHARE, LANES)).reshape(FAR * SHARE, LANES))
     (near,) = call(sum_body, [((SCALARS + 8, LANES), F32)], operands=(near,))
     peer = swap_cores(near)
@@ -587,7 +583,7 @@
         finish_body,
         [((OWN, COEFF), F32), ((OWN, COEFF), F32), ((4,), F32)],
         [pltpu.VMEM((LANES, FULL), F32), sum_scratch, shift_scratch],
-        (near, peer, weights, tables, tmat, inwards, incident, image),
+        (near, peer, weights, tables, tmat, orders, incident, image),
         out_spaces={2: pltpu.SMEM},
     )
     return solution_rows, sensitivity_rows, arnoldi

time: 79.6 us -> 78.7 us (0.989)
  local copies, waits for them, and re-layouts: 6.21 us -> 3.35 us
  waiting for transfers between devices: 9.14 us -> 11.7 us
    all_to_all x1, waiting for transfers between devices: 4.84 us -> 8.21 us  [spread_far(): return lax.all_to_all(parts, FAR_AXES, 0, 0).reshape(lines.shape)]
    unnamed x28 -> x22, local copies, waits for them, and re-layouts: 5.84 us -> 2.97 us
    ppermute x4, waiting for transfers between devices: 4.3 us -> 3.44 us  [swap_cores(): return lax.ppermute(array, 'co', [(0, 1), (1, 0)])]
    pallas_call x9 -> x10, Pallas kernels: 9.8 us -> 9.55 us  [call(): pl.pallas_call(body, out_shape=[jax.ShapeDtypeStruct(shape, kind) for sha...]
where the time goes in v6:
time: 78.7 us; the launch traced here: 78.3 us
  blocking collectives  33 us (42%)
  starting transfers between devices  19.9 us (25%)
  waiting for transfers between devices  11.7 us (15%)
  Pallas kernels  9.55 us (12%)
  local copies, waits for them, and re-layouts  3.35 us (4%)
  between operations  0.79 us (1%)
    all_to_all x2, blocking collectives, spread_far(): return lax.all_to_all(parts, FAR_AXES, 0, 0).reshape(lines.shape)  33 us
    all_to_all x1, starting transfers between devices, spread_far(): return lax.all_to_all(parts, FAR_AXES, 0, 0).reshape(lines.shape)  12 us
    pallas_call x10, Pallas kernels, call(): pl.pallas_call(body, out_shape=[jax.ShapeDtypeStruct(shape, kind) for sha...  9.55 us
    all_to_all x1, waiting for transfers between devices, spread_far(): return lax.all_to_all(parts, FAR_AXES, 0, 0).reshape(lines.shape)  8.21 us
    ppermute x4, starting transfers between devices, swap_cores(): return lax.ppermute(array, 'co', [(0, 1), (1, 0)])  7.97 us
    ppermute x4, waiting for transfers between devices, swap_cores(): return lax.ppermute(array, 'co', [(0, 1), (1, 0)])  3.44 us
    unnamed x22, local copies, waits for them, and re-layouts  2.97 us
  transfers between devices with their start and end apart: 5, of which 4 were waited for; matrix products, arithmetic and copies ran while one was open for 0% of the time, Pallas kernels for 6%

profile of v6, /device:TPU:1, one launch (start us, length us, event | category | flops | bytes accessed | tf_op | source)
XLA Modules:
  0.0 78.3 jit_solution(6403551818991232398)
XLA Ops:
  0.6 0.7 copy-done
  1.4 1.0 %shard_map.121 = f32[1536,128]{1,0:T(8,128)} custom-call(f32[6,480]{1,0:T(8,128)S(1)} %copy-done), custom_call_target="tpu_custom_call" | custom-call | tf_op jit(solution)/shard_map/pallas_call | solution.py:471
  2.4 12.0 %all-to-all-start = ((f32[64,24,128]{2,1,0:T(8,128)}), f32[64,24,128]{2,1,0:T(8,128)S(1)}, u32[]{:S(2)}, u32[]{:S(2)}) async-start(f32[64,24,128]{2,1,0:T(8,128)} %bitcast), calls=%async_computation | async-start | bytes 1572864 | tf_op jit(solution)/shard_map/all_to_all | solution.py:489
  14.6 0.1 reshape.37
  14.8 1.2 %copy-done.2 = bf16[2,480,480]{2,1,0:T(8,128)(2,1)S(1)} copy-done((bf16[2,480,480]{2,1,0:T(8,128)(2,1)S(1)}, bf16[2,480,480]{2,1,0:T(8,128)(2,1)}, u32[]{:S(2)}) %copy-start.2) | copy-done | bytes 921624
  16.0 1.0 %copy-done.3 = bf16[480,480]{1,0:T(8,128)(2,1)S(1)} copy-done((bf16[480,480]{1,0:T(8,128)(2,1)S(1)}, bf16[480,480]{1,0:T(8,128)(2,1)}, u32[]{:S(2)}) %copy-start.3) | copy-done | bytes 460824
  17.0 2.6 %shard_map.122 = (bf16[656,768]{1,0:T(8,128)(2,1)S(1)}, bf16[2,512,512]{2,1,0:T(8,128)(2,1)S(1)}, bf16[512,256]{1,0:T(8,128)(2,1)S(1)}, f32[4,256]{1,0:T(4,128)S...) custom-call(s32[1,768]{1,0:T(1,128)S(1)} %reshape.36.site, ...), custom_call_target="tpu_custom_call" | custom-call | flops 8000000000 | bytes 8000000 | tf_op jit(solution)/shard_map/pallas_call | solution.py:471
  19.7 8.2 %all-to-all-done = f32[64,24,128]{2,1,0:T(8,128)S(1)} async-done(((f32[64,24,128]{2,1,0:T(8,128)}), f32[64,24,128]{2,1,0:T(8,128)S(1)}, u32[]{:S(2)}, u32[]{:S(2)}) %all-to-all-start) | async-done | bytes 786464 | tf_op jit(solution)/shard_map/all_to_all | solution.py:489
  27.9 2.9 %collective-permute-start = (f32[1536,128]{1,0:T(8,128)S(1)}, f32[1536,128]{1,0:T(8,128)S(1)}, u32[]{:S(2)}, u32[]{:S(2)}) collective-permute-start(f32[1536,128]{1,0:T(8,128)S(1)} %shard_map.123.near), channel_id=1, source_target_pairs={{0,32},{32,0},{1,33},{33,1},{2,34},{34,2},{3,35},{35,3},{4,36},{36... | collective-permute-start | bytes 2359304 | tf_op jit(solution)/shard_map/ppermute | solution.py:484
  30.8 0.5 shard_map.124
  31.3 1.4 %collective-permute-done.peer = f32[1536,128]{1,0:T(8,128)S(1)} collective-permute-done((f32[1536,128]{1,0:T(8,128)S(1)}, f32[1536,128]{1,0:T(8,128)S(1)}, u32[]{:S(2)}, u32[]{:S(2)}) %collective-permute-start) | collective-permute-done | bytes 786464 | tf_op jit(solution)/shard_map/ppermute | solution.py:484
  32.7 1.3 %shard_map.125 = (f32[1536,128]{1,0:T(8,128)S(1)}, f32[8,512]{1,0:T(8,128)S(1)}) custom-call(f32[656,512]{1,0:T(8,128)S(1)} %get-tuple-element.20.near_sums, f32[2,512]{1,0:T(2,128)S(1)} %get-tuple-element.21.near_totals, f32[1536,128]{1,0:T(8,128)S(1)} %collective-permute-done.peer, bf16[656,768]{1,0:T(8,128)(2,1)S(1)} %get-tuple-element.19.pairs, ...), custom_call_target="tpu_custom_call" | custom-call | tf_op jit(solution)/shard_map/pallas_call | solution.py:471
  34.0 18.6 %all_to_all.15 = f32[64,24,128]{2,1,0:T(8,128)S(1)} all-to-all(f32[64,24,128]{2,1,0:T(8,128)S(1)} %bitcast.16), channel_id=1, replica_groups=mesh['xl'=2,'co'=2,'z'=4,'xh'=2,'y'=4] {'xl','z','xh','y'}, dimensions={0} | all-to-all | bytes 1572864 | tf_op jit(solution)/shard_map/all_to_all | solution.py:489
  52.6 2.8 %collective-permute-start.1 = (f32[1536,128]{1,0:T(8,128)S(1)}, f32[1536,128]{1,0:T(8,128)S(1)}, u32[]{:S(2)}, u32[]{:S(2)}) collective-permute-start(f32[1536,128]{1,0:T(8,128)S(1)} %bitcast.13), channel_id=1, source_target_pairs={{0,32},{32,0},{1,33},{33,1},{2,34},{34,2},{3,35},{35,3},{4,36},{36... | collective-permute-start | bytes 2359304 | tf_op jit(solution)/shard_map/ppermute | solution.py:484
  55.3 0.7 shard_map.127
  56.0 1.2 %collective-permute-done.1.peer = f32[1536,128]{1,0:T(8,128)S(1)} collective-permute-done((f32[1536,128]{1,0:T(8,128)S(1)}, f32[1536,128]{1,0:T(8,128)S(1)}, u32[]{:S(2)}, u32[]{:S(2)}) %collective-permute-start.1) | collective-permute-done | bytes 786464 | tf_op jit(solution)/shard_map/ppermute | solution.py:484
  57.2 0.3 shard_map.126
  57.5 0.4 collective-permute-start.2
  57.9 1.2 %shard_map.128 = (f32[8,128]{1,0:T(8,128)S(1)}, bf16[656,128]{1,0:T(8,128)(2,1)S(1)}) custom-call(f32[1536,128]{1,0:T(8,128)S(1)} %bitcast.15, f32[656,512]{1,0:T(8,128)S(1)} %get-tuple-element.29.near_sums, f32[2,512]{1,0:T(2,128)S(1)} %get-tuple-element.30.near_gradient, f32[1536,128]{1,0:T(8,128)S(1)} %collective-permute-done.1.peer, ...), custom_call_target="tpu_custom_call" | custom-call | flops 8000000000 | bytes 4000000 | tf_op jit(solution)/shard_map/pallas_call | solution.py:471
  59.2 14.5 %all_to_all.16 = f32[64,8,128]{2,1,0:T(8,128)S(1)} all-to-all(f32[64,8,128]{2,1,0:T(8,128)S(1)} %broadcast_in_dim.2), channel_id=1, replica_groups=mesh['xl'=2,'co'=2,'z'=4,'xh'=2,'y'=4] {'xl','z','xh','y'}, dimensions={0} | all-to-all | bytes 524288 | tf_op jit(solution)/shard_map/all_to_all | solution.py:489
  73.6 0.2 shard_map.129.near
  73.9 1.9 %collective-permute-start.3 = (f32[32,128]{1,0:T(8,128)S(1)}, f32[32,128]{1,0:T(8,128)S(1)}, u32[]{:S(2)}, u32[]{:S(2)}) collective-permute-start(f32[32,128]{1,0:T(8,128)S(1)} %shard_map.129.near), channel_id=1, source_target_pairs={{0,32},{32,0},{1,33},{33,1},{2,34},{34,2},{3,35},{35,3},{4,36},{36... | collective-permute-start | bytes 49160 | tf_op jit(solution)/shard_map/ppermute | solution.py:484
  75.8 0.8 %collective-permute-done.3.peer = f32[32,128]{1,0:T(8,128)S(1)} collective-permute-done((f32[32,128]{1,0:T(8,128)S(1)}, f32[32,128]{1,0:T(8,128)S(1)}, u32[]{:S(2)}, u32[]{:S(2)}) %collective-permute-start.3) | collective-permute-done | bytes 16416 | tf_op jit(solution)/shard_map/ppermute | solution.py:484
  76.6 1.7 %shard_map.130 = (f32[6,480]{1,0:T(8,128)}, f32[6,480]{1,0:T(8,128)}, f32[4]{0:T(128)}) custom-call(f32[32,128]{1,0:T(8,128)S(1)} %shard_map.129.near, f32[32,128]{1,0:T(8,128)S(1)} %collective-permute-done.3.peer, bf16[656,128]{1,0:T(8,128)(2,1)S(1)} %get-tuple-element.34.weights, bf16[2,512,512]{2,1,0:T(8,128)(2,1)S(1)} %get-tuple-element.22.tables, ...), custom_call_target="tpu_custom_call" | custom-call | tf_op jit(solution)/shard_map/pallas_call | solution.py:471
  (28 shorter events, 0.3 us)
Async XLA Ops:
  0.6 0.7 copy-start
  1.4 13.0 %copy-start.10 = (s32[768]{0:T(1024)S(1)}, s32[768]{0:T(1024)}, u32[]{:S(2)}) copy-start(s32[768]{0:T(1024)} %param.11) | copy-start | bytes 9220
  1.4 13.2 %copy-start.9 = (f32[3,768]{1,0:T(4,128)S(1)}, f32[3,768]{1,0:T(4,128)}, u32[]{:S(2)}) copy-start(f32[3,768]{1,0:T(4,128)} %param.12) | copy-start | bytes 27652
  1.4 13.4 %copy-start.1 = (f32[6,480]{1,0:T(8,128)S(1)}, f32[6,480]{1,0:T(8,128)}, u32[]{:S(2)}) copy-start(f32[6,480]{1,0:T(8,128)} %incident.5) | copy-start | bytes 34564
  1.4 13.4 %copy-start.4 = (bf16[256,480]{0,1:T(8,128)(2,1)S(1)}, bf16[256,480]{0,1:T(8,128)(2,1)}, u32[]{:S(2)}) copy-start(bf16[256,480]{0,1:T(8,128)(2,1)} %param.17) | copy-start | bytes 737284
  1.4 13.4 %copy-start.5 = (f32[2,240]{1,0:T(2,128)S(1)}, f32[2,240]{1,0:T(2,128)}, u32[]{:S(2)}) copy-start(f32[2,240]{1,0:T(2,128)} %tmat.1) | copy-start | bytes 5764
  1.4 13.4 %copy-start.6 = (s32[256]{0:T(256)S(1)}, s32[256]{0:T(256)}, u32[]{:S(2)}) copy-start(s32[256]{0:T(256)} %param.18) | copy-start | bytes 3076
  1.4 13.4 %copy-start.7 = (f32[6]{0:T(128)S(1)}, f32[6]{0:T(128)}, u32[]{:S(2)}) copy-start(f32[6]{0:T(128)} %radius.1) | copy-start | bytes 76
  1.4 13.4 %copy-start.8 = (s32[1,256]{1,0:T(1,128)S(1)}, s32[1,256]{1,0:T(1,128)}, u32[]{:S(2)}) copy-start(s32[1,256]{1,0:T(1,128)} %constant.2.clone.orders) | copy-start | bytes 3076
  2.4 25.5 %all-to-all-start = ((f32[64,24,128]{2,1,0:T(8,128)}), f32[64,24,128]{2,1,0:T(8,128)S(1)}, u32[]{:S(2)}, u32[]{:S(2)}) async-start(f32[64,24,128]{2,1,0:T(8,128)} %bitcast), calls=%async_computation | async-start | bytes 1572864 | tf_op jit(solution)/shard_map/all_to_all | solution.py:489
  14.8 1.2 %copy-start.2 = (bf16[2,480,480]{2,1,0:T(8,128)(2,1)S(1)}, bf16[2,480,480]{2,1,0:T(8,128)(2,1)}, u32[]{:S(2)}) copy-start(bf16[2,480,480]{2,1,0:T(8,128)(2,1)} %axial.1) | copy-start | bytes 2764804
  16.0 1.0 %copy-start.3 = (bf16[480,480]{1,0:T(8,128)(2,1)S(1)}, bf16[480,480]{1,0:T(8,128)(2,1)}, u32[]{:S(2)}) copy-start(bf16[480,480]{1,0:T(8,128)(2,1)} %rotation.1) | copy-start | bytes 1382404
  27.9 4.8 %collective-permute-start = (f32[1536,128]{1,0:T(8,128)S(1)}, f32[1536,128]{1,0:T(8,128)S(1)}, u32[]{:S(2)}, u32[]{:S(2)}) collective-permute-start(f32[1536,128]{1,0:T(8,128)S(1)} %shard_map.123.near), channel_id=1, source_target_pairs={{0,32},{32,0},{1,33},{33,1},{2,34},{34,2},{3,35},{35,3},{4,36},{36... | collective-permute-start | bytes 2359304 | tf_op jit(solution)/shard_map/ppermute | solution.py:484
  52.6 4.7 %collective-permute-start.1 = (f32[1536,128]{1,0:T(8,128)S(1)}, f32[1536,128]{1,0:T(8,128)S(1)}, u32[]{:S(2)}, u32[]{:S(2)}) collective-permute-start(f32[1536,128]{1,0:T(8,128)S(1)} %bitcast.13), channel_id=1, source_target_pairs={{0,32},{32,0},{1,33},{33,1},{2,34},{34,2},{3,35},{35,3},{4,36},{36... | collective-permute-start | bytes 2359304 | tf_op jit(solution)/shard_map/ppermute | solution.py:484
  57.5 1.6 %collective-permute-start.2 = (f32[8,128]{1,0:T(8,128)S(1)}, f32[8,128]{1,0:T(8,128)S(1)}, u32[]{:S(2)}, u32[]{:S(2)}) collective-permute-start(f32[8,128]{1,0:T(8,128)S(1)} %shard_map.126), channel_id=1, source_target_pairs={{0,32},{32,0},{1,33},{33,1},{2,34},{34,2},{3,35},{35,3},{4,36},{36... | collective-permute-start | bytes 12296 | tf_op jit(solution)/shard_map/ppermute | solution.py:484
  73.9 2.8 %collective-permute-start.3 = (f32[32,128]{1,0:T(8,128)S(1)}, f32[32,128]{1,0:T(8,128)S(1)}, u32[]{:S(2)}, u32[]{:S(2)}) collective-permute-start(f32[32,128]{1,0:T(8,128)S(1)} %shard_map.129.near), channel_id=1, source_target_pairs={{0,32},{32,0},{1,33},{33,1},{2,34},{34,2},{3,35},{35,3},{4,36},{36... | collective-permute-start | bytes 49160 | tf_op jit(solution)/shard_map/ppermute | solution.py:484

commit v7 on v6

--- a/solution.py
+++ b/solution.py
@@ -420,7 +420,9 @@
     second = jnp.concatenate([even[0:1], odd[0:1], even[1:2], odd[1:2]], axis=0)
     diag_first = 1.0 + g01
     below_sq = g11 - g01 * g01
-    inverse = 1.0 / below_sq
+    full = below_sq > 0.0
+    below_sq = jnp.where(full, below_sq, 0.0)
+    inverse = 1.0 / jnp.where(full, below_sq, 1.0)
     upper = g02 - g01 * g01
     shift = g12 - g01 * (g11 + g02 - g01 * g01)
     norm_sq = g22 - g01 * (2.0 * g12 - g01 * g11)
@@ -428,9 +430,11 @@
     gram_first = diag_first * diag_first + below_sq
     gram_second = (below_sq + 2.0 * shift + norm_sq) * inverse
     cross_scaled = cross * inverse
-    determinant = gram_first * gram_second - cross * cross_scaled
+    determinant = jnp.where(full, gram_first * gram_second - cross * cross_scaled, 1.0)
     for_image = (upper - diag_first * (1.0 + shift * inverse)) / determinant
     for_base = (diag_first * gram_second - upper * cross_scaled) / determinant - for_image * g01
+    for_image = jnp.where(full, for_image, 0.0)
+    for_base = jnp.where(full, for_base, diag_first / gram_first)
     below_first = jnp.sqrt(below_sq)
     shift_second = shift * inverse
     diag_second = 1.0 + shift_second
@@ -474,7 +478,7 @@
         in_specs=[pl.BlockSpec(memory_space=spaces.get(i, pltpu.VMEM)) for i in range(len(operands))],
         out_specs=[pl.BlockSpec(memory_space=out_spaces.get(i, pltpu.VMEM)) for i in range(len(outs))],
         scratch_shapes=list(scratch),
-        compiler_params=pltpu.CompilerParams(vmem_limit_bytes=16 * 1024 * 1024),
+        compiler_params=pltpu.CompilerParams(vmem_limit_bytes=8 * 1024 * 1024),
         cost_estimate=cost,
         input_output_aliases=aliases or {},
     )(*operands)

time: 78.7 us -> 78.7 us (level)
  no operation moved by 1% of the time
where the time goes in v7:
time: 78.7 us; the launch traced here: 78.3 us
  blocking collectives  33 us (42%)
  starting transfers between devices  19.9 us (25%)
  waiting for transfers between devices  11.7 us (15%)
  Pallas kernels  9.56 us (12%)
  local copies, waits for them, and re-layouts  3.35 us (4%)
  between operations  0.79 us (1%)
    all_to_all x2, blocking collectives, spread_far(): return lax.all_to_all(parts, FAR_AXES, 0, 0).reshape(lines.shape)  33 us
    all_to_all x1, starting transfers between devices, spread_far(): return lax.all_to_all(parts, FAR_AXES, 0, 0).reshape(lines.shape)  12 us
    pallas_call x10, Pallas kernels, call(): pl.pallas_call(body, out_shape=[jax.ShapeDtypeStruct(shape, kind) for sha...  9.56 us
    all_to_all x1, waiting for transfers between devices, spread_far(): return lax.all_to_all(parts, FAR_AXES, 0, 0).reshape(lines.shape)  8.21 us
    ppermute x4, starting transfers between devices, swap_cores(): return lax.ppermute(array, 'co', [(0, 1), (1, 0)])  7.97 us
    ppermute x4, waiting for transfers between devices, swap_cores(): return lax.ppermute(array, 'co', [(0, 1), (1, 0)])  3.44 us
    unnamed x22, local copies, waits for them, and re-layouts  2.97 us
  transfers between devices with their start and end apart: 5, of which 4 were waited for; matrix products, arithmetic and copies ran while one was open for 0% of the time, Pallas kernels for 6%

profile of v7, /device:TPU:1, one launch (start us, length us, event | category | flops | bytes accessed | tf_op | source)
XLA Modules:
  0.0 78.3 jit_solution(8259581759550425582)
XLA Ops:
  0.6 0.7 copy-done
  1.4 1.0 %shard_map.121 = f32[1536,128]{1,0:T(8,128)} custom-call(f32[6,480]{1,0:T(8,128)S(1)} %copy-done), custom_call_target="tpu_custom_call" | custom-call | tf_op jit(solution)/shard_map/pallas_call | solution.py:475
  2.4 12.0 %all-to-all-start = ((f32[64,24,128]{2,1,0:T(8,128)}), f32[64,24,128]{2,1,0:T(8,128)S(1)}, u32[]{:S(2)}, u32[]{:S(2)}) async-start(f32[64,24,128]{2,1,0:T(8,128)} %bitcast), calls=%async_computation | async-start | bytes 1572864 | tf_op jit(solution)/shard_map/all_to_all | solution.py:493
  14.6 0.1 reshape.37
  14.8 1.2 %copy-done.2 = bf16[2,480,480]{2,1,0:T(8,128)(2,1)S(1)} copy-done((bf16[2,480,480]{2,1,0:T(8,128)(2,1)S(1)}, bf16[2,480,480]{2,1,0:T(8,128)(2,1)}, u32[]{:S(2)}) %copy-start.2) | copy-done | bytes 921624
  16.0 1.0 %copy-done.3 = bf16[480,480]{1,0:T(8,128)(2,1)S(1)} copy-done((bf16[480,480]{1,0:T(8,128)(2,1)S(1)}, bf16[480,480]{1,0:T(8,128)(2,1)}, u32[]{:S(2)}) %copy-start.3) | copy-done | bytes 460824
  17.0 2.6 %shard_map.122 = (bf16[656,768]{1,0:T(8,128)(2,1)S(1)}, bf16[2,512,512]{2,1,0:T(8,128)(2,1)S(1)}, bf16[512,256]{1,0:T(8,128)(2,1)S(1)}, f32[4,256]{1,0:T(4,128)S...) custom-call(s32[1,768]{1,0:T(1,128)S(1)} %reshape.36.site, ...), custom_call_target="tpu_custom_call" | custom-call | flops 8000000000 | bytes 8000000 | tf_op jit(solution)/shard_map/pallas_call | solution.py:475
  19.7 8.2 %all-to-all-done = f32[64,24,128]{2,1,0:T(8,128)S(1)} async-done(((f32[64,24,128]{2,1,0:T(8,128)}), f32[64,24,128]{2,1,0:T(8,128)S(1)}, u32[]{:S(2)}, u32[]{:S(2)}) %all-to-all-start) | async-done | bytes 786464 | tf_op jit(solution)/shard_map/all_to_all | solution.py:493
  27.9 2.9 %collective-permute-start = (f32[1536,128]{1,0:T(8,128)S(1)}, f32[1536,128]{1,0:T(8,128)S(1)}, u32[]{:S(2)}, u32[]{:S(2)}) collective-permute-start(f32[1536,128]{1,0:T(8,128)S(1)} %shard_map.123.near), channel_id=1, source_target_pairs={{0,32},{32,0},{1,33},{33,1},{2,34},{34,2},{3,35},{35,3},{4,36},{36... | collective-permute-start | bytes 2359304 | tf_op jit(solution)/shard_map/ppermute | solution.py:488
  30.8 0.5 shard_map.124
  31.3 1.4 %collective-permute-done.peer = f32[1536,128]{1,0:T(8,128)S(1)} collective-permute-done((f32[1536,128]{1,0:T(8,128)S(1)}, f32[1536,128]{1,0:T(8,128)S(1)}, u32[]{:S(2)}, u32[]{:S(2)}) %collective-permute-start) | collective-permute-done | bytes 786464 | tf_op jit(solution)/shard_map/ppermute | solution.py:488
  32.7 1.3 %shard_map.125 = (f32[1536,128]{1,0:T(8,128)S(1)}, f32[8,512]{1,0:T(8,128)S(1)}) custom-call(f32[656,512]{1,0:T(8,128)S(1)} %get-tuple-element.20.near_sums, f32[2,512]{1,0:T(2,128)S(1)} %get-tuple-element.21.near_totals, f32[1536,128]{1,0:T(8,128)S(1)} %collective-permute-done.peer, bf16[656,768]{1,0:T(8,128)(2,1)S(1)} %get-tuple-element.19.pairs, ...), custom_call_target="tpu_custom_call" | custom-call | tf_op jit(solution)/shard_map/pallas_call | solution.py:475
  34.0 18.6 %all_to_all.15 = f32[64,24,128]{2,1,0:T(8,128)S(1)} all-to-all(f32[64,24,128]{2,1,0:T(8,128)S(1)} %bitcast.16), channel_id=1, replica_groups=mesh['xl'=2,'co'=2,'z'=4,'xh'=2,'y'=4] {'xl','z','xh','y'}, dimensions={0} | all-to-all | bytes 1572864 | tf_op jit(solution)/shard_map/all_to_all | solution.py:493
  52.6 2.8 %collective-permute-start.1 = (f32[1536,128]{1,0:T(8,128)S(1)}, f32[1536,128]{1,0:T(8,128)S(1)}, u32[]{:S(2)}, u32[]{:S(2)}) collective-permute-start(f32[1536,128]{1,0:T(8,128)S(1)} %bitcast.13), channel_id=1, source_target_pairs={{0,32},{32,0},{1,33},{33,1},{2,34},{34,2},{3,35},{35,3},{4,36},{36... | collective-permute-start | bytes 2359304 | tf_op jit(solution)/shard_map/ppermute | solution.py:488
  55.3 0.7 shard_map.127
  56.0 1.2 %collective-permute-done.1.peer = f32[1536,128]{1,0:T(8,128)S(1)} collective-permute-done((f32[1536,128]{1,0:T(8,128)S(1)}, f32[1536,128]{1,0:T(8,128)S(1)}, u32[]{:S(2)}, u32[]{:S(2)}) %collective-permute-start.1) | collective-permute-done | bytes 786464 | tf_op jit(solution)/shard_map/ppermute | solution.py:488
  57.2 0.3 shard_map.126
  57.5 0.4 collective-permute-start.2
  57.9 1.2 %shard_map.128 = (f32[8,128]{1,0:T(8,128)S(1)}, bf16[656,128]{1,0:T(8,128)(2,1)S(1)}) custom-call(f32[1536,128]{1,0:T(8,128)S(1)} %bitcast.15, f32[656,512]{1,0:T(8,128)S(1)} %get-tuple-element.29.near_sums, f32[2,512]{1,0:T(2,128)S(1)} %get-tuple-element.30.near_gradient, f32[1536,128]{1,0:T(8,128)S(1)} %collective-permute-done.1.peer, ...), custom_call_target="tpu_custom_call" | custom-call | flops 8000000000 | bytes 4000000 | tf_op jit(solution)/shard_map/pallas_call | solution.py:475
  59.2 14.5 %all_to_all.16 = f32[64,8,128]{2,1,0:T(8,128)S(1)} all-to-all(f32[64,8,128]{2,1,0:T(8,128)S(1)} %broadcast_in_dim.2), channel_id=1, replica_groups=mesh['xl'=2,'co'=2,'z'=4,'xh'=2,'y'=4] {'xl','z','xh','y'}, dimensions={0} | all-to-all | bytes 524288 | tf_op jit(solution)/shard_map/all_to_all | solution.py:493
  73.6 0.2 shard_map.129.near
  73.9 1.9 %collective-permute-start.3 = (f32[32,128]{1,0:T(8,128)S(1)}, f32[32,128]{1,0:T(8,128)S(1)}, u32[]{:S(2)}, u32[]{:S(2)}) collective-permute-start(f32[32,128]{1,0:T(8,128)S(1)} %shard_map.129.near), channel_id=1, source_target_pairs={{0,32},{32,0},{1,33},{33,1},{2,34},{34,2},{3,35},{35,3},{4,36},{36... | collective-permute-start | bytes 49160 | tf_op jit(solution)/shard_map/ppermute | solution.py:488
  75.8 0.8 %collective-permute-done.3.peer = f32[32,128]{1,0:T(8,128)S(1)} collective-permute-done((f32[32,128]{1,0:T(8,128)S(1)}, f32[32,128]{1,0:T(8,128)S(1)}, u32[]{:S(2)}, u32[]{:S(2)}) %collective-permute-start.3) | collective-permute-done | bytes 16416 | tf_op jit(solution)/shard_map/ppermute | solution.py:488
  76.6 1.7 %shard_map.130 = (f32[6,480]{1,0:T(8,128)}, f32[6,480]{1,0:T(8,128)}, f32[4]{0:T(128)}) custom-call(f32[32,128]{1,0:T(8,128)S(1)} %shard_map.129.near, f32[32,128]{1,0:T(8,128)S(1)} %collective-permute-done.3.peer, bf16[656,128]{1,0:T(8,128)(2,1)S(1)} %get-tuple-element.34.weights, bf16[2,512,512]{2,1,0:T(8,128)(2,1)S(1)} %get-tuple-element.22.tables, ...), custom_call_target="tpu_custom_call" | custom-call | tf_op jit(solution)/shard_map/pallas_call | solution.py:475
  (28 shorter events, 0.3 us)
Async XLA Ops:
  0.6 0.7 copy-start
  1.4 13.0 %copy-start.10 = (s32[768]{0:T(1024)S(1)}, s32[768]{0:T(1024)}, u32[]{:S(2)}) copy-start(s32[768]{0:T(1024)} %param.11) | copy-start | bytes 9220
  1.4 13.2 %copy-start.9 = (f32[3,768]{1,0:T(4,128)S(1)}, f32[3,768]{1,0:T(4,128)}, u32[]{:S(2)}) copy-start(f32[3,768]{1,0:T(4,128)} %param.12) | copy-start | bytes 27652
  1.4 13.4 %copy-start.1 = (f32[6,480]{1,0:T(8,128)S(1)}, f32[6,480]{1,0:T(8,128)}, u32[]{:S(2)}) copy-start(f32[6,480]{1,0:T(8,128)} %incident.5) | copy-start | bytes 34564
  1.4 13.4 %copy-start.4 = (bf16[256,480]{0,1:T(8,128)(2,1)S(1)}, bf16[256,480]{0,1:T(8,128)(2,1)}, u32[]{:S(2)}) copy-start(bf16[256,480]{0,1:T(8,128)(2,1)} %param.17) | copy-start | bytes 737284
  1.4 13.4 %copy-start.5 = (f32[2,240]{1,0:T(2,128)S(1)}, f32[2,240]{1,0:T(2,128)}, u32[]{:S(2)}) copy-start(f32[2,240]{1,0:T(2,128)} %tmat.1) | copy-start | bytes 5764
  1.4 13.4 %copy-start.6 = (s32[256]{0:T(256)S(1)}, s32[256]{0:T(256)}, u32[]{:S(2)}) copy-start(s32[256]{0:T(256)} %param.18) | copy-start | bytes 3076
  1.4 13.4 %copy-start.7 = (f32[6]{0:T(128)S(1)}, f32[6]{0:T(128)}, u32[]{:S(2)}) copy-start(f32[6]{0:T(128)} %radius.1) | copy-start | bytes 76
  1.4 13.4 %copy-start.8 = (s32[1,256]{1,0:T(1,128)S(1)}, s32[1,256]{1,0:T(1,128)}, u32[]{:S(2)}) copy-start(s32[1,256]{1,0:T(1,128)} %constant.2.clone.orders) | copy-start | bytes 3076
  2.4 25.5 %all-to-all-start = ((f32[64,24,128]{2,1,0:T(8,128)}), f32[64,24,128]{2,1,0:T(8,128)S(1)}, u32[]{:S(2)}, u32[]{:S(2)}) async-start(f32[64,24,128]{2,1,0:T(8,128)} %bitcast), calls=%async_computation | async-start | bytes 1572864 | tf_op jit(solution)/shard_map/all_to_all | solution.py:493
  14.8 1.2 %copy-start.2 = (bf16[2,480,480]{2,1,0:T(8,128)(2,1)S(1)}, bf16[2,480,480]{2,1,0:T(8,128)(2,1)}, u32[]{:S(2)}) copy-start(bf16[2,480,480]{2,1,0:T(8,128)(2,1)} %axial.1) | copy-start | bytes 2764804
  16.0 1.0 %copy-start.3 = (bf16[480,480]{1,0:T(8,128)(2,1)S(1)}, bf16[480,480]{1,0:T(8,128)(2,1)}, u32[]{:S(2)}) copy-start(bf16[480,480]{1,0:T(8,128)(2,1)} %rotation.1) | copy-start | bytes 1382404
  27.9 4.8 %collective-permute-start = (f32[1536,128]{1,0:T(8,128)S(1)}, f32[1536,128]{1,0:T(8,128)S(1)}, u32[]{:S(2)}, u32[]{:S(2)}) collective-permute-start(f32[1536,128]{1,0:T(8,128)S(1)} %shard_map.123.near), channel_id=1, source_target_pairs={{0,32},{32,0},{1,33},{33,1},{2,34},{34,2},{3,35},{35,3},{4,36},{36... | collective-permute-start | bytes 2359304 | tf_op jit(solution)/shard_map/ppermute | solution.py:488
  52.6 4.7 %collective-permute-start.1 = (f32[1536,128]{1,0:T(8,128)S(1)}, f32[1536,128]{1,0:T(8,128)S(1)}, u32[]{:S(2)}, u32[]{:S(2)}) collective-permute-start(f32[1536,128]{1,0:T(8,128)S(1)} %bitcast.13), channel_id=1, source_target_pairs={{0,32},{32,0},{1,33},{33,1},{2,34},{34,2},{3,35},{35,3},{4,36},{36... | collective-permute-start | bytes 2359304 | tf_op jit(solution)/shard_map/ppermute | solution.py:488
  57.5 1.6 %collective-permute-start.2 = (f32[8,128]{1,0:T(8,128)S(1)}, f32[8,128]{1,0:T(8,128)S(1)}, u32[]{:S(2)}, u32[]{:S(2)}) collective-permute-start(f32[8,128]{1,0:T(8,128)S(1)} %shard_map.126), channel_id=1, source_target_pairs={{0,32},{32,0},{1,33},{33,1},{2,34},{34,2},{3,35},{35,3},{4,36},{36... | collective-permute-start | bytes 12296 | tf_op jit(solution)/shard_map/ppermute | solution.py:488
  73.9 2.8 %collective-permute-start.3 = (f32[32,128]{1,0:T(8,128)S(1)}, f32[32,128]{1,0:T(8,128)S(1)}, u32[]{:S(2)}, u32[]{:S(2)}) collective-permute-start(f32[32,128]{1,0:T(8,128)S(1)} %shard_map.129.near), channel_id=1, source_target_pairs={{0,32},{32,0},{1,33},{33,1},{2,34},{34,2},{3,35},{35,3},{4,36},{36... | collective-permute-start | bytes 49160 | tf_op jit(solution)/shard_map/ppermute | solution.py:488

commit v8 on v7

--- a/solution.py
+++ b/solution.py
@@ -12,6 +12,7 @@
 LATTICE_STEP = 2.5
 
 SPHERES = 768
+HALF_SPHERES = SPHERES // 2
 COEFF = 480
 HALF = 240
 GROUPS = 4
@@ -117,7 +118,7 @@
     core = lax.axis_index("co")
 
     def own_core_first(place):
-        other = jnp.concatenate([place[:, SPHERES // 2 :], place[:, : SPHERES // 2]], axis=1)
+        other = jnp.concatenate([place[:, HALF_SPHERES :], place[:, : HALF_SPHERES]], axis=1)
         return jnp.where(core == 0, place, other)
 
     place_x = own_core_first((sites & 7).astype(F32) * LATTICE_STEP + jitter[0:1, :])
@@ -126,12 +127,16 @@
     lane = lax.broadcasted_iota(jnp.int32, (ROWS, SPHERES), 1)
     line = lax.broadcasted_iota(jnp.int32, (ROWS, SPHERES), 0)
     same = lane == line + own
+    same_peer = lane == line + own + HALF_SPHERES
 
     def offset(place):
         here = jnp.sum(jnp.where(same, place, 0.0), axis=1, keepdims=True)
-        return here - place
+        peer = jnp.sum(jnp.where(same_peer, place, 0.0), axis=1, keepdims=True)
+        return jnp.concatenate([here - place, peer - place[:, :HALF_SPHERES]], axis=1)
 
     dx, dy, dz = offset(place_x), offset(place_y), offset(place_z)
+    line = lax.broadcasted_iota(jnp.int32, dx.shape, 0)
+    same = lax.broadcasted_iota(jnp.int32, dx.shape, 1) == line + own
     distance = jnp.sqrt(jnp.where(same, 1.0, dx * dx + dy * dy + dz * dz))
     phase = WAVENUMBER * distance
     none = same | (line >= OWN)
@@ -178,7 +183,7 @@
 
 
 def load_rows(lines):
-    parts = [lines[pl.ds(part, SPHERES // 2, stride=4), :].astype(BF) for part in range(4)]
+    parts = [lines[pl.ds(part, HALF_SPHERES, stride=4), :].astype(BF) for part in range(4)]
     return jnp.concatenate(parts, axis=1)
 
 
@@ -199,22 +204,36 @@
     return jnp.concatenate([first[0:1], second[0:1], first[1:2], second[1:2]], axis=0)
 
 
-def order_body(near_in, pairs, near_out):
-    del near_in, pairs, near_out
-
-
-def first_near_body(near, pairs, sums_out, totals_out):
-    sums_out[...] = dot(pairs[:, : SPHERES // 2], load_rows(near))
-    totals_out[...] = half_sums(near)
+def order_body(near_in, pairs, tables, near_out):
+    del near_in, pairs, tables, near_out
+
+
+def own_field(near, pairs, tables, orders, sums, shifted):
+    sums[...] = dot(pairs[:, :HALF_SPHERES], load_rows(near))
+    return mix(sums, shifted, tables, orders)
+
+
+def peer_field(near, pairs, tables, orders, sums, shifted):
+    sums[...] = dot(pairs[:, SPHERES:], load_rows(near))
+    return mix(sums, shifted, tables, orders)
+
+
+def first_peer_body(near, pairs, tables, orders, field_out, sums, shifted):
+    field = peer_field(near, pairs, tables, orders, sums, shifted)
+    field_out[...] = jnp.concatenate([field[:OWN], half_sums(near)], axis=0)
+
+
+def first_own_body(near, pairs, tables, orders, probes, seen, field_out, gradient_out, sums, shifted):
+    field_out[...] = own_field(near, pairs, tables, orders, sums, shifted)
+    gradient_out[...] = half_gradient(half_sums(near), probes, seen, lax.axis_index("co"))
 
 
 def second_near_body(near, pairs, probes, seen, sums_out, gradient_out):
-    sums_out[...] = dot(pairs[:, : SPHERES // 2], load_rows(near))
-    gradient_out[...] = half_gradient(near, probes, seen, lax.axis_index("co"))
-
-
-def half_gradient(lines, probes, seen, core):
-    totals = half_sums(lines)
+    sums_out[...] = dot(pairs[:, :HALF_SPHERES], load_rows(near))
+    gradient_out[...] = half_gradient(half_sums(near), probes, seen, lax.axis_index("co"))
+
+
+def half_gradient(totals, probes, seen, core):
     lane = lax.broadcasted_iota(jnp.int32, totals.shape, 1)
     totals = jnp.where((lane & (WIDE - 1)) < HALF, totals, 0.0)
     first, second = seen[0:2, :], seen[2:4, :]
@@ -301,13 +320,12 @@
 
 
 def first_body(
-    near_sums, near_totals, peer, pairs, tables, tmat, radius, orders, probes, seen,
-    chunk, rows_out, sums, shifted, lines,
+    field, received, near_gradient, tmat, radius, probes, seen,
+    chunk, rows_out, lines,
 ):
-    sums[...] = near_sums[...] + dot(pairs[:, SPHERES // 2 :], load_rows(peer))
-    gradient = gradient_of(all_groups(near_totals[...], half_sums(peer)), probes, seen[...])
-    field = mix(sums, shifted, tables, orders)
-    image = scatter(field, tmat, radius[...])
+    peer_gradient = half_gradient(received[OWN:, :], probes, seen, 1 - lax.axis_index("co"))
+    gradient = all_groups(near_gradient[...], peer_gradient)
+    image = scatter(field[...] + received[...], tmat, radius[...])
     rows_out[...] = image
     lane = lax.broadcasted_iota(jnp.int32, (ROWS, FULL), 1)
     marked = jnp.where(lane == PAD + own_group(), jnp.concatenate([radius[...]] * 4, axis=1), image)
@@ -359,14 +377,14 @@
 
 
 def second_gradient_body(peer, probes, seen, send):
-    send[...] = to_lines(half_gradient(peer, probes, seen, 1 - lax.axis_index("co")))
+    send[...] = to_lines(half_gradient(half_sums(peer), probes, seen, 1 - lax.axis_index("co")))
 
 
 def second_body(
     near, near_sums, near_gradient, peer, pairs, tables, tmat, radius, orders, base, image,
     extra, weights_out, sums, shifted,
 ):
-    sums[...] = near_sums[...] + dot(pairs[:, SPHERES // 2 :], load_rows(peer))
+    sums[...] = near_sums[...] + dot(pairs[:, HALF_SPHERES:SPHERES], load_rows(peer))
     for block in range(BLOCKS):
         k = block if block <= TOP else block - TOP
         at = pl.ds(block * BLOCK, BLOCK)
@@ -521,7 +539,7 @@
     pairs, tables, probes, seen, tmat, orders, base, radius = call(
         prepare_body,
         [
-            ((BLOCKS * BLOCK, SPHERES), BF),
+            ((BLOCKS * BLOCK, SPHERES + HALF_SPHERES), BF),
             ((2, FULL, FULL), BF),
             ((FULL, PROBES_OWN), BF),
             ((GROUPS, PROBES_OWN), F32),
@@ -546,27 +564,38 @@
         cost=pl.CostEstimate(flops=8_000_000_000, bytes_accessed=8_000_000, transcendentals=20_000),
     )
 
+    scratch = [sum_scratch, shift_scratch]
+    half_shape = ((2, FULL), F32)
+
     near = spread_far(chunk)
-    (near,) = call(order_body, [chunk_shape], operands=(near, pairs), spaces={1: pl.ANY}, aliases={0: 0})
-    sums_shape = ((BLOCKS * BLOCK, FULL), F32)
-    near_sums, near_totals = call(
-        first_near_body,
-        [sums_shape, ((2, FULL), F32)],
-        operands=(near, pairs),
+    (near,) = call(
+        order_body,
+        [chunk_shape],
+        operands=(near, pairs, tables),
+        spaces={1: pl.ANY, 2: pl.ANY},
+        aliases={0: 0},
+    )
+    (field_peer,) = call(first_peer_body, [rows_shape], scratch, (near, pairs, tables, orders), cost=half_cost)
+    field_received = swap_cores(field_peer)
+    field, near_gradient = call(
+        first_own_body,
+        [rows_shape, half_shape],
+        scratch,
+        (near, pairs, tables, orders, probes, seen),
         cost=half_cost,
     )
     chunk, image = call(
         first_body,
         [chunk_shape, rows_shape],
-        [sum_scratch, shift_scratch, line_scratch],
-        (near_sums, near_totals, swap_cores(near), pairs, tables, tmat, radius, orders, probes, seen),
+        [line_scratch],
+        (field, field_received, near_gradient, tmat, radius, probes, seen),
     )
 
     near = spread_far(chunk)
     peer = swap_cores(near)
     near_sums, near_gradient = call(
         second_near_body,
-        [sums_shape, ((2, FULL), F32)],
+        [((BLOCKS * BLOCK, FULL), F32), half_shape],
         operands=(near, pairs, probes, seen),
         cost=half_cost,
     )
@@ -586,7 +615,7 @@
     solution_rows, sensitivity_rows, arnoldi = call(
         finish_body,
         [((OWN, COEFF), F32), ((OWN, COEFF), F32), ((4,), F32)],
-        [pltpu.VMEM((LANES, FULL), F32), sum_scratch, shift_scratch],
+        [pltpu.VMEM((LANES, FULL), F32)] + scratch,
         (near, peer, weights, tables, tmat, orders, incident, image),
         out_spaces={2: pltpu.SMEM},
     )

time: 78.7 us -> 78.6 us (level)
  waiting for transfers between devices: 11.7 us -> 8.52 us
  local copies, waits for them, and re-layouts: 3.35 us -> 4.98 us
  Pallas kernels: 9.56 us -> 10.8 us
  blocking collectives: 33 us -> 33.9 us
    all_to_all x1, waiting for transfers between devices: 8.21 us -> 6.47 us  [spread_far(): return lax.all_to_all(parts, FAR_AXES, 0, 0).reshape(lines.shape)]
    unnamed x22 -> x26, local copies, waits for them, and re-layouts: 2.97 us -> 4.61 us
    ppermute x4, waiting for transfers between devices: 3.44 us -> 2.05 us  [swap_cores(): return lax.ppermute(array, 'co', [(0, 1), (1, 0)])]
    pallas_call x10 -> x11, Pallas kernels: 9.56 us -> 10.8 us  [call(): pl.pallas_call(body, out_shape=[jax.ShapeDtypeStruct(shape, kind) for sha...]
    all_to_all x2, blocking collectives: 33 us -> 33.9 us  [spread_far(): return lax.all_to_all(parts, FAR_AXES, 0, 0).reshape(lines.shape)]
  transfers between devices with their start and end apart: 5 -> 5, of which waited for: 4 -> 3; matrix products, arithmetic and copies ran while one was open for 0% -> 0% of each run, Pallas kernels for 6% -> 8%
where the time goes in v8:
time: 78.6 us; the launch traced here: 78.1 us
  blocking collectives  33.9 us (43%)
  starting transfers between devices  19.2 us (24%)
  Pallas kernels  10.8 us (14%)
  waiting for transfers between devices  8.52 us (11%)
  local copies, waits for them, and re-layouts  4.98 us (6%)
  between operations  0.79 us (1%)
    all_to_all x2, blocking collectives, spread_far(): return lax.all_to_all(parts, FAR_AXES, 0, 0).reshape(lines.shape)  33.9 us
    all_to_all x1, starting transfers between devices, spread_far(): return lax.all_to_all(parts, FAR_AXES, 0, 0).reshape(lines.shape)  12 us
    pallas_call x11, Pallas kernels, call(): pl.pallas_call(body, out_shape=[jax.ShapeDtypeStruct(shape, kind) for sha...  10.8 us
    ppermute x4, starting transfers between devices, swap_cores(): return lax.ppermute(array, 'co', [(0, 1), (1, 0)])  7.2 us
    all_to_all x1, waiting for transfers between devices, spread_far(): return lax.all_to_all(parts, FAR_AXES, 0, 0).reshape(lines.shape)  6.47 us
    unnamed x26, local copies, waits for them, and re-layouts  4.61 us
    ppermute x4, waiting for transfers between devices, swap_cores(): return lax.ppermute(array, 'co', [(0, 1), (1, 0)])  2.05 us
  transfers between devices with their start and end apart: 5, of which 3 were waited for; matrix products, arithmetic and copies ran while one was open for 0% of the time, Pallas kernels for 8%

profile of v8, /device:TPU:1, one launch (start us, length us, event | category | flops | bytes accessed | tf_op | source)
XLA Modules:
  0.0 78.1 jit_solution(13741886104928166017)
XLA Ops:
  0.6 0.7 copy-done.2
  1.4 1.0 %shard_map.121 = f32[1536,128]{1,0:T(8,128)} custom-call(f32[6,480]{1,0:T(8,128)S(1)} %copy-done.2), custom_call_target="tpu_custom_call" | custom-call | tf_op jit(solution)/shard_map/pallas_call | solution.py:493
  2.4 12.0 %all-to-all-start = ((f32[64,24,128]{2,1,0:T(8,128)}), f32[64,24,128]{2,1,0:T(8,128)S(1)}, u32[]{:S(2)}, u32[]{:S(2)}) async-start(f32[64,24,128]{2,1,0:T(8,128)} %bitcast), calls=%async_computation | async-start | bytes 1572864 | tf_op jit(solution)/shard_map/all_to_all | solution.py:511
  14.8 1.2 %copy-done.4 = bf16[2,480,480]{2,1,0:T(8,128)(2,1)S(1)} copy-done((bf16[2,480,480]{2,1,0:T(8,128)(2,1)S(1)}, bf16[2,480,480]{2,1,0:T(8,128)(2,1)}, u32[]{:S(2)}) %copy-start.4) | copy-done | bytes 921624
  16.0 1.0 %copy-done.5 = bf16[480,480]{1,0:T(8,128)(2,1)S(1)} copy-done((bf16[480,480]{1,0:T(8,128)(2,1)S(1)}, bf16[480,480]{1,0:T(8,128)(2,1)}, u32[]{:S(2)}) %copy-start.5) | copy-done | bytes 460824
  17.0 0.9 %copy-done.6 = bf16[256,480]{0,1:T(8,128)(2,1)S(1)} copy-done((bf16[256,480]{0,1:T(8,128)(2,1)S(1)}, bf16[256,480]{0,1:T(8,128)(2,1)}, u32[]{:S(2)}) %copy-start.6) | copy-done | bytes 245784
  18.0 2.7 %shard_map.122 = (bf16[656,1152]{1,0:T(8,128)(2,1)S(1)}, bf16[2,512,512]{2,1,0:T(8,128)(2,1)S(1)}, bf16[512,256]{1,0:T(8,128)(2,1)S(1)}, f32[4,256]{1,0:T(4,128)...) custom-call(s32[1,768]{1,0:T(1,128)S(1)} %reshape.36.site, ...), custom_call_target="tpu_custom_call" | custom-call | flops 8000000000 | bytes 8000000 | tf_op jit(solution)/shard_map/pallas_call | solution.py:493
  20.7 0.7 copy-done
  21.4 6.5 %all-to-all-done = f32[64,24,128]{2,1,0:T(8,128)S(1)} async-done(((f32[64,24,128]{2,1,0:T(8,128)}), f32[64,24,128]{2,1,0:T(8,128)S(1)}, u32[]{:S(2)}, u32[]{:S(2)}) %all-to-all-start) | async-done | bytes 786464 | tf_op jit(solution)/shard_map/all_to_all | solution.py:511
  27.9 1.0 %shard_map.125 = f32[8,512]{1,0:T(8,128)S(1)} custom-call(f32[1536,128]{1,0:T(8,128)S(1)} %shard_map.123.near, bf16[656,1152]{1,0:T(8,128)(2,1)S(1)} %get-tuple-element.19.pairs, bf16[2,512,512]{2,1,0:T(8,128)(2,1)S(1)} %get-tuple-element.20.tables, s32[8,256]{1,0:T(8,128)S(1)} %get-tuple-element.21.orders), custom_call_target="tpu_custom_call" | custom-call | flops 8000000000 | bytes 4000000 | tf_op jit(solution)/shard_map/pallas_call | solution.py:493
  28.9 3.0 %collective-permute-start = (f32[8,512]{1,0:T(8,128)S(1)}, f32[8,512]{1,0:T(8,128)S(1)}, u32[]{:S(2)}, u32[]{:S(2)}) collective-permute-start(f32[8,512]{1,0:T(8,128)S(1)} %shard_map.125), channel_id=1, source_target_pairs={{0,32},{32,0},{1,33},{33,1},{2,34},{34,2},{3,35},{35,3},{4,36},{36... | collective-permute-start | bytes 49160 | tf_op jit(solution)/shard_map/ppermute | solution.py:506
  31.9 1.3 %shard_map.124 = (f32[8,512]{1,0:T(8,128)S(1)}, f32[2,512]{1,0:T(2,128)S(1)}) custom-call(f32[1536,128]{1,0:T(8,128)S(1)} %shard_map.123.near, bf16[656,1152]{1,0:T(8,128)(2,1)S(1)} %get-tuple-element.19.pairs, bf16[2,512,512]{2,1,0:T(8,128)(2,1)S(1)} %get-tuple-element.20.tables, s32[8,256]{1,0:T(8,128)S(1)} %get-tuple-element.21.orders, ...), custom_call_target="tpu_custom_call" | custom-call | flops 8000000000 | bytes 4000000 | tf_op jit(solution)/shard_map/pallas_call | solution.py:493
  33.2 0.6 shard_map.126
  33.8 19.2 %all_to_all.15 = f32[64,24,128]{2,1,0:T(8,128)S(1)} all-to-all(f32[64,24,128]{2,1,0:T(8,128)S(1)} %bitcast.16), channel_id=1, replica_groups=mesh['xl'=2,'co'=2,'z'=4,'xh'=2,'y'=4] {'xl','z','xh','y'}, dimensions={0} | all-to-all | bytes 1572864 | tf_op jit(solution)/shard_map/all_to_all | solution.py:511
  53.0 1.9 %collective-permute-start.1 = (f32[1536,128]{1,0:T(8,128)S(1)}, f32[1536,128]{1,0:T(8,128)S(1)}, u32[]{:S(2)}, u32[]{:S(2)}) collective-permute-start(f32[1536,128]{1,0:T(8,128)S(1)} %bitcast.13), channel_id=1, source_target_pairs={{0,32},{32,0},{1,33},{33,1},{2,34},{34,2},{3,35},{35,3},{4,36},{36... | collective-permute-start | bytes 2359304 | tf_op jit(solution)/shard_map/ppermute | solution.py:506
  54.9 0.7 shard_map.128
  55.6 1.2 %collective-permute-done.1.peer = f32[1536,128]{1,0:T(8,128)S(1)} collective-permute-done((f32[1536,128]{1,0:T(8,128)S(1)}, f32[1536,128]{1,0:T(8,128)S(1)}, u32[]{:S(2)}, u32[]{:S(2)}) %collective-permute-start.1) | collective-permute-done | bytes 786464 | tf_op jit(solution)/shard_map/ppermute | solution.py:506
  56.8 0.3 shard_map.127
  57.1 0.4 collective-permute-start.2
  57.5 1.2 %shard_map.129 = (f32[8,128]{1,0:T(8,128)S(1)}, bf16[656,128]{1,0:T(8,128)(2,1)S(1)}) custom-call(f32[1536,128]{1,0:T(8,128)S(1)} %bitcast.15, f32[656,512]{1,0:T(8,128)S(1)} %get-tuple-element.29.near_sums, f32[2,512]{1,0:T(2,128)S(1)} %get-tuple-element.30.near_gradient, f32[1536,128]{1,0:T(8,128)S(1)} %collective-permute-done.1.peer, ...), custom_call_target="tpu_custom_call" | custom-call | flops 8000000000 | bytes 4000000 | tf_op jit(solution)/shard_map/pallas_call | solution.py:493
  58.8 14.7 %all_to_all.16 = f32[64,8,128]{2,1,0:T(8,128)S(1)} all-to-all(f32[64,8,128]{2,1,0:T(8,128)S(1)} %broadcast_in_dim.2), channel_id=1, replica_groups=mesh['xl'=2,'co'=2,'z'=4,'xh'=2,'y'=4] {'xl','z','xh','y'}, dimensions={0} | all-to-all | bytes 524288 | tf_op jit(solution)/shard_map/all_to_all | solution.py:511
  73.7 1.9 %collective-permute-start.3 = (f32[32,128]{1,0:T(8,128)S(1)}, f32[32,128]{1,0:T(8,128)S(1)}, u32[]{:S(2)}, u32[]{:S(2)}) collective-permute-start(f32[32,128]{1,0:T(8,128)S(1)} %shard_map.130.near), channel_id=1, source_target_pairs={{0,32},{32,0},{1,33},{33,1},{2,34},{34,2},{3,35},{35,3},{4,36},{36... | collective-permute-start | bytes 49160 | tf_op jit(solution)/shard_map/ppermute | solution.py:506
  75.6 0.8 %collective-permute-done.3.peer = f32[32,128]{1,0:T(8,128)S(1)} collective-permute-done((f32[32,128]{1,0:T(8,128)S(1)}, f32[32,128]{1,0:T(8,128)S(1)}, u32[]{:S(2)}, u32[]{:S(2)}) %collective-permute-start.3) | collective-permute-done | bytes 16416 | tf_op jit(solution)/shard_map/ppermute | solution.py:506
  76.5 1.7 %shard_map.131 = (f32[6,480]{1,0:T(8,128)}, f32[6,480]{1,0:T(8,128)}, f32[4]{0:T(128)}) custom-call(f32[32,128]{1,0:T(8,128)S(1)} %shard_map.130.near, f32[32,128]{1,0:T(8,128)S(1)} %collective-permute-done.3.peer, bf16[656,128]{1,0:T(8,128)(2,1)S(1)} %get-tuple-element.34.weights, bf16[2,512,512]{2,1,0:T(8,128)(2,1)S(1)} %get-tuple-element.20.tables, ...), custom_call_target="tpu_custom_call" | custom-call | tf_op jit(solution)/shard_map/pallas_call | solution.py:493
  (33 shorter events, 0.7 us)
Async XLA Ops:
  0.6 0.7 copy-start.2
  1.4 13.0 %copy-start.12 = (s32[768]{0:T(1024)S(1)}, s32[768]{0:T(1024)}, u32[]{:S(2)}) copy-start(s32[768]{0:T(1024)} %param.11) | copy-start | bytes 9220
  1.4 13.2 %copy-start.11 = (f32[3,768]{1,0:T(4,128)S(1)}, f32[3,768]{1,0:T(4,128)}, u32[]{:S(2)}) copy-start(f32[3,768]{1,0:T(4,128)} %param.12) | copy-start | bytes 27652
  1.4 13.4 %copy-start.3 = (f32[6,480]{1,0:T(8,128)S(1)}, f32[6,480]{1,0:T(8,128)}, u32[]{:S(2)}) copy-start(f32[6,480]{1,0:T(8,128)} %incident.5) | copy-start | bytes 34564
  1.4 13.4 %copy-start.7 = (f32[2,240]{1,0:T(2,128)S(1)}, f32[2,240]{1,0:T(2,128)}, u32[]{:S(2)}) copy-start(f32[2,240]{1,0:T(2,128)} %tmat.1) | copy-start | bytes 5764
  1.4 13.4 %copy-start.8 = (s32[256]{0:T(256)S(1)}, s32[256]{0:T(256)}, u32[]{:S(2)}) copy-start(s32[256]{0:T(256)} %param.18) | copy-start | bytes 3076
  1.4 13.4 %copy-start.9 = (f32[6]{0:T(128)S(1)}, f32[6]{0:T(128)}, u32[]{:S(2)}) copy-start(f32[6]{0:T(128)} %radius.1) | copy-start | bytes 76
  1.4 13.4 %copy-start.10 = (s32[1,256]{1,0:T(1,128)S(1)}, s32[1,256]{1,0:T(1,128)}, u32[]{:S(2)}) copy-start(s32[1,256]{1,0:T(1,128)} %constant.2.clone.orders) | copy-start | bytes 3076
  2.4 25.5 %all-to-all-start = ((f32[64,24,128]{2,1,0:T(8,128)}), f32[64,24,128]{2,1,0:T(8,128)S(1)}, u32[]{:S(2)}, u32[]{:S(2)}) async-start(f32[64,24,128]{2,1,0:T(8,128)} %bitcast), calls=%async_computation | async-start | bytes 1572864 | tf_op jit(solution)/shard_map/all_to_all | solution.py:511
  14.8 1.2 %copy-start.4 = (bf16[2,480,480]{2,1,0:T(8,128)(2,1)S(1)}, bf16[2,480,480]{2,1,0:T(8,128)(2,1)}, u32[]{:S(2)}) copy-start(bf16[2,480,480]{2,1,0:T(8,128)(2,1)} %axial.1) | copy-start | bytes 2764804
  16.0 1.0 %copy-start.5 = (bf16[480,480]{1,0:T(8,128)(2,1)S(1)}, bf16[480,480]{1,0:T(8,128)(2,1)}, u32[]{:S(2)}) copy-start(bf16[480,480]{1,0:T(8,128)(2,1)} %rotation.1) | copy-start | bytes 1382404
  17.0 0.9 %copy-start.6 = (bf16[256,480]{0,1:T(8,128)(2,1)S(1)}, bf16[256,480]{0,1:T(8,128)(2,1)}, u32[]{:S(2)}) copy-start(bf16[256,480]{0,1:T(8,128)(2,1)} %param.17) | copy-start | bytes 737284
  20.7 0.7 copy-start
  27.9 4.0 %copy-start.1 = (bf16[512,256]{1,0:T(8,128)(2,1)S(1)}, bf16[512,256]{1,0:T(8,128)(2,1)}, u32[]{:S(2)}) copy-start(bf16[512,256]{1,0:T(8,128)(2,1)} %copy-done) | copy-start | bytes 786436
  28.9 4.2 %collective-permute-start = (f32[8,512]{1,0:T(8,128)S(1)}, f32[8,512]{1,0:T(8,128)S(1)}, u32[]{:S(2)}, u32[]{:S(2)}) collective-permute-start(f32[8,512]{1,0:T(8,128)S(1)} %shard_map.125), channel_id=1, source_target_pairs={{0,32},{32,0},{1,33},{33,1},{2,34},{34,2},{3,35},{35,3},{4,36},{36... | collective-permute-start | bytes 49160 | tf_op jit(solution)/shard_map/ppermute | solution.py:506
  53.0 3.8 %collective-permute-start.1 = (f32[1536,128]{1,0:T(8,128)S(1)}, f32[1536,128]{1,0:T(8,128)S(1)}, u32[]{:S(2)}, u32[]{:S(2)}) collective-permute-start(f32[1536,128]{1,0:T(8,128)S(1)} %bitcast.13), channel_id=1, source_target_pairs={{0,32},{32,0},{1,33},{33,1},{2,34},{34,2},{3,35},{35,3},{4,36},{36... | collective-permute-start | bytes 2359304 | tf_op jit(solution)/shard_map/ppermute | solution.py:506
  57.1 1.6 %collective-permute-start.2 = (f32[8,128]{1,0:T(8,128)S(1)}, f32[8,128]{1,0:T(8,128)S(1)}, u32[]{:S(2)}, u32[]{:S(2)}) collective-permute-start(f32[8,128]{1,0:T(8,128)S(1)} %shard_map.127), channel_id=1, source_target_pairs={{0,32},{32,0},{1,33},{33,1},{2,34},{34,2},{3,35},{35,3},{4,36},{36... | collective-permute-start | bytes 12296 | tf_op jit(solution)/shard_map/ppermute | solution.py:506
  73.7 2.8 %collective-permute-start.3 = (f32[32,128]{1,0:T(8,128)S(1)}, f32[32,128]{1,0:T(8,128)S(1)}, u32[]{:S(2)}, u32[]{:S(2)}) collective-permute-start(f32[32,128]{1,0:T(8,128)S(1)} %shard_map.130.near), channel_id=1, source_target_pairs={{0,32},{32,0},{1,33},{33,1},{2,34},{34,2},{3,35},{35,3},{4,36},{36... | collective-permute-start | bytes 49160 | tf_op jit(solution)/shard_map/ppermute | solution.py:506

commit v9 on v7

--- a/solution.py
+++ b/solution.py
@@ -39,7 +39,7 @@
 BF = jnp.bfloat16
 F32 = jnp.float32
 
-FAR_AXES = ("xl", "z", "xh", "y")
+FAR_AXES = ("xl", "xh", "y", "z")
 ALL_AXES = ("xl", "co", "z", "xh", "y")
 
 
@@ -111,7 +111,7 @@
 ):
     own = (
         lax.axis_index("xl") * PER_GROUP
-        + ((lax.axis_index("z") * 2 + lax.axis_index("xh")) * 4 + lax.axis_index("y")) * OWN
+        + ((lax.axis_index("xh") * 4 + lax.axis_index("y")) * 4 + lax.axis_index("z")) * OWN
     )
     sites = site[...]
     core = lax.axis_index("co")
@@ -516,7 +516,10 @@
 
     def by_core(array):
         lead = array.shape[:-1]
-        return jnp.swapaxes(array.reshape(lead + (2, 2, PER_GROUP)), -3, -2).reshape(lead + (SPHERES,))
+        at = len(lead)
+        by_device = array.reshape(lead + (2, 2, 4, 2, 4, OWN))
+        order = tuple(range(at)) + tuple(at + axis for axis in (1, 0, 3, 4, 2, 5))
+        return by_device.transpose(order).reshape(lead + (SPHERES,))
 
     pairs, tables, probes, seen, tmat, orders, base, radius = call(
         prepare_body,

time: 78.7 us -> 78.6 us (level)
  transfers between devices with their start and end apart: 5 -> 5, of which waited for: 4 -> 4; matrix products, arithmetic and copies ran while one was open for 0% -> 1% of each run, Pallas kernels for 6% -> 6%
where the time goes in v9:
time: 78.6 us; the launch traced here: 78.1 us
  blocking collectives  32.8 us (42%)
  starting transfers between devices  19.4 us (25%)
  waiting for transfers between devices  11.8 us (15%)
  Pallas kernels  9.57 us (12%)
  local copies, waits for them, and re-layouts  3.85 us (5%)
  between operations  0.82 us (1%)
    all_to_all x2, blocking collectives, spread_far(): return lax.all_to_all(parts, FAR_AXES, 0, 0).reshape(lines.shape)  32.8 us
    all_to_all x1, starting transfers between devices, spread_far(): return lax.all_to_all(parts, FAR_AXES, 0, 0).reshape(lines.shape)  12.1 us
    pallas_call x10, Pallas kernels, call(): pl.pallas_call(body, out_shape=[jax.ShapeDtypeStruct(shape, kind) for sha...  9.57 us
    all_to_all x1, waiting for transfers between devices, spread_far(): return lax.all_to_all(parts, FAR_AXES, 0, 0).reshape(lines.shape)  8.33 us
    ppermute x4, starting transfers between devices, swap_cores(): return lax.ppermute(array, 'co', [(0, 1), (1, 0)])  7.27 us
    ppermute x4, waiting for transfers between devices, swap_cores(): return lax.ppermute(array, 'co', [(0, 1), (1, 0)])  3.44 us
    unnamed x22, local copies, waits for them, and re-layouts  2.97 us
  transfers between devices with their start and end apart: 5, of which 4 were waited for; matrix products, arithmetic and copies ran while one was open for 1% of the time, Pallas kernels for 6%

profile of v9, /device:TPU:1, one launch (start us, length us, event | category | flops | bytes accessed | tf_op | source)
XLA Modules:
  0.0 78.1 jit_solution(17410767233166525264)
XLA Ops:
  0.6 0.7 copy-done
  1.4 1.0 %shard_map.121 = f32[1536,128]{1,0:T(8,128)} custom-call(f32[6,480]{1,0:T(8,128)S(1)} %copy-done), custom_call_target="tpu_custom_call" | custom-call | tf_op jit(solution)/shard_map/pallas_call | solution.py:475
  2.4 12.1 %all-to-all-start = ((f32[64,24,128]{2,1,0:T(8,128)}), f32[64,24,128]{2,1,0:T(8,128)S(1)}, u32[]{:S(2)}, u32[]{:S(2)}) async-start(f32[64,24,128]{2,1,0:T(8,128)} %bitcast), calls=%async_computation | async-start | bytes 1572864 | tf_op jit(solution)/shard_map/all_to_all | solution.py:493
  14.9 0.3 reshape.37
  15.5 1.2 %copy-done.2 = bf16[2,480,480]{2,1,0:T(8,128)(2,1)S(1)} copy-done((bf16[2,480,480]{2,1,0:T(8,128)(2,1)S(1)}, bf16[2,480,480]{2,1,0:T(8,128)(2,1)}, u32[]{:S(2)}) %copy-start.2) | copy-done | bytes 921624
  16.7 1.0 %copy-done.3 = bf16[480,480]{1,0:T(8,128)(2,1)S(1)} copy-done((bf16[480,480]{1,0:T(8,128)(2,1)S(1)}, bf16[480,480]{1,0:T(8,128)(2,1)}, u32[]{:S(2)}) %copy-start.3) | copy-done | bytes 460824
  17.7 2.6 %shard_map.122 = (bf16[656,768]{1,0:T(8,128)(2,1)S(1)}, bf16[2,512,512]{2,1,0:T(8,128)(2,1)S(1)}, bf16[512,256]{1,0:T(8,128)(2,1)S(1)}, f32[4,256]{1,0:T(4,128)S...) custom-call(s32[1,768]{1,0:T(1,128)S(1)} %reshape.36.site, ...), custom_call_target="tpu_custom_call" | custom-call | flops 8000000000 | bytes 8000000 | tf_op jit(solution)/shard_map/pallas_call | solution.py:475
  20.3 8.3 %all-to-all-done = f32[64,24,128]{2,1,0:T(8,128)S(1)} async-done(((f32[64,24,128]{2,1,0:T(8,128)}), f32[64,24,128]{2,1,0:T(8,128)S(1)}, u32[]{:S(2)}, u32[]{:S(2)}) %all-to-all-start) | async-done | bytes 786464 | tf_op jit(solution)/shard_map/all_to_all | solution.py:493
  28.7 2.8 %collective-permute-start = (f32[1536,128]{1,0:T(8,128)S(1)}, f32[1536,128]{1,0:T(8,128)S(1)}, u32[]{:S(2)}, u32[]{:S(2)}) collective-permute-start(f32[1536,128]{1,0:T(8,128)S(1)} %shard_map.123.near), channel_id=1, source_target_pairs={{0,32},{32,0},{1,33},{33,1},{2,34},{34,2},{3,35},{35,3},{4,36},{36... | collective-permute-start | bytes 2359304 | tf_op jit(solution)/shard_map/ppermute | solution.py:488
  31.5 0.5 shard_map.124
  32.0 1.4 %collective-permute-done.peer = f32[1536,128]{1,0:T(8,128)S(1)} collective-permute-done((f32[1536,128]{1,0:T(8,128)S(1)}, f32[1536,128]{1,0:T(8,128)S(1)}, u32[]{:S(2)}, u32[]{:S(2)}) %collective-permute-start) | collective-permute-done | bytes 786464 | tf_op jit(solution)/shard_map/ppermute | solution.py:488
  33.4 1.3 %shard_map.125 = (f32[1536,128]{1,0:T(8,128)S(1)}, f32[8,512]{1,0:T(8,128)S(1)}) custom-call(f32[656,512]{1,0:T(8,128)S(1)} %get-tuple-element.20.near_sums, f32[2,512]{1,0:T(2,128)S(1)} %get-tuple-element.21.near_totals, f32[1536,128]{1,0:T(8,128)S(1)} %collective-permute-done.peer, bf16[656,768]{1,0:T(8,128)(2,1)S(1)} %get-tuple-element.19.pairs, ...), custom_call_target="tpu_custom_call" | custom-call | tf_op jit(solution)/shard_map/pallas_call | solution.py:475
  34.7 18.9 %all_to_all.15 = f32[64,24,128]{2,1,0:T(8,128)S(1)} all-to-all(f32[64,24,128]{2,1,0:T(8,128)S(1)} %bitcast.16), channel_id=1, replica_groups=mesh['xl'=2,'co'=2,'z'=4,'xh'=2,'y'=4] {'xl','xh','y','z'}, dimensions={0} | all-to-all | bytes 1572864 | tf_op jit(solution)/shard_map/all_to_all | solution.py:493
  53.6 2.2 %collective-permute-start.1 = (f32[1536,128]{1,0:T(8,128)S(1)}, f32[1536,128]{1,0:T(8,128)S(1)}, u32[]{:S(2)}, u32[]{:S(2)}) collective-permute-start(f32[1536,128]{1,0:T(8,128)S(1)} %bitcast.13), channel_id=1, source_target_pairs={{0,32},{32,0},{1,33},{33,1},{2,34},{34,2},{3,35},{35,3},{4,36},{36... | collective-permute-start | bytes 2359304 | tf_op jit(solution)/shard_map/ppermute | solution.py:488
  55.8 0.7 shard_map.127
  56.5 1.2 %collective-permute-done.1.peer = f32[1536,128]{1,0:T(8,128)S(1)} collective-permute-done((f32[1536,128]{1,0:T(8,128)S(1)}, f32[1536,128]{1,0:T(8,128)S(1)}, u32[]{:S(2)}, u32[]{:S(2)}) %collective-permute-start.1) | collective-permute-done | bytes 786464 | tf_op jit(solution)/shard_map/ppermute | solution.py:488
  57.7 0.3 shard_map.126
  58.1 0.4 collective-permute-start.2
  58.4 1.2 %shard_map.128 = (f32[8,128]{1,0:T(8,128)S(1)}, bf16[656,128]{1,0:T(8,128)(2,1)S(1)}) custom-call(f32[1536,128]{1,0:T(8,128)S(1)} %bitcast.15, f32[656,512]{1,0:T(8,128)S(1)} %get-tuple-element.29.near_sums, f32[2,512]{1,0:T(2,128)S(1)} %get-tuple-element.30.near_gradient, f32[1536,128]{1,0:T(8,128)S(1)} %collective-permute-done.1.peer, ...), custom_call_target="tpu_custom_call" | custom-call | flops 8000000000 | bytes 4000000 | tf_op jit(solution)/shard_map/pallas_call | solution.py:475
  59.7 13.8 %all_to_all.16 = f32[64,8,128]{2,1,0:T(8,128)S(1)} all-to-all(f32[64,8,128]{2,1,0:T(8,128)S(1)} %broadcast_in_dim.2), channel_id=1, replica_groups=mesh['xl'=2,'co'=2,'z'=4,'xh'=2,'y'=4] {'xl','xh','y','z'}, dimensions={0} | all-to-all | bytes 524288 | tf_op jit(solution)/shard_map/all_to_all | solution.py:493
  73.5 0.2 shard_map.129.near
  73.7 1.9 %collective-permute-start.3 = (f32[32,128]{1,0:T(8,128)S(1)}, f32[32,128]{1,0:T(8,128)S(1)}, u32[]{:S(2)}, u32[]{:S(2)}) collective-permute-start(f32[32,128]{1,0:T(8,128)S(1)} %shard_map.129.near), channel_id=1, source_target_pairs={{0,32},{32,0},{1,33},{33,1},{2,34},{34,2},{3,35},{35,3},{4,36},{36... | collective-permute-start | bytes 49160 | tf_op jit(solution)/shard_map/ppermute | solution.py:488
  75.6 0.8 %collective-permute-done.3.peer = f32[32,128]{1,0:T(8,128)S(1)} collective-permute-done((f32[32,128]{1,0:T(8,128)S(1)}, f32[32,128]{1,0:T(8,128)S(1)}, u32[]{:S(2)}, u32[]{:S(2)}) %collective-permute-start.3) | collective-permute-done | bytes 16416 | tf_op jit(solution)/shard_map/ppermute | solution.py:488
  76.5 1.7 %shard_map.130 = (f32[6,480]{1,0:T(8,128)}, f32[6,480]{1,0:T(8,128)}, f32[4]{0:T(128)}) custom-call(f32[32,128]{1,0:T(8,128)S(1)} %shard_map.129.near, f32[32,128]{1,0:T(8,128)S(1)} %collective-permute-done.3.peer, bf16[656,128]{1,0:T(8,128)(2,1)S(1)} %get-tuple-element.34.weights, bf16[2,512,512]{2,1,0:T(8,128)(2,1)S(1)} %get-tuple-element.22.tables, ...), custom_call_target="tpu_custom_call" | custom-call | tf_op jit(solution)/shard_map/pallas_call | solution.py:475
  (28 shorter events, 0.7 us)
Async XLA Ops:
  0.6 0.7 copy-start
  1.4 13.2 %copy-start.10 = (s32[768]{0:T(1024)S(1)}, s32[768]{0:T(1024)}, u32[]{:S(2)}) copy-start(s32[768]{0:T(1024)} %param.11) | copy-start | bytes 9220
  1.4 13.5 %copy-start.9 = (f32[3,768]{1,0:T(4,128)S(1)}, f32[3,768]{1,0:T(4,128)}, u32[]{:S(2)}) copy-start(f32[3,768]{1,0:T(4,128)} %param.12) | copy-start | bytes 27652
  2.4 13.1 %copy-start.1 = (f32[6,480]{1,0:T(8,128)S(1)}, f32[6,480]{1,0:T(8,128)}, u32[]{:S(2)}) copy-start(f32[6,480]{1,0:T(8,128)} %incident.5) | copy-start | bytes 34564
  2.4 13.1 %copy-start.4 = (bf16[256,480]{0,1:T(8,128)(2,1)S(1)}, bf16[256,480]{0,1:T(8,128)(2,1)}, u32[]{:S(2)}) copy-start(bf16[256,480]{0,1:T(8,128)(2,1)} %param.17) | copy-start | bytes 737284
  2.4 13.1 %copy-start.5 = (f32[2,240]{1,0:T(2,128)S(1)}, f32[2,240]{1,0:T(2,128)}, u32[]{:S(2)}) copy-start(f32[2,240]{1,0:T(2,128)} %tmat.1) | copy-start | bytes 5764
  2.4 13.1 %copy-start.6 = (s32[256]{0:T(256)S(1)}, s32[256]{0:T(256)}, u32[]{:S(2)}) copy-start(s32[256]{0:T(256)} %param.18) | copy-start | bytes 3076
  2.4 13.1 %copy-start.7 = (f32[6]{0:T(128)S(1)}, f32[6]{0:T(128)}, u32[]{:S(2)}) copy-start(f32[6]{0:T(128)} %radius.1) | copy-start | bytes 76
  2.4 13.1 %copy-start.8 = (s32[1,256]{1,0:T(1,128)S(1)}, s32[1,256]{1,0:T(1,128)}, u32[]{:S(2)}) copy-start(s32[1,256]{1,0:T(1,128)} %constant.2.clone.orders) | copy-start | bytes 3076
  2.4 26.3 %all-to-all-start = ((f32[64,24,128]{2,1,0:T(8,128)}), f32[64,24,128]{2,1,0:T(8,128)S(1)}, u32[]{:S(2)}, u32[]{:S(2)}) async-start(f32[64,24,128]{2,1,0:T(8,128)} %bitcast), calls=%async_computation | async-start | bytes 1572864 | tf_op jit(solution)/shard_map/all_to_all | solution.py:493
  15.5 1.2 %copy-start.2 = (bf16[2,480,480]{2,1,0:T(8,128)(2,1)S(1)}, bf16[2,480,480]{2,1,0:T(8,128)(2,1)}, u32[]{:S(2)}) copy-start(bf16[2,480,480]{2,1,0:T(8,128)(2,1)} %axial.1) | copy-start | bytes 2764804
  16.7 1.0 %copy-start.3 = (bf16[480,480]{1,0:T(8,128)(2,1)S(1)}, bf16[480,480]{1,0:T(8,128)(2,1)}, u32[]{:S(2)}) copy-start(bf16[480,480]{1,0:T(8,128)(2,1)} %rotation.1) | copy-start | bytes 1382404
  28.7 4.7 %collective-permute-start = (f32[1536,128]{1,0:T(8,128)S(1)}, f32[1536,128]{1,0:T(8,128)S(1)}, u32[]{:S(2)}, u32[]{:S(2)}) collective-permute-start(f32[1536,128]{1,0:T(8,128)S(1)} %shard_map.123.near), channel_id=1, source_target_pairs={{0,32},{32,0},{1,33},{33,1},{2,34},{34,2},{3,35},{35,3},{4,36},{36... | collective-permute-start | bytes 2359304 | tf_op jit(solution)/shard_map/ppermute | solution.py:488
  53.6 4.1 %collective-permute-start.1 = (f32[1536,128]{1,0:T(8,128)S(1)}, f32[1536,128]{1,0:T(8,128)S(1)}, u32[]{:S(2)}, u32[]{:S(2)}) collective-permute-start(f32[1536,128]{1,0:T(8,128)S(1)} %bitcast.13), channel_id=1, source_target_pairs={{0,32},{32,0},{1,33},{33,1},{2,34},{34,2},{3,35},{35,3},{4,36},{36... | collective-permute-start | bytes 2359304 | tf_op jit(solution)/shard_map/ppermute | solution.py:488
  58.1 1.6 %collective-permute-start.2 = (f32[8,128]{1,0:T(8,128)S(1)}, f32[8,128]{1,0:T(8,128)S(1)}, u32[]{:S(2)}, u32[]{:S(2)}) collective-permute-start(f32[8,128]{1,0:T(8,128)S(1)} %shard_map.126), channel_id=1, source_target_pairs={{0,32},{32,0},{1,33},{33,1},{2,34},{34,2},{3,35},{35,3},{4,36},{36... | collective-permute-start | bytes 12296 | tf_op jit(solution)/shard_map/ppermute | solution.py:488
  73.7 2.7 %collective-permute-start.3 = (f32[32,128]{1,0:T(8,128)S(1)}, f32[32,128]{1,0:T(8,128)S(1)}, u32[]{:S(2)}, u32[]{:S(2)}) collective-permute-start(f32[32,128]{1,0:T(8,128)S(1)} %shard_map.129.near), channel_id=1, source_target_pairs={{0,32},{32,0},{1,33},{33,1},{2,34},{34,2},{3,35},{35,3},{4,36},{36... | collective-permute-start | bytes 49160 | tf_op jit(solution)/shard_map/ppermute | solution.py:488

commit v10 on v9

--- a/solution.py
+++ b/solution.py
@@ -39,7 +39,7 @@
 BF = jnp.bfloat16
 F32 = jnp.float32
 
-FAR_AXES = ("xl", "xh", "y", "z")
+FAR_AXES = ("xl", "y", "z", "xh")
 ALL_AXES = ("xl", "co", "z", "xh", "y")
 
 
@@ -111,7 +111,7 @@
 ):
     own = (
         lax.axis_index("xl") * PER_GROUP
-        + ((lax.axis_index("xh") * 4 + lax.axis_index("y")) * 4 + lax.axis_index("z")) * OWN
+        + ((lax.axis_index("y") * 4 + lax.axis_index("z")) * 2 + lax.axis_index("xh")) * OWN
     )
     sites = site[...]
     core = lax.axis_index("co")
@@ -518,7 +518,7 @@
         lead = array.shape[:-1]
         at = len(lead)
         by_device = array.reshape(lead + (2, 2, 4, 2, 4, OWN))
-        order = tuple(range(at)) + tuple(at + axis for axis in (1, 0, 3, 4, 2, 5))
+        order = tuple(range(at)) + tuple(at + axis for axis in (1, 0, 4, 2, 3, 5))
         return by_device.transpose(order).reshape(lead + (SPHERES,))
 
     pairs, tables, probes, seen, tmat, orders, base, radius = call(

time: 78.6 us -> 78.3 us (level)
  starting transfers between devices: 19.4 us -> 18.6 us
where the time goes in v10:
time: 78.3 us; the launch traced here: 77.9 us
  blocking collectives  33 us (42%)
  starting transfers between devices  18.6 us (24%)
  waiting for transfers between devices  12 us (15%)
  Pallas kernels  9.55 us (12%)
  local copies, waits for them, and re-layouts  3.96 us (5%)
  between operations  0.81 us (1%)
    all_to_all x2, blocking collectives, spread_far(): return lax.all_to_all(parts, FAR_AXES, 0, 0).reshape(lines.shape)  33 us
    all_to_all x1, starting transfers between devices, spread_far(): return lax.all_to_all(parts, FAR_AXES, 0, 0).reshape(lines.shape)  12.1 us
    pallas_call x10, Pallas kernels, call(): pl.pallas_call(body, out_shape=[jax.ShapeDtypeStruct(shape, kind) for sha...  9.55 us
    all_to_all x1, waiting for transfers between devices, spread_far(): return lax.all_to_all(parts, FAR_AXES, 0, 0).reshape(lines.shape)  8.55 us
    ppermute x4, starting transfers between devices, swap_cores(): return lax.ppermute(array, 'co', [(0, 1), (1, 0)])  6.5 us
    ppermute x4, waiting for transfers between devices, swap_cores(): return lax.ppermute(array, 'co', [(0, 1), (1, 0)])  3.44 us
    unnamed x22, local copies, waits for them, and re-layouts  2.97 us
  transfers between devices with their start and end apart: 5, of which 4 were waited for; matrix products, arithmetic and copies ran while one was open for 1% of the time, Pallas kernels for 6%

profile of v10, /device:TPU:1, one launch (start us, length us, event | category | flops | bytes accessed | tf_op | source)
XLA Modules:
  0.0 77.9 jit_solution(6031593455897161125)
XLA Ops:
  0.6 0.7 copy-done
  1.4 1.0 %shard_map.121 = f32[1536,128]{1,0:T(8,128)} custom-call(f32[6,480]{1,0:T(8,128)S(1)} %copy-done), custom_call_target="tpu_custom_call" | custom-call | tf_op jit(solution)/shard_map/pallas_call | solution.py:475
  2.4 12.1 %all-to-all-start = ((f32[64,24,128]{2,1,0:T(8,128)}), f32[64,24,128]{2,1,0:T(8,128)S(1)}, u32[]{:S(2)}, u32[]{:S(2)}) async-start(f32[64,24,128]{2,1,0:T(8,128)} %bitcast), calls=%async_computation | async-start | bytes 1572864 | tf_op jit(solution)/shard_map/all_to_all | solution.py:493
  14.9 0.3 reshape.37
  15.3 0.3 reshape.38.jitter
  15.6 1.2 %copy-done.2 = bf16[2,480,480]{2,1,0:T(8,128)(2,1)S(1)} copy-done((bf16[2,480,480]{2,1,0:T(8,128)(2,1)S(1)}, bf16[2,480,480]{2,1,0:T(8,128)(2,1)}, u32[]{:S(2)}) %copy-start.2) | copy-done | bytes 921624
  16.8 1.0 %copy-done.3 = bf16[480,480]{1,0:T(8,128)(2,1)S(1)} copy-done((bf16[480,480]{1,0:T(8,128)(2,1)S(1)}, bf16[480,480]{1,0:T(8,128)(2,1)}, u32[]{:S(2)}) %copy-start.3) | copy-done | bytes 460824
  17.8 2.6 %shard_map.122 = (bf16[656,768]{1,0:T(8,128)(2,1)S(1)}, bf16[2,512,512]{2,1,0:T(8,128)(2,1)S(1)}, bf16[512,256]{1,0:T(8,128)(2,1)S(1)}, f32[4,256]{1,0:T(4,128)S...) custom-call(s32[1,768]{1,0:T(1,128)S(1)} %reshape.36.site, ...), custom_call_target="tpu_custom_call" | custom-call | flops 8000000000 | bytes 8000000 | tf_op jit(solution)/shard_map/pallas_call | solution.py:475
  20.4 8.6 %all-to-all-done = f32[64,24,128]{2,1,0:T(8,128)S(1)} async-done(((f32[64,24,128]{2,1,0:T(8,128)}), f32[64,24,128]{2,1,0:T(8,128)S(1)}, u32[]{:S(2)}, u32[]{:S(2)}) %all-to-all-start) | async-done | bytes 786464 | tf_op jit(solution)/shard_map/all_to_all | solution.py:493
  29.0 2.4 %collective-permute-start = (f32[1536,128]{1,0:T(8,128)S(1)}, f32[1536,128]{1,0:T(8,128)S(1)}, u32[]{:S(2)}, u32[]{:S(2)}) collective-permute-start(f32[1536,128]{1,0:T(8,128)S(1)} %shard_map.123.near), channel_id=1, source_target_pairs={{0,32},{32,0},{1,33},{33,1},{2,34},{34,2},{3,35},{35,3},{4,36},{36... | collective-permute-start | bytes 2359304 | tf_op jit(solution)/shard_map/ppermute | solution.py:488
  31.4 0.5 shard_map.124
  31.9 1.4 %collective-permute-done.peer = f32[1536,128]{1,0:T(8,128)S(1)} collective-permute-done((f32[1536,128]{1,0:T(8,128)S(1)}, f32[1536,128]{1,0:T(8,128)S(1)}, u32[]{:S(2)}, u32[]{:S(2)}) %collective-permute-start) | collective-permute-done | bytes 786464 | tf_op jit(solution)/shard_map/ppermute | solution.py:488
  33.3 1.3 %shard_map.125 = (f32[1536,128]{1,0:T(8,128)S(1)}, f32[8,512]{1,0:T(8,128)S(1)}) custom-call(f32[656,512]{1,0:T(8,128)S(1)} %get-tuple-element.20.near_sums, f32[2,512]{1,0:T(2,128)S(1)} %get-tuple-element.21.near_totals, f32[1536,128]{1,0:T(8,128)S(1)} %collective-permute-done.peer, bf16[656,768]{1,0:T(8,128)(2,1)S(1)} %get-tuple-element.19.pairs, ...), custom_call_target="tpu_custom_call" | custom-call | tf_op jit(solution)/shard_map/pallas_call | solution.py:475
  34.6 19.1 %all_to_all.15 = f32[64,24,128]{2,1,0:T(8,128)S(1)} all-to-all(f32[64,24,128]{2,1,0:T(8,128)S(1)} %bitcast.16), channel_id=1, replica_groups=mesh['xl'=2,'co'=2,'z'=4,'xh'=2,'y'=4] {'xl','y','z','xh'}, dimensions={0} | all-to-all | bytes 1572864 | tf_op jit(solution)/shard_map/all_to_all | solution.py:493
  53.7 1.9 %collective-permute-start.1 = (f32[1536,128]{1,0:T(8,128)S(1)}, f32[1536,128]{1,0:T(8,128)S(1)}, u32[]{:S(2)}, u32[]{:S(2)}) collective-permute-start(f32[1536,128]{1,0:T(8,128)S(1)} %bitcast.13), channel_id=1, source_target_pairs={{0,32},{32,0},{1,33},{33,1},{2,34},{34,2},{3,35},{35,3},{4,36},{36... | collective-permute-start | bytes 2359304 | tf_op jit(solution)/shard_map/ppermute | solution.py:488
  55.6 0.7 shard_map.127
  56.3 1.2 %collective-permute-done.1.peer = f32[1536,128]{1,0:T(8,128)S(1)} collective-permute-done((f32[1536,128]{1,0:T(8,128)S(1)}, f32[1536,128]{1,0:T(8,128)S(1)}, u32[]{:S(2)}, u32[]{:S(2)}) %collective-permute-start.1) | collective-permute-done | bytes 786464 | tf_op jit(solution)/shard_map/ppermute | solution.py:488
  57.5 0.3 shard_map.126
  57.8 0.4 collective-permute-start.2
  58.2 1.2 %shard_map.128 = (f32[8,128]{1,0:T(8,128)S(1)}, bf16[656,128]{1,0:T(8,128)(2,1)S(1)}) custom-call(f32[1536,128]{1,0:T(8,128)S(1)} %bitcast.15, f32[656,512]{1,0:T(8,128)S(1)} %get-tuple-element.29.near_sums, f32[2,512]{1,0:T(2,128)S(1)} %get-tuple-element.30.near_gradient, f32[1536,128]{1,0:T(8,128)S(1)} %collective-permute-done.1.peer, ...), custom_call_target="tpu_custom_call" | custom-call | flops 8000000000 | bytes 4000000 | tf_op jit(solution)/shard_map/pallas_call | solution.py:475
  59.5 13.9 %all_to_all.16 = f32[64,8,128]{2,1,0:T(8,128)S(1)} all-to-all(f32[64,8,128]{2,1,0:T(8,128)S(1)} %broadcast_in_dim.2), channel_id=1, replica_groups=mesh['xl'=2,'co'=2,'z'=4,'xh'=2,'y'=4] {'xl','y','z','xh'}, dimensions={0} | all-to-all | bytes 524288 | tf_op jit(solution)/shard_map/all_to_all | solution.py:493
  73.6 1.8 %collective-permute-start.3 = (f32[32,128]{1,0:T(8,128)S(1)}, f32[32,128]{1,0:T(8,128)S(1)}, u32[]{:S(2)}, u32[]{:S(2)}) collective-permute-start(f32[32,128]{1,0:T(8,128)S(1)} %shard_map.129.near), channel_id=1, source_target_pairs={{0,32},{32,0},{1,33},{33,1},{2,34},{34,2},{3,35},{35,3},{4,36},{36... | collective-permute-start | bytes 49160 | tf_op jit(solution)/shard_map/ppermute | solution.py:488
  75.4 0.8 %collective-permute-done.3.peer = f32[32,128]{1,0:T(8,128)S(1)} collective-permute-done((f32[32,128]{1,0:T(8,128)S(1)}, f32[32,128]{1,0:T(8,128)S(1)}, u32[]{:S(2)}, u32[]{:S(2)}) %collective-permute-start.3) | collective-permute-done | bytes 16416 | tf_op jit(solution)/shard_map/ppermute | solution.py:488
  76.2 1.7 %shard_map.130 = (f32[6,480]{1,0:T(8,128)}, f32[6,480]{1,0:T(8,128)}, f32[4]{0:T(128)}) custom-call(f32[32,128]{1,0:T(8,128)S(1)} %shard_map.129.near, f32[32,128]{1,0:T(8,128)S(1)} %collective-permute-done.3.peer, bf16[656,128]{1,0:T(8,128)(2,1)S(1)} %get-tuple-element.34.weights, bf16[2,512,512]{2,1,0:T(8,128)(2,1)S(1)} %get-tuple-element.22.tables, ...), custom_call_target="tpu_custom_call" | custom-call | tf_op jit(solution)/shard_map/pallas_call | solution.py:475
  (28 shorter events, 0.7 us)
Async XLA Ops:
  0.6 0.7 copy-start
  1.4 13.2 %copy-start.10 = (s32[768]{0:T(1024)S(1)}, s32[768]{0:T(1024)}, u32[]{:S(2)}) copy-start(s32[768]{0:T(1024)} %param.11) | copy-start | bytes 9220
  1.4 13.5 %copy-start.9 = (f32[3,768]{1,0:T(4,128)S(1)}, f32[3,768]{1,0:T(4,128)}, u32[]{:S(2)}) copy-start(f32[3,768]{1,0:T(4,128)} %param.12) | copy-start | bytes 27652
  2.4 13.2 %copy-start.1 = (f32[6,480]{1,0:T(8,128)S(1)}, f32[6,480]{1,0:T(8,128)}, u32[]{:S(2)}) copy-start(f32[6,480]{1,0:T(8,128)} %incident.5) | copy-start | bytes 34564
  2.4 13.2 %copy-start.4 = (bf16[256,480]{0,1:T(8,128)(2,1)S(1)}, bf16[256,480]{0,1:T(8,128)(2,1)}, u32[]{:S(2)}) copy-start(bf16[256,480]{0,1:T(8,128)(2,1)} %param.17) | copy-start | bytes 737284
  2.4 13.2 %copy-start.5 = (f32[2,240]{1,0:T(2,128)S(1)}, f32[2,240]{1,0:T(2,128)}, u32[]{:S(2)}) copy-start(f32[2,240]{1,0:T(2,128)} %tmat.1) | copy-start | bytes 5764
  2.4 13.2 %copy-start.6 = (s32[256]{0:T(256)S(1)}, s32[256]{0:T(256)}, u32[]{:S(2)}) copy-start(s32[256]{0:T(256)} %param.18) | copy-start | bytes 3076
  2.4 13.2 %copy-start.7 = (f32[6]{0:T(128)S(1)}, f32[6]{0:T(128)}, u32[]{:S(2)}) copy-start(f32[6]{0:T(128)} %radius.1) | copy-start | bytes 76
  2.4 13.2 %copy-start.8 = (s32[1,256]{1,0:T(1,128)S(1)}, s32[1,256]{1,0:T(1,128)}, u32[]{:S(2)}) copy-start(s32[1,256]{1,0:T(1,128)} %constant.2.clone.orders) | copy-start | bytes 3076
  2.4 26.6 %all-to-all-start = ((f32[64,24,128]{2,1,0:T(8,128)}), f32[64,24,128]{2,1,0:T(8,128)S(1)}, u32[]{:S(2)}, u32[]{:S(2)}) async-start(f32[64,24,128]{2,1,0:T(8,128)} %bitcast), calls=%async_computation | async-start | bytes 1572864 | tf_op jit(solution)/shard_map/all_to_all | solution.py:493
  15.6 1.2 %copy-start.2 = (bf16[2,480,480]{2,1,0:T(8,128)(2,1)S(1)}, bf16[2,480,480]{2,1,0:T(8,128)(2,1)}, u32[]{:S(2)}) copy-start(bf16[2,480,480]{2,1,0:T(8,128)(2,1)} %axial.1) | copy-start | bytes 2764804
  16.8 1.0 %copy-start.3 = (bf16[480,480]{1,0:T(8,128)(2,1)S(1)}, bf16[480,480]{1,0:T(8,128)(2,1)}, u32[]{:S(2)}) copy-start(bf16[480,480]{1,0:T(8,128)(2,1)} %rotation.1) | copy-start | bytes 1382404
  29.0 4.3 %collective-permute-start = (f32[1536,128]{1,0:T(8,128)S(1)}, f32[1536,128]{1,0:T(8,128)S(1)}, u32[]{:S(2)}, u32[]{:S(2)}) collective-permute-start(f32[1536,128]{1,0:T(8,128)S(1)} %shard_map.123.near), channel_id=1, source_target_pairs={{0,32},{32,0},{1,33},{33,1},{2,34},{34,2},{3,35},{35,3},{4,36},{36... | collective-permute-start | bytes 2359304 | tf_op jit(solution)/shard_map/ppermute | solution.py:488
  53.7 3.8 %collective-permute-start.1 = (f32[1536,128]{1,0:T(8,128)S(1)}, f32[1536,128]{1,0:T(8,128)S(1)}, u32[]{:S(2)}, u32[]{:S(2)}) collective-permute-start(f32[1536,128]{1,0:T(8,128)S(1)} %bitcast.13), channel_id=1, source_target_pairs={{0,32},{32,0},{1,33},{33,1},{2,34},{34,2},{3,35},{35,3},{4,36},{36... | collective-permute-start | bytes 2359304 | tf_op jit(solution)/shard_map/ppermute | solution.py:488
  57.8 1.6 %collective-permute-start.2 = (f32[8,128]{1,0:T(8,128)S(1)}, f32[8,128]{1,0:T(8,128)S(1)}, u32[]{:S(2)}, u32[]{:S(2)}) collective-permute-start(f32[8,128]{1,0:T(8,128)S(1)} %shard_map.126), channel_id=1, source_target_pairs={{0,32},{32,0},{1,33},{33,1},{2,34},{34,2},{3,35},{35,3},{4,36},{36... | collective-permute-start | bytes 12296 | tf_op jit(solution)/shard_map/ppermute | solution.py:488
  73.6 2.6 %collective-permute-start.3 = (f32[32,128]{1,0:T(8,128)S(1)}, f32[32,128]{1,0:T(8,128)S(1)}, u32[]{:S(2)}, u32[]{:S(2)}) collective-permute-start(f32[32,128]{1,0:T(8,128)S(1)} %shard_map.129.near), channel_id=1, source_target_pairs={{0,32},{32,0},{1,33},{33,1},{2,34},{34,2},{3,35},{35,3},{4,36},{36... | collective-permute-start | bytes 49160 | tf_op jit(solution)/shard_map/ppermute | solution.py:488

commit v11 on v10

--- a/solution.py
+++ b/solution.py
@@ -107,7 +107,7 @@
 
 def prepare_body(
     site, jitter, rotation, axial, probes, probe_group, tmat, orders, incident, radius,
-    pairs, tables, probes_out, seen_out, tmat_out, orders_out, base_out, radius_out,
+    pairs, tables, tables_t, probes_out, seen_out, tmat_out, orders_out, base_out, radius_out,
 ):
     own = (
         lax.axis_index("xl") * PER_GROUP
@@ -164,6 +164,7 @@
     turned = padded(rotation[...], 0)
     for radial in range(2):
         tables[radial] = fine_dot(0.5 * dot(turned, axial[radial]), turned, dot_t, 2).astype(BF)
+        tables_t[radial] = fine_dot(0.5 * dot_t(turned, axial[radial]), turned, dot_t, 2).astype(BF)
     line = lax.broadcasted_iota(jnp.int32, (GROUPS, PROBES_OWN), 0)
     seen_out[...] = jnp.where(line == probe_group[...], 1.0, 0.0)
     tmat_rows = jnp.concatenate([tmat[...], jnp.zeros((2, WIDE - HALF), F32)], axis=1)
@@ -454,7 +455,7 @@
     places[at, :WIDE] = real * grad_re + imag * grad_im
     places[at, WIDE:] = real * grad_im - imag * grad_re
     sums[...] = dot(weights[...], places[...].astype(BF))
-    field = mix(sums, shifted, tables, orders, dot_t)
+    field = mix(sums, shifted, tables, orders)
     group = own_group()
     own = jnp.zeros((1, FULL), F32)
     for g in range(GROUPS):
@@ -521,10 +522,11 @@
         order = tuple(range(at)) + tuple(at + axis for axis in (1, 0, 4, 2, 3, 5))
         return by_device.transpose(order).reshape(lead + (SPHERES,))
 
-    pairs, tables, probes, seen, tmat, orders, base, radius = call(
+    pairs, tables, tables_t, probes, seen, tmat, orders, base, radius = call(
         prepare_body,
         [
             ((BLOCKS * BLOCK, SPHERES), BF),
+            ((2, FULL, FULL), BF),
             ((2, FULL, FULL), BF),
             ((FULL, PROBES_OWN), BF),
             ((GROUPS, PROBES_OWN), F32),
@@ -590,7 +592,7 @@
         finish_body,
         [((OWN, COEFF), F32), ((OWN, COEFF), F32), ((4,), F32)],
         [pltpu.VMEM((LANES, FULL), F32), sum_scratch, shift_scratch],
-        (near, peer, weights, tables, tmat, orders, incident, image),
+        (near, peer, weights, tables_t, tmat, orders, incident, image),
         out_spaces={2: pltpu.SMEM},
     )
     return solution_rows, sensitivity_rows, arnoldi

time: 78.3 us -> 78.4 us (level)
  waiting for transfers between devices: 12 us -> 9.36 us
  Pallas kernels: 9.55 us -> 11.2 us
  local copies, waits for them, and re-layouts: 3.96 us -> 4.95 us
    all_to_all x1, waiting for transfers between devices: 8.55 us -> 5.92 us  [spread_far(): return lax.all_to_all(parts, FAR_AXES, 0, 0).reshape(lines.shape)]
    pallas_call x10, Pallas kernels: 9.55 us -> 11.2 us  [call(): pl.pallas_call(body, out_shape=[jax.ShapeDtypeStruct(shape, kind) for sha...]
    unnamed x22 -> x26, local copies, waits for them, and re-layouts: 2.97 us -> 3.98 us
  transfers between devices with their start and end apart: 5 -> 5, of which waited for: 4 -> 4; matrix products, arithmetic and copies ran while one was open for 1% -> 1% of each run, Pallas kernels for 6% -> 9%
where the time goes in v11:
time: 78.4 us; the launch traced here: 78 us
  blocking collectives  33 us (42%)
  starting transfers between devices  18.7 us (24%)
  Pallas kernels  11.2 us (14%)
  waiting for transfers between devices  9.36 us (12%)
  local copies, waits for them, and re-layouts  4.95 us (6%)
  between operations  0.82 us (1%)
    all_to_all x2, blocking collectives, spread_far(): return lax.all_to_all(parts, FAR_AXES, 0, 0).reshape(lines.shape)  33 us
    all_to_all x1, starting transfers between devices, spread_far(): return lax.all_to_all(parts, FAR_AXES, 0, 0).reshape(lines.shape)  12.1 us
    pallas_call x10, Pallas kernels, call(): pl.pallas_call(body, out_shape=[jax.ShapeDtypeStruct(shape, kind) for sha...  11.2 us
    ppermute x4, starting transfers between devices, swap_cores(): return lax.ppermute(array, 'co', [(0, 1), (1, 0)])  6.54 us
    all_to_all x1, waiting for transfers between devices, spread_far(): return lax.all_to_all(parts, FAR_AXES, 0, 0).reshape(lines.shape)  5.92 us
    unnamed x26, local copies, waits for them, and re-layouts  3.98 us
    ppermute x4, waiting for transfers between devices, swap_cores(): return lax.ppermute(array, 'co', [(0, 1), (1, 0)])  3.44 us
  transfers between devices with their start and end apart: 5, of which 4 were waited for; matrix products, arithmetic and copies ran while one was open for 1% of the time, Pallas kernels for 9%

profile of v11, /device:TPU:1, one launch (start us, length us, event | category | flops | bytes accessed | tf_op | source)
XLA Modules:
  0.0 78.0 jit_solution(14421218056583561607)
XLA Ops:
  0.6 0.7 copy-done.2
  1.4 1.0 %shard_map.121 = f32[1536,128]{1,0:T(8,128)} custom-call(f32[6,480]{1,0:T(8,128)S(1)} %copy-done.2), custom_call_target="tpu_custom_call" | custom-call | tf_op jit(solution)/shard_map/pallas_call | solution.py:476
  2.4 12.1 %all-to-all-start = ((f32[64,24,128]{2,1,0:T(8,128)}), f32[64,24,128]{2,1,0:T(8,128)S(1)}, u32[]{:S(2)}, u32[]{:S(2)}) async-start(f32[64,24,128]{2,1,0:T(8,128)} %bitcast), calls=%async_computation | async-start | bytes 1572864 | tf_op jit(solution)/shard_map/all_to_all | solution.py:494
  15.3 0.3 reshape.38.jitter
  15.6 1.2 %copy-done.4 = bf16[2,480,480]{2,1,0:T(8,128)(2,1)S(1)} copy-done((bf16[2,480,480]{2,1,0:T(8,128)(2,1)S(1)}, bf16[2,480,480]{2,1,0:T(8,128)(2,1)}, u32[]{:S(2)}) %copy-start.4) | copy-done | bytes 921624
  16.8 1.0 %copy-done.5 = bf16[480,480]{1,0:T(8,128)(2,1)S(1)} copy-done((bf16[480,480]{1,0:T(8,128)(2,1)S(1)}, bf16[480,480]{1,0:T(8,128)(2,1)}, u32[]{:S(2)}) %copy-start.5) | copy-done | bytes 460824
  17.8 4.3 %shard_map.122 = (bf16[656,768]{1,0:T(8,128)(2,1)S(1)}, bf16[2,512,512]{2,1,0:T(8,128)(2,1)S(1)}, bf16[2,512,512]{2,1,0:T(8,128)(2,1)S(1)}, bf16[512,256]{1,0:T(...) custom-call(s32[1,768]{1,0:T(1,128)S(1)} %reshape.36.site, ...), custom_call_target="tpu_custom_call" | custom-call | flops 8000000000 | bytes 8000000 | tf_op jit(solution)/shard_map/pallas_call | solution.py:476
  22.1 1.0 %copy-done = bf16[2,512,512]{2,1,0:T(8,128)(2,1)} copy-done((bf16[2,512,512]{2,1,0:T(8,128)(2,1)}, bf16[2,512,512]{2,1,0:T(8,128)(2,1)S(1)}, u32[]{:S(2)}) %copy-start) | copy-done | bytes 1048600
  23.1 5.9 %all-to-all-done = f32[64,24,128]{2,1,0:T(8,128)S(1)} async-done(((f32[64,24,128]{2,1,0:T(8,128)}), f32[64,24,128]{2,1,0:T(8,128)S(1)}, u32[]{:S(2)}, u32[]{:S(2)}) %all-to-all-start) | async-done | bytes 786464 | tf_op jit(solution)/shard_map/all_to_all | solution.py:494
  29.0 2.4 %collective-permute-start = (f32[1536,128]{1,0:T(8,128)S(1)}, f32[1536,128]{1,0:T(8,128)S(1)}, u32[]{:S(2)}, u32[]{:S(2)}) collective-permute-start(f32[1536,128]{1,0:T(8,128)S(1)} %shard_map.123.near), channel_id=1, source_target_pairs={{0,32},{32,0},{1,33},{33,1},{2,34},{34,2},{3,35},{35,3},{4,36},{36... | collective-permute-start | bytes 2359304 | tf_op jit(solution)/shard_map/ppermute | solution.py:489
  31.4 0.5 shard_map.124
  32.0 1.4 %collective-permute-done.peer = f32[1536,128]{1,0:T(8,128)S(1)} collective-permute-done((f32[1536,128]{1,0:T(8,128)S(1)}, f32[1536,128]{1,0:T(8,128)S(1)}, u32[]{:S(2)}, u32[]{:S(2)}) %collective-permute-start) | collective-permute-done | bytes 786464 | tf_op jit(solution)/shard_map/ppermute | solution.py:489
  33.4 1.3 %shard_map.125 = (f32[1536,128]{1,0:T(8,128)S(1)}, f32[8,512]{1,0:T(8,128)S(1)}) custom-call(f32[656,512]{1,0:T(8,128)S(1)} %get-tuple-element.21.near_sums, f32[2,512]{1,0:T(2,128)S(1)} %get-tuple-element.22.near_totals, f32[1536,128]{1,0:T(8,128)S(1)} %collective-permute-done.peer, bf16[656,768]{1,0:T(8,128)(2,1)S(1)} %get-tuple-element.20.pairs, ...), custom_call_target="tpu_custom_call" | custom-call | tf_op jit(solution)/shard_map/pallas_call | solution.py:476
  34.7 19.0 %all_to_all.15 = f32[64,24,128]{2,1,0:T(8,128)S(1)} all-to-all(f32[64,24,128]{2,1,0:T(8,128)S(1)} %bitcast.16), channel_id=1, replica_groups=mesh['xl'=2,'co'=2,'z'=4,'xh'=2,'y'=4] {'xl','y','z','xh'}, dimensions={0} | all-to-all | bytes 1572864 | tf_op jit(solution)/shard_map/all_to_all | solution.py:494
  53.7 2.0 %collective-permute-start.1 = (f32[1536,128]{1,0:T(8,128)S(1)}, f32[1536,128]{1,0:T(8,128)S(1)}, u32[]{:S(2)}, u32[]{:S(2)}) collective-permute-start(f32[1536,128]{1,0:T(8,128)S(1)} %bitcast.13), channel_id=1, source_target_pairs={{0,32},{32,0},{1,33},{33,1},{2,34},{34,2},{3,35},{35,3},{4,36},{36... | collective-permute-start | bytes 2359304 | tf_op jit(solution)/shard_map/ppermute | solution.py:489
  55.7 0.7 shard_map.127
  56.4 1.2 %collective-permute-done.1.peer = f32[1536,128]{1,0:T(8,128)S(1)} collective-permute-done((f32[1536,128]{1,0:T(8,128)S(1)}, f32[1536,128]{1,0:T(8,128)S(1)}, u32[]{:S(2)}, u32[]{:S(2)}) %collective-permute-start.1) | collective-permute-done | bytes 786464 | tf_op jit(solution)/shard_map/ppermute | solution.py:489
  57.6 0.3 shard_map.126
  57.9 0.4 collective-permute-start.2
  58.3 1.2 %shard_map.128 = (f32[8,128]{1,0:T(8,128)S(1)}, bf16[656,128]{1,0:T(8,128)(2,1)S(1)}) custom-call(f32[1536,128]{1,0:T(8,128)S(1)} %bitcast.15, f32[656,512]{1,0:T(8,128)S(1)} %get-tuple-element.30.near_sums, f32[2,512]{1,0:T(2,128)S(1)} %get-tuple-element.31.near_gradient, f32[1536,128]{1,0:T(8,128)S(1)} %collective-permute-done.1.peer, ...), custom_call_target="tpu_custom_call" | custom-call | flops 8000000000 | bytes 4000000 | tf_op jit(solution)/shard_map/pallas_call | solution.py:476
  59.5 14.0 %all_to_all.16 = f32[64,8,128]{2,1,0:T(8,128)S(1)} all-to-all(f32[64,8,128]{2,1,0:T(8,128)S(1)} %broadcast_in_dim.2), channel_id=1, replica_groups=mesh['xl'=2,'co'=2,'z'=4,'xh'=2,'y'=4] {'xl','y','z','xh'}, dimensions={0} | all-to-all | bytes 524288 | tf_op jit(solution)/shard_map/all_to_all | solution.py:494
  73.8 1.8 %collective-permute-start.3 = (f32[32,128]{1,0:T(8,128)S(1)}, f32[32,128]{1,0:T(8,128)S(1)}, u32[]{:S(2)}, u32[]{:S(2)}) collective-permute-start(f32[32,128]{1,0:T(8,128)S(1)} %shard_map.129.near), channel_id=1, source_target_pairs={{0,32},{32,0},{1,33},{33,1},{2,34},{34,2},{3,35},{35,3},{4,36},{36... | collective-permute-start | bytes 49160 | tf_op jit(solution)/shard_map/ppermute | solution.py:489
  75.6 0.8 %collective-permute-done.3.peer = f32[32,128]{1,0:T(8,128)S(1)} collective-permute-done((f32[32,128]{1,0:T(8,128)S(1)}, f32[32,128]{1,0:T(8,128)S(1)}, u32[]{:S(2)}, u32[]{:S(2)}) %collective-permute-start.3) | collective-permute-done | bytes 16416 | tf_op jit(solution)/shard_map/ppermute | solution.py:489
  76.4 1.6 %shard_map.130 = (f32[6,480]{1,0:T(8,128)}, f32[6,480]{1,0:T(8,128)}, f32[4]{0:T(128)}) custom-call(f32[32,128]{1,0:T(8,128)S(1)} %shard_map.129.near, f32[32,128]{1,0:T(8,128)S(1)} %collective-permute-done.3.peer, bf16[656,128]{1,0:T(8,128)(2,1)S(1)} %get-tuple-element.35.weights, bf16[2,512,512]{2,1,0:T(8,128)(2,1)S(1)} %copy-done.1, ...), custom_call_target="tpu_custom_call" | custom-call | tf_op jit(solution)/shard_map/pallas_call | solution.py:476
  (32 shorter events, 1.0 us)
Async XLA Ops:
  0.6 0.7 copy-start.2
  1.4 13.2 %copy-start.12 = (s32[768]{0:T(1024)S(1)}, s32[768]{0:T(1024)}, u32[]{:S(2)}) copy-start(s32[768]{0:T(1024)} %param.11) | copy-start | bytes 9220
  1.4 13.6 %copy-start.11 = (f32[3,768]{1,0:T(4,128)S(1)}, f32[3,768]{1,0:T(4,128)}, u32[]{:S(2)}) copy-start(f32[3,768]{1,0:T(4,128)} %param.12) | copy-start | bytes 27652
  2.4 13.2 %copy-start.3 = (f32[6,480]{1,0:T(8,128)S(1)}, f32[6,480]{1,0:T(8,128)}, u32[]{:S(2)}) copy-start(f32[6,480]{1,0:T(8,128)} %incident.5) | copy-start | bytes 34564
  2.4 13.2 %copy-start.6 = (bf16[256,480]{0,1:T(8,128)(2,1)S(1)}, bf16[256,480]{0,1:T(8,128)(2,1)}, u32[]{:S(2)}) copy-start(bf16[256,480]{0,1:T(8,128)(2,1)} %param.17) | copy-start | bytes 737284
  2.4 13.2 %copy-start.7 = (f32[2,240]{1,0:T(2,128)S(1)}, f32[2,240]{1,0:T(2,128)}, u32[]{:S(2)}) copy-start(f32[2,240]{1,0:T(2,128)} %tmat.1) | copy-start | bytes 5764
  2.4 13.2 %copy-start.8 = (s32[256]{0:T(256)S(1)}, s32[256]{0:T(256)}, u32[]{:S(2)}) copy-start(s32[256]{0:T(256)} %param.18) | copy-start | bytes 3076
  2.4 13.2 %copy-start.9 = (f32[6]{0:T(128)S(1)}, f32[6]{0:T(128)}, u32[]{:S(2)}) copy-start(f32[6]{0:T(128)} %radius.1) | copy-start | bytes 76
  2.4 13.2 %copy-start.10 = (s32[1,256]{1,0:T(1,128)S(1)}, s32[1,256]{1,0:T(1,128)}, u32[]{:S(2)}) copy-start(s32[1,256]{1,0:T(1,128)} %constant.2.clone.orders) | copy-start | bytes 3076
  2.4 26.6 %all-to-all-start = ((f32[64,24,128]{2,1,0:T(8,128)}), f32[64,24,128]{2,1,0:T(8,128)S(1)}, u32[]{:S(2)}, u32[]{:S(2)}) async-start(f32[64,24,128]{2,1,0:T(8,128)} %bitcast), calls=%async_computation | async-start | bytes 1572864 | tf_op jit(solution)/shard_map/all_to_all | solution.py:494
  15.6 1.2 %copy-start.4 = (bf16[2,480,480]{2,1,0:T(8,128)(2,1)S(1)}, bf16[2,480,480]{2,1,0:T(8,128)(2,1)}, u32[]{:S(2)}) copy-start(bf16[2,480,480]{2,1,0:T(8,128)(2,1)} %axial.1) | copy-start | bytes 2764804
  16.8 1.0 %copy-start.5 = (bf16[480,480]{1,0:T(8,128)(2,1)S(1)}, bf16[480,480]{1,0:T(8,128)(2,1)}, u32[]{:S(2)}) copy-start(bf16[480,480]{1,0:T(8,128)(2,1)} %rotation.1) | copy-start | bytes 1382404
  22.1 1.0 %copy-start = (bf16[2,512,512]{2,1,0:T(8,128)(2,1)}, bf16[2,512,512]{2,1,0:T(8,128)(2,1)S(1)}, u32[]{:S(2)}) copy-start(bf16[2,512,512]{2,1,0:T(8,128)(2,1)S(1)} %get-tuple-element.36.tables) | copy-start | bytes 3145732
  29.0 4.3 %collective-permute-start = (f32[1536,128]{1,0:T(8,128)S(1)}, f32[1536,128]{1,0:T(8,128)S(1)}, u32[]{:S(2)}, u32[]{:S(2)}) collective-permute-start(f32[1536,128]{1,0:T(8,128)S(1)} %shard_map.123.near), channel_id=1, source_target_pairs={{0,32},{32,0},{1,33},{33,1},{2,34},{34,2},{3,35},{35,3},{4,36},{36... | collective-permute-start | bytes 2359304 | tf_op jit(solution)/shard_map/ppermute | solution.py:489
  53.7 3.9 %collective-permute-start.1 = (f32[1536,128]{1,0:T(8,128)S(1)}, f32[1536,128]{1,0:T(8,128)S(1)}, u32[]{:S(2)}, u32[]{:S(2)}) collective-permute-start(f32[1536,128]{1,0:T(8,128)S(1)} %bitcast.13), channel_id=1, source_target_pairs={{0,32},{32,0},{1,33},{33,1},{2,34},{34,2},{3,35},{35,3},{4,36},{36... | collective-permute-start | bytes 2359304 | tf_op jit(solution)/shard_map/ppermute | solution.py:489
  57.9 1.6 %collective-permute-start.2 = (f32[8,128]{1,0:T(8,128)S(1)}, f32[8,128]{1,0:T(8,128)S(1)}, u32[]{:S(2)}, u32[]{:S(2)}) collective-permute-start(f32[8,128]{1,0:T(8,128)S(1)} %shard_map.126), channel_id=1, source_target_pairs={{0,32},{32,0},{1,33},{33,1},{2,34},{34,2},{3,35},{35,3},{4,36},{36... | collective-permute-start | bytes 12296 | tf_op jit(solution)/shard_map/ppermute | solution.py:489
  59.5 16.9 %copy-start.1 = (bf16[2,512,512]{2,1,0:T(8,128)(2,1)S(1)}, bf16[2,512,512]{2,1,0:T(8,128)(2,1)}, u32[]{:S(2)}) copy-start(bf16[2,512,512]{2,1,0:T(8,128)(2,1)} %copy-done) | copy-start | bytes 3145732
  73.8 2.6 %collective-permute-start.3 = (f32[32,128]{1,0:T(8,128)S(1)}, f32[32,128]{1,0:T(8,128)S(1)}, u32[]{:S(2)}, u32[]{:S(2)}) collective-permute-start(f32[32,128]{1,0:T(8,128)S(1)} %shard_map.129.near), channel_id=1, source_target_pairs={{0,32},{32,0},{1,33},{33,1},{2,34},{34,2},{3,35},{35,3},{4,36},{36... | collective-permute-start | bytes 49160 | tf_op jit(solution)/shard_map/ppermute | solution.py:489
